TPU v7x, 32 devices: a whole 2x2x4 slice. The times are simulated.
32 devices in a mesh: dp: 16 (over z, x, core), tensor: 2 (over y).
Axes of the slice: x: 2, y: 2, z: 4, core: 2. Of those that a mesh axis runs over, the one named last changes fastest.
Arguments:
- tokens: bfloat16 [1024, 48, 1152], P('tensor', 'dp'), may hold values from -6 to 6
- conditioning: bfloat16 [29, 1152], replicated, may hold values from -6 to 6
- cotangent: bfloat16 [1024, 48, 1152], P('tensor', 'dp'), may hold values from -6 to 6
- latent_counts: int32 [16], replicated, may hold values from 0 to 3, as said below
- latent_order: int32 [29], replicated, may hold values from 0 to 28, each once
- w_ada: bfloat16 [1152, 6, 1152], P('dp', None, 'tensor'), may hold values from -0.1875 to 0.1875
- b_ada: bfloat16 [6, 1152], replicated, may hold values from -3 to 3
- w_qkv: bfloat16 [1152, 3, 1152], P('dp', None, 'tensor'), may hold values from -0.1875 to 0.1875
- b_qv: bfloat16 [2, 1152], replicated, may hold values from -3 to 3
- w_out: bfloat16 [1152, 1152], P('tensor', 'dp'), may hold values from -3 to 3
- w_fc1: bfloat16 [1152, 4608], P('dp', 'tensor'), may hold values from -0.1875 to 0.1875
- b_fc1: bfloat16 [4608], replicated, may hold values from -3 to 3
- w_fc2: bfloat16 [4608, 1152], P('tensor', 'dp'), may hold values from -0.375 to 0.375
- b_out2: bfloat16 [2, 1152], replicated, may hold values from -3 to 3
Outputs:
- out_tokens: bfloat16 [1024, 48, 1152], P('tensor', 'dp')
- grad_tokens: bfloat16 [1024, 48, 1152], P('tensor', 'dp')
- grad_cond: float32 [29, 1152], replicated
- grad_w_ada: float32 [1152, 6, 1152], P('dp', None, 'tensor')
- grad_b_ada: float32 [6, 1152], replicated
- grad_w_qkv: float32 [1152, 3, 1152], P('dp', None, 'tensor')
- grad_b_qv: float32 [2, 1152], replicated
- grad_w_out: float32 [1152, 1152], P('tensor', 'dp')
- grad_w_fc1: float32 [1152, 4608], P('dp', 'tensor')
- grad_b_fc1: float32 [4608], replicated
- grad_w_fc2: float32 [4608, 1152], P('tensor', 'dp')
- grad_b_out2: float32 [2, 1152], replicated
Inputs may be any that keep to these rules, and one draw needn't show every extreme that they name: latent_counts[r] is the number of latents held by index r of dp; they sum to 29, and some index holds 3. Each latent once. Index r of dp holds latent_order[c], ..., latent_order[c + latent_counts[r] - 1] in its first slots, c the sum of latent_counts over lower indices; tokens and cotangent of its other slots are not used.
All inputs are finite; a program needn't handle non-finite values.
Results may differ from a plain program's by a relative error of at most 0.015.
The roundings to bfloat16 on the way count: a program that leaves them out, or rounds other values in their place, can miss the bound.
Values may be sent and summed in bfloat16 or wider, within the bound.
No kernel may reach another device: no remote copies, remote signals or barrier semaphores. Data moves between devices by JAX's collectives and lax.ppermute only.
A program may use at most 320 MiB of HBM per device.

v0:
```python
from functools import partial

import jax
import jax.numpy as jnp
from jax import lax
from jax.sharding import PartitionSpec as P

HEADS = 16
HEAD_DIM = 72


EPSILON = 1e-06


def layer_norm(values):
    center = values - jnp.mean(values, axis=-1, keepdims=True)
    spread = jnp.mean(center * center, axis=-1, keepdims=True)
    return center * lax.rsqrt(spread + EPSILON)


def attend_forward(query, keys_all, values):
    seq_len, slots, heads_here, head_dim = query.shape
    block = min(512, seq_len)
    block_count = seq_len // block
    scale = head_dim ** (-0.5)

    def one_slot(items):
        query_slot, key_slot, value_slot = items

        def one_block(query_block):
            scores = (
                jnp.einsum(
                    "qhd,khd->hqk", query_block, key_slot, preferred_element_type=jnp.float32
                )
                * scale
            )
            peak = jnp.max(scores, axis=-1, keepdims=True)
            expo = jnp.exp(scores - peak)
            total = jnp.sum(expo, axis=-1, keepdims=True)
            probs = (expo / total).astype(jnp.bfloat16)
            mixed = jnp.einsum(
                "hqk,khd->qhd", probs, value_slot, preferred_element_type=jnp.float32
            )
            return (mixed.astype(jnp.bfloat16), (peak + jnp.log(total))[..., 0])

        mixed, log_total = lax.map(
            one_block, query_slot.reshape(block_count, block, heads_here, head_dim)
        )
        return (mixed.reshape(seq_len, heads_here * head_dim), log_total)

    mixed, log_total = lax.map(
        one_slot,
        (jnp.swapaxes(query, 0, 1), jnp.swapaxes(keys_all, 0, 1), jnp.swapaxes(values, 0, 1)),
    )
    return (jnp.swapaxes(mixed, 0, 1), log_total)


def attend_backward(query, keys_all, values, d_mixed, log_total):
    seq_len, slots, heads_here, head_dim = query.shape
    block = min(512, seq_len)
    block_count = seq_len // block
    scale = head_dim ** (-0.5)

    def one_slot(items):
        query_slot, key_slot, value_slot, grad_slot, log_slot = items
        query_blocks = query_slot.reshape(block_count, block, heads_here, head_dim)
        grad_blocks = grad_slot.reshape(block_count, block, heads_here, head_dim)

        def step(carry, blocks):
            key_total, value_total = carry
            query_block, grad_block, log_block = blocks
            scores = (
                jnp.einsum(
                    "qhd,khd->hqk", query_block, key_slot, preferred_element_type=jnp.float32
                )
                * scale
            )
            probs = jnp.exp(scores - log_block[..., None])
            value_total = value_total + jnp.einsum(
                "hqk,qhd->khd",
                probs.astype(jnp.bfloat16),
                grad_block,
                preferred_element_type=jnp.float32,
            )
            d_probs = jnp.einsum(
                "qhd,khd->hqk", grad_block, value_slot, preferred_element_type=jnp.float32
            )
            d_scores = (
                probs * (d_probs - jnp.sum(d_probs * probs, axis=-1, keepdims=True))
            ).astype(jnp.bfloat16)
            d_query = (
                jnp.einsum("hqk,khd->qhd", d_scores, key_slot, preferred_element_type=jnp.float32)
                * scale
            ).astype(jnp.bfloat16)
            key_total = key_total + jnp.einsum(
                "hqk,qhd->khd", d_scores, query_block, preferred_element_type=jnp.float32
            )
            return ((key_total, value_total), d_query)

        empty = jnp.zeros((seq_len, heads_here, head_dim), jnp.float32)
        (key_total, value_total), d_query = lax.scan(
            step, (empty, empty), (query_blocks, grad_blocks, log_slot)
        )
        return (
            d_query.reshape(seq_len, heads_here, head_dim),
            (key_total * scale).astype(jnp.bfloat16),
            value_total.astype(jnp.bfloat16),
        )

    d_query, d_keys, d_values = lax.map(
        one_slot,
        (
            jnp.swapaxes(query, 0, 1),
            jnp.swapaxes(keys_all, 0, 1),
            jnp.swapaxes(values, 0, 1),
            jnp.swapaxes(d_mixed, 0, 1),
            log_total,
        ),
    )
    return (jnp.swapaxes(d_query, 0, 1), jnp.swapaxes(d_keys, 0, 1), jnp.swapaxes(d_values, 0, 1))


def per_device(
    tokens,
    conditioning,
    cotangent,
    latent_counts,
    latent_order,
    w_ada,
    b_ada,
    w_qkv,
    b_qv,
    w_out,
    w_fc1,
    b_fc1,
    w_fc2,
    b_out2,
):
    tensor_size = lax.axis_size("tensor")
    tensor_rank = lax.axis_index("tensor")
    data_rank = lax.axis_index("dp")
    rows_here, slots, width = tokens.shape
    latents = conditioning.shape[0]
    heads_here = HEADS // tensor_size
    slab = heads_here * HEAD_DIM
    hidden_here = w_fc1.shape[1]
    ada_rows = w_ada.shape[0]
    starts = jnp.cumsum(latent_counts) - latent_counts
    slot_index = jnp.arange(slots, dtype=jnp.int32)
    live = (slot_index < latent_counts[data_rank]).astype(jnp.float32)
    chosen = latent_order[jnp.clip(starts[data_rank] + slot_index, 0, latents - 1)]
    picker = (chosen[:, None] == jnp.arange(latents, dtype=jnp.int32)[None, :]).astype(jnp.float32)
    cond_all = conditioning.astype(jnp.float32)
    silu_all = jax.nn.silu(cond_all).astype(jnp.bfloat16)
    silu_rows = jnp.dot(
        picker, silu_all.astype(jnp.float32), precision=lax.Precision.HIGHEST
    ).astype(jnp.bfloat16)
    ada_full, qkv_full, out_full, fc1_full, fc2_full = (
        lax.all_gather(w_ada, "dp", axis=0, tiled=True),
        lax.all_gather(w_qkv, "dp", axis=0, tiled=True),
        lax.all_gather(w_out, "dp", axis=1, tiled=True),
        lax.all_gather(w_fc1, "dp", axis=0, tiled=True),
        lax.all_gather(w_fc2, "dp", axis=1, tiled=True),
    )
    ada_bias = lax.dynamic_slice_in_dim(b_ada.astype(jnp.float32), tensor_rank * slab, slab, 1)
    mod_part = (
        jnp.einsum("sd,djc->sjc", silu_rows, ada_full, preferred_element_type=jnp.float32)
        + ada_bias[None]
    )
    modulation = lax.all_gather(mod_part, "tensor", axis=2, tiled=True)
    shift_attn = modulation[None, :, 0]
    scale_attn = modulation[None, :, 1]
    gate_attn = modulation[None, :, 2]
    shift_mlp = modulation[None, :, 3]
    scale_mlp = modulation[None, :, 4]
    gate_mlp = modulation[None, :, 5]
    bias_query = lax.dynamic_slice_in_dim(b_qv[0].astype(jnp.float32), tensor_rank * slab, slab, 0)
    bias_value = lax.dynamic_slice_in_dim(b_qv[1].astype(jnp.float32), tensor_rank * slab, slab, 0)
    bias_fc1 = lax.dynamic_slice_in_dim(
        b_fc1.astype(jnp.float32), tensor_rank * hidden_here, hidden_here, 0
    )
    bias_attn_out = b_out2[0].astype(jnp.float32)
    bias_mlp_out = b_out2[1].astype(jnp.float32)
    tokens_in = tokens.astype(jnp.float32)
    norm_attn = layer_norm(tokens_in)
    mixed_attn = (norm_attn * (1.0 + scale_attn) + shift_attn).astype(jnp.bfloat16)
    piece = lax.all_gather(mixed_attn, "tensor", axis=0, tiled=True)
    projected = jnp.einsum("psd,dkc->pskc", piece, qkv_full, preferred_element_type=jnp.float32)
    gathered = piece
    head_shape = (projected.shape[0], slots, heads_here, HEAD_DIM)
    query_rows = (projected[:, :, 0] + bias_query).astype(jnp.bfloat16).reshape(head_shape)
    key_rows = projected[:, :, 1].astype(jnp.bfloat16).reshape(head_shape)
    value_rows = (projected[:, :, 2] + bias_value).astype(jnp.bfloat16).reshape(head_shape)
    mixed_rows = gathered
    attn_mixed, log_total = attend_forward(query_rows, key_rows, value_rows)
    part_rows = attn_mixed
    branch_attn = (
        lax.psum_scatter(
            jnp.einsum("psc,cd->psd", part_rows, out_full, preferred_element_type=jnp.float32),
            "tensor",
            scatter_dimension=0,
            tiled=True,
        )
        + bias_attn_out
    )
    middle = tokens_in + gate_attn * branch_attn
    norm_mlp = layer_norm(middle)
    mixed_mlp = (norm_mlp * (1.0 + scale_mlp) + shift_mlp).astype(jnp.bfloat16)
    piece = lax.all_gather(mixed_mlp, "tensor", axis=0, tiled=True)
    expanded = jnp.einsum("psd,df->psf", piece, fc1_full, preferred_element_type=jnp.float32)
    gathered = piece
    pre_act = expanded + bias_fc1
    hidden = jax.nn.gelu(pre_act, approximate=True).astype(jnp.bfloat16)
    part_rows = hidden
    branch_mlp = (
        lax.psum_scatter(
            jnp.einsum("psf,fd->psd", part_rows, fc2_full, preferred_element_type=jnp.float32),
            "tensor",
            scatter_dimension=0,
            tiled=True,
        )
        + bias_mlp_out
    )
    finished = middle + gate_mlp * branch_mlp
    out_tokens = (finished * live[None, :, None]).astype(jnp.bfloat16)
    grad_out = cotangent.astype(jnp.float32) * live[None, :, None]
    d_branch_mlp = (grad_out * gate_mlp).astype(jnp.bfloat16)
    d_gate_mlp = jnp.sum(grad_out * branch_mlp, axis=0)
    piece = lax.all_gather(d_branch_mlp, "tensor", axis=0, tiled=True)
    d_hidden = jnp.einsum("psd,fd->psf", piece, fc2_full, preferred_element_type=jnp.float32)
    d_branch_rows = piece
    grad_fc2 = jnp.einsum("psf,psd->fd", hidden, d_branch_rows, preferred_element_type=jnp.float32)
    _, gelu_back = jax.vjp(partial(jax.nn.gelu, approximate=True), pre_act)
    d_pre = gelu_back(d_hidden)[0].astype(jnp.bfloat16)
    grad_fc1 = jnp.einsum("psd,psf->df", gathered, d_pre, preferred_element_type=jnp.float32)
    d_bias_fc1 = jnp.sum(d_pre.astype(jnp.float32), axis=(0, 1))
    part_rows = d_pre
    d_mixed_mlp = lax.psum_scatter(
        jnp.einsum("psf,df->psd", part_rows, fc1_full, preferred_element_type=jnp.float32),
        "tensor",
        scatter_dimension=0,
        tiled=True,
    )
    d_shift_mlp = jnp.sum(d_mixed_mlp, axis=0)
    d_scale_mlp = jnp.sum(d_mixed_mlp * norm_mlp, axis=0)
    _, norm_back_mlp = jax.vjp(layer_norm, middle)
    d_middle = grad_out + norm_back_mlp(d_mixed_mlp * (1.0 + scale_mlp))[0]
    d_branch_attn = (d_middle * gate_attn).astype(jnp.bfloat16)
    d_gate_attn = jnp.sum(d_middle * branch_attn, axis=0)
    piece = lax.all_gather(d_branch_attn, "tensor", axis=0, tiled=True)
    d_attn_mixed = jnp.einsum(
        "psd,cd->psc", piece, out_full, preferred_element_type=jnp.float32
    ).astype(jnp.bfloat16)
    grad_out_w = jnp.einsum("psc,psd->cd", attn_mixed, piece, preferred_element_type=jnp.float32)
    d_query, d_keys, d_values = attend_backward(
        query_rows, key_rows, value_rows, d_attn_mixed, log_total
    )
    seq_len = d_query.shape[0]
    d_qkv = jnp.stack([d_query, d_keys, d_values], axis=2).reshape(seq_len, slots, 3, slab)
    grad_qkv = jnp.einsum("psd,pskc->dkc", mixed_rows, d_qkv, preferred_element_type=jnp.float32)
    d_bias_qv = jnp.sum(d_qkv[:, :, 0::2].astype(jnp.float32), axis=(0, 1))
    part_rows = d_qkv
    d_mixed_attn = lax.psum_scatter(
        jnp.einsum("pskc,dkc->psd", part_rows, qkv_full, preferred_element_type=jnp.float32),
        "tensor",
        scatter_dimension=0,
        tiled=True,
    )
    d_shift_attn = jnp.sum(d_mixed_attn, axis=0)
    d_scale_attn = jnp.sum(d_mixed_attn * norm_attn, axis=0)
    _, norm_back_attn = jax.vjp(layer_norm, tokens_in)
    grad_tokens = (d_middle + norm_back_attn(d_mixed_attn * (1.0 + scale_attn))[0]).astype(
        jnp.bfloat16
    )
    d_mod_slots = jnp.stack(
        [d_shift_attn, d_scale_attn, d_gate_attn, d_shift_mlp, d_scale_mlp, d_gate_mlp], axis=1
    )
    d_mod_latent = jnp.einsum("sl,sjd->ljd", picker, d_mod_slots, precision=lax.Precision.HIGHEST)
    d_bias_qv_full = lax.dynamic_update_slice(
        jnp.zeros((2, width), jnp.float32), d_bias_qv, (0, tensor_rank * slab)
    )
    d_bias_fc1_full = lax.dynamic_update_slice(
        jnp.zeros((hidden_here * tensor_size,), jnp.float32),
        d_bias_fc1,
        (tensor_rank * hidden_here,),
    )
    d_bias_out = jnp.stack(
        [
            jnp.sum(d_branch_attn.astype(jnp.float32), axis=(0, 1)),
            jnp.sum(d_branch_mlp.astype(jnp.float32), axis=(0, 1)),
        ]
    )
    mod_total, grad_b_qv, grad_b_fc1, grad_b_out2 = lax.psum(
        (d_mod_latent, d_bias_qv_full, d_bias_fc1_full, d_bias_out), ("dp", "tensor")
    )
    grad_b_ada = jnp.sum(mod_total, axis=0)
    mod_slab = lax.dynamic_slice_in_dim(mod_total, tensor_rank * slab, slab, 2)
    silu_block = lax.dynamic_slice_in_dim(
        silu_all.astype(jnp.float32), data_rank * ada_rows, ada_rows, 1
    )
    grad_w_ada = jnp.einsum("lr,ljc->rjc", silu_block, mod_slab, precision=lax.Precision.HIGHEST)
    d_silu = jnp.einsum(
        "ljc,djc->ld", mod_slab, ada_full.astype(jnp.float32), precision=lax.Precision.HIGHEST
    )
    _, silu_back = jax.vjp(jax.nn.silu, cond_all)
    grad_cond = lax.psum(silu_back(d_silu)[0], "tensor")
    grad_w_qkv, grad_w_out, grad_w_fc1, grad_w_fc2 = (
        lax.psum_scatter(grad_qkv, "dp", scatter_dimension=0, tiled=True),
        lax.psum_scatter(grad_out_w, "dp", scatter_dimension=1, tiled=True),
        lax.psum_scatter(grad_fc1, "dp", scatter_dimension=0, tiled=True),
        lax.psum_scatter(grad_fc2, "dp", scatter_dimension=1, tiled=True),
    )
    return (
        out_tokens,
        grad_tokens,
        grad_cond,
        grad_w_ada,
        grad_b_ada,
        grad_w_qkv,
        grad_b_qv,
        grad_w_out,
        grad_w_fc1,
        grad_b_fc1,
        grad_w_fc2,
        grad_b_out2,
    )


def solution(mesh):
    placed = (
        P("tensor", "dp", None),
        P(),
        P("tensor", "dp", None),
        P(),
        P(),
        P("dp", None, "tensor"),
        P(),
        P("dp", None, "tensor"),
        P(),
        P("tensor", "dp"),
        P("dp", "tensor"),
        P(),
        P("tensor", "dp"),
        P(),
    )
    return jax.shard_map(
        per_device,
        mesh=mesh,
        in_specs=placed,
        out_specs=(
            P("tensor", "dp", None),
            P("tensor", "dp", None),
            P(),
            P("dp", None, "tensor"),
            P(),
            P("dp", None, "tensor"),
            P(),
            P("tensor", "dp"),
            P("dp", "tensor"),
            P(),
            P("tensor", "dp"),
            P(),
        ),
        check_vma=False,
    )
```

profile of v0, /device:TPU:0, one launch (start us, length us, event | category | flops | bytes accessed | tf_op | source)
XLA Modules:
  0.0 2487.4 jit_solution(3276217855947897061)
XLA Ops:
  22.1 68.6 %all-gather.10.cloned.1.call-done = bf16[1152,6,576]{2,0,1:T(8,128)(2,1)} async-done(((bf16[72,6,576]{2,0,1:T(8,128)(2,1)}), bf16[1152,6,576]{2,0,1:T(8,128)(2,1)}) %all-gather.10.cloned.1.call-update) | async-done | bytes 7962640 | tf_op jit(solution)/shard_map/all_gather | solution.py:159
  98.4 29.0 %all_gather.31 = f32[3,6,1152]{1,0,2:T(4,128)S(1)} all-gather(f32[3,6,576]{1,0,2:T(4,128)} %copy.103), channel_id=1, replica_groups=mesh['dp'=16,'tensor'=2] {'tensor'}, dimensions={2}, use_global_device_ids=true | all-gather | bytes 124416 | tf_op jit(solution)/shard_map/all_gather | solution.py:170
  127.4 9.3 fusion.112
  149.9 85.6 %all-gather.12.cloned.1.call-done = bf16[1024,3,1152]{2,0,1:T(8,128)(2,1)} async-done(((bf16[512,3,1152]{2,0,1:T(8,128)(2,1)}), bf16[1024,3,1152]{2,0,1:T(8,128)(2,1)}) %all-gather.12.cloned.1.call-update) | async-done | bytes 7077904 | tf_op jit(solution)/shard_map/all_gather | solution.py:187
  235.5 20.8 fusion.57
  261.7 13.3 fusion.111
  275.0 6.2 fusion.72
  284.1 106.9 %while.54 = (s32[]{:T(128)}, bf16[3,1024,576]{1,2,0:T(8,128)(2,1)}, f32[3,2,8,512]{3,2,1,0:T(8,128)}, bf16[3,1024,8,72]{1,3,2,0:T(8,128)(2,1)}, bf16[3,1024,8,72...) while((s32[]{:T(128)}, bf16[3,1024,576]{1,2,0:T(8,128)(2,1)}, ...), condition=%wide.region_8.9_spmd, body=%wide.region_3.8_spmd.sunk | while | flops 1245999104 | bytes 82641280 | solution.py:51
  289.0 25.3 %while.57 = (s32[]{:T(128)}, bf16[2,512,8,72]{1,3,2,0:T(8,128)(2,1)}, f32[2,8,512]{2,1,0:T(8,128)}, bf16[2,512,8,72]{1,3,2,0:T(8,128)(2,1)S(1)}, bf16[1024,8,72]...) while((s32[]{:T(128)}, bf16[2,512,8,72]{1,3,2,0:T(8,128)(2,1)}, ...), condition=%wide.region_7.7_spmd, body=%wide.region_4.6_spmd.sunk | while | flops 1245999104 | bytes 63701200 | solution.py:46
  324.5 25.3 %while.57 = (s32[]{:T(128)}, bf16[2,512,8,72]{1,3,2,0:T(8,128)(2,1)}, f32[2,8,512]{2,1,0:T(8,128)}, bf16[2,512,8,72]{1,3,2,0:T(8,128)(2,1)S(1)}, bf16[1024,8,72]...) while((s32[]{:T(128)}, bf16[2,512,8,72]{1,3,2,0:T(8,128)(2,1)}, ...), condition=%wide.region_7.7_spmd, body=%wide.region_4.6_spmd.sunk | while | flops 1245999104 | bytes 63701200 | solution.py:46
  360.0 25.3 %while.57 = (s32[]{:T(128)}, bf16[2,512,8,72]{1,3,2,0:T(8,128)(2,1)}, f32[2,8,512]{2,1,0:T(8,128)}, bf16[2,512,8,72]{1,3,2,0:T(8,128)(2,1)S(1)}, bf16[1024,8,72]...) while((s32[]{:T(128)}, bf16[2,512,8,72]{1,3,2,0:T(8,128)(2,1)}, ...), condition=%wide.region_7.7_spmd, body=%wide.region_4.6_spmd.sunk | while | flops 1245999104 | bytes 63701200 | solution.py:46
  391.1 11.2 fusion.75
  414.4 149.6 %reduce-scatter.11.cloned.1.call-done = f32[512,3,1152]{2,0,1:T(8,128)} async-done(((f32[1024,3,1152]{2,0,1:T(8,128)}), f32[512,3,1152]{2,0,1:T(8,128)}) %reduce-scatter.11.cloned.1.call-update) | async-done | bytes 7077904 | tf_op jit(solution)/shard_map/reduce_scatter | solution.py:198
  584.5 38.0 %all-gather.20.cloned.1.call-done = bf16[1152,2304]{1,0:T(8,128)(2,1)} async-done(((bf16[72,2304]{1,0:T(8,128)(2,1)}), bf16[1152,2304]{1,0:T(8,128)(2,1)}) %all-gather.20.cloned.1.call-update) | async-done | bytes 5308432 | tf_op jit(solution)/shard_map/all_gather | solution.py:162
  622.5 90.0 %all-gather.18.cloned.1.call-done = bf16[1024,3,1152]{2,0,1:T(8,128)(2,1)} async-done(((bf16[512,3,1152]{2,0,1:T(8,128)(2,1)}), bf16[1024,3,1152]{2,0,1:T(8,128)(2,1)}) %all-gather.18.cloned.1.call-update) | async-done | bytes 7077904 | tf_op jit(solution)/shard_map/all_gather | solution.py:209
  712.4 24.9 %fusion.67 = f32[1024,3,2304]{2,0,1:T(8,128)} fusion(bf16[1024,3,1152]{2,0,1:T(8,128)(2,1)} %all-gather.18.cloned.1.call-done, bf16[1152,2304]{1,0:T(8,128)(2,1)} %all-gather.20.cloned.1.call-done), kind=kOutput, calls=%fused_computation.118 | convolution fusion | flops 16307453952 | bytes 40697856 | tf_op jit(solution)/shard_map/psd,df->psf/dot_general | solution.py:210
  737.3 33.7 %all-gather.22.cloned.1.call-done = bf16[2304,1152]{0,1:T(8,128)(2,1)} async-done(((bf16[2304,72]{0,1:T(8,128)(2,1)}), bf16[2304,1152]{0,1:T(8,128)(2,1)}) %all-gather.22.cloned.1.call-update) | async-done | bytes 5308432 | tf_op jit(solution)/shard_map/all_gather | solution.py:163
  771.0 89.4 %all-gather.24.cloned.1.call-done = bf16[1024,3,1152]{2,0,1:T(8,128)(2,1)} async-done(((bf16[512,3,1152]{2,0,1:T(8,128)(2,1)}), bf16[1024,3,1152]{2,0,1:T(8,128)(2,1)}) %all-gather.24.cloned.1.call-update) | async-done | bytes 7077904 | tf_op jit(solution)/shard_map/all_gather | solution.py:229
  860.4 42.5 %convert_reduce_fusion = (f32[2304]{0:T(1024)}, bf16[1024,3,2304]{2,0,1:T(8,128)(2,1)}) fusion(f32[1024,3,2304]{2,0,1:T(8,128)} %fusion.67, f32[2304]{0:T(1024)S(1)} %dynamic-slice_convert_fusion.1, bf16[1024,3,1152]{2,0,1:T(8,128)(2,1)} %all-gather.24.cloned.1.call-done, bf16[2304,1152]{0,1:T(8,128)(2,1)} %all-gather.22.cloned.1.call-done), kind=kOutput, calls=%fused_computation.68 | convolution fusion | flops 16470243328 | bytes 54872064 | tf_op jit(solution)/shard_map/psd,fd->psf/dot_general | solution.py:230
  902.9 24.5 fusion.65
  927.5 32.5 %fusion.63 = f32[1024,3,1152]{2,0,1:T(8,128)} fusion(bf16[2304,1152]{0,1:T(8,128)(2,1)} %all-gather.22.cloned.1.call-done, f32[1024,3,2304]{2,0,1:T(8,128)} %fusion.67, f32[2304]{0:T(1024)S(1)} %dynamic-slice_convert_fusion.1), kind=kOutput, calls=%fused_computation.114 | convolution fusion | flops 16378232832 | bytes 47784960 | tf_op jit(solution)/shard_map/psf,fd->psd/dot_general | solution.py:217
  960.1 128.9 %reduce-scatter.15.cloned.1.call-done = f32[512,3,1152]{2,0,1:T(8,128)} async-done(((f32[1024,3,1152]{2,0,1:T(8,128)}), f32[512,3,1152]{2,0,1:T(8,128)}) %reduce-scatter.15.cloned.1.call-update) | async-done | bytes 7077904 | tf_op jit(solution)/shard_map/reduce_scatter | solution.py:238
  1089.0 6.3 multiply_reduce_fusion.5
  1096.1 7.0 multiply_reduce_fusion.3
  1103.7 149.1 %reduce-scatter.13.cloned.1.call-done = f32[512,3,1152]{2,0,1:T(8,128)} async-done(((f32[1024,3,1152]{2,0,1:T(8,128)}), f32[512,3,1152]{2,0,1:T(8,128)}) %reduce-scatter.13.cloned.1.call-update) | async-done | bytes 7077904 | tf_op jit(solution)/shard_map/reduce_scatter | solution.py:216
  1252.8 15.8 multiply_reduce_fusion.2
  1268.7 89.3 %all-gather.26.cloned.1.call-done = bf16[1024,3,1152]{2,0,1:T(8,128)(2,1)} async-done(((bf16[512,3,1152]{2,0,1:T(8,128)(2,1)}), bf16[1024,3,1152]{2,0,1:T(8,128)(2,1)}) %all-gather.26.cloned.1.call-update) | async-done | bytes 7077904 | tf_op jit(solution)/shard_map/all_gather | solution.py:250
  1358.0 10.0 convert_bitcast_fusion
  1368.0 319.0 %while.56 = (s32[]{:T(128)}, bf16[3,1024,8,72]{3,2,1,0:T(8,128)(2,1)}, bf16[3,1024,8,72]{1,3,2,0:T(8,128)(2,1)}, bf16[3,1024,8,72]{1,3,2,0:T(8,128)(2,1)}, bf16[...) while((s32[]{:T(128)}, ...), condition=%wide.region_20.21_spmd, body=%wide.region_16.20_spmd.sunk | while | flops 3074945024 | bytes 241025584 | solution.py:110
  1380.8 82.8 %while.58 = (s32[]{:T(128)}, f32[1024,8,72]{0,2,1:T(8,128)}, f32[1024,8,72]{0,2,1:T(8,128)}, bf16[2,512,8,72]{1,3,2,0:T(8,128)(2,1)}, bf16[2,512,8,72]{1,3,2,0:T...) while((s32[]{:T(128)}, f32[1024,8,72]{0,2,1:T(8,128)}, ...), condition=%wide.region_19.19_spmd.clone, body=%wide.region_17.18_spmd.clone.sunk | while | flops 3073175552 | bytes 199016720 | solution.py:101
  1389.4 9.8 multiply_reduce_fusion.9
  1399.2 10.6 multiply_convert_fusion.11
  1409.8 7.3 fusion.161
  1431.4 9.8 multiply_reduce_fusion.9
  1441.2 10.6 multiply_convert_fusion.11
  1451.8 7.3 fusion.161
  1487.0 82.7 %while.58 = (s32[]{:T(128)}, f32[1024,8,72]{0,2,1:T(8,128)}, f32[1024,8,72]{0,2,1:T(8,128)}, bf16[2,512,8,72]{1,3,2,0:T(8,128)(2,1)}, bf16[2,512,8,72]{1,3,2,0:T...) while((s32[]{:T(128)}, f32[1024,8,72]{0,2,1:T(8,128)}, ...), condition=%wide.region_19.19_spmd.clone, body=%wide.region_17.18_spmd.clone.sunk | while | flops 3073175552 | bytes 199016720 | solution.py:101
  1495.5 9.8 multiply_reduce_fusion.9
  1505.3 10.6 multiply_convert_fusion.11
  1515.9 7.3 fusion.161
  1537.5 9.8 multiply_reduce_fusion.9
  1547.3 10.6 multiply_convert_fusion.11
  1557.9 7.3 fusion.161
  1593.2 82.7 %while.58 = (s32[]{:T(128)}, f32[1024,8,72]{0,2,1:T(8,128)}, f32[1024,8,72]{0,2,1:T(8,128)}, bf16[2,512,8,72]{1,3,2,0:T(8,128)(2,1)}, bf16[2,512,8,72]{1,3,2,0:T...) while((s32[]{:T(128)}, f32[1024,8,72]{0,2,1:T(8,128)}, ...), condition=%wide.region_19.19_spmd.clone, body=%wide.region_17.18_spmd.clone.sunk | while | flops 3073175552 | bytes 199016720 | solution.py:101
  1601.7 9.8 multiply_reduce_fusion.9
  1611.5 10.6 multiply_convert_fusion.11
  1622.1 7.3 fusion.161
  1643.7 9.8 multiply_reduce_fusion.9
  1653.5 10.6 multiply_convert_fusion.11
  1664.1 7.3 fusion.161
  1687.0 7.0 copy.112
  1694.0 23.6 convolution_bitcast_fusion.2
  1717.7 161.5 %reduce-scatter.17.cloned.1.call-done = f32[512,3,1152]{2,0,1:T(8,128)} async-done(((f32[1024,3,1152]{2,0,1:T(8,128)}), f32[512,3,1152]{2,0,1:T(8,128)}) %reduce-scatter.17.cloned.1.call-update) | async-done | bytes 7077904 | tf_op jit(solution)/shard_map/reduce_scatter | solution.py:263
  1896.8 26.6 %convolution_bitcast_fusion = f32[2304,1152]{0,1:T(8,128)} fusion(bf16[1024,3,1152]{2,0,1:T(8,128)(2,1)} %all-gather.24.cloned.1.call-done, f32[1024,3,2304]{2,0,1:T(8,128)} %fusion.67, f32[2304]{0:T(1024)} %copy-done.47), kind=kOutput, calls=%fused_computation.71 | convolution fusion | flops 16378232832 | bytes 46015488 | tf_op jit(solution)/shard_map/psf,psd->fd/dot_general | solution.py:232
  1923.5 24.3 convolution_bitcast_fusion.1
  1947.9 11.6 fusion.77
  1959.6 23.2 fusion.59
  1993.8 41.0 %all-reduce.1 = (f32[2,1152]{1,0:T(2,128)}, f32[4608]{0:T(1024)}, f32[2,1152]{1,0:T(2,128)}) all-reduce(f32[2,1152]{1,0:T(2,128)S(1)} %dynamic_update_slice.35, f32[4608]{0:T(1024)S(1)} %copy-done.35, f32[2,1152]{1,0:T(2,128)S(1)} %pad_maximum_fusion.1), channel_id=1, replica_groups=mesh['dp'=16,'tensor'=2] {'dp','tensor'}, use_global_device_ids=true, to_apply=%region_35.36 | all-reduce | flops 9216 | bytes 73728 | tf_op jit(solution)/shard_map/psum | solution.py:293
  2034.9 12.6 fusion.93
  2050.7 99.4 %reduce-scatter.23.cloned.1.call-done = f32[2304,72]{0,1:T(8,128)} async-done(((f32[2304,1152]{0,1:T(8,128)}), f32[2304,72]{0,1:T(8,128)}) %reduce-scatter.23.cloned.1.call-update) | async-done | bytes 663568 | tf_op jit(solution)/shard_map/reduce_scatter | solution.py:311
  2150.1 124.5 %reduce-scatter.21.cloned.1.call-done = f32[72,2304]{1,0:T(8,128)} async-done(((f32[1152,2304]{1,0:T(8,128)}), f32[72,2304]{1,0:T(8,128)}) %reduce-scatter.21.cloned.1.call-update) | async-done | bytes 663568 | tf_op jit(solution)/shard_map/reduce_scatter | solution.py:310
  2274.6 69.4 %reduce-scatter.25.cloned.1.call-done = f32[576,72]{0,1:T(8,128)} async-done(((f32[576,1152]{0,1:T(8,128)}), f32[576,72]{0,1:T(8,128)}) %reduce-scatter.25.cloned.1.call-update) | async-done | bytes 165904
  2344.1 110.5 %reduce-scatter.19.cloned.1.call-done = f32[72,3,576]{2,0,1:T(8,128)} async-done(((f32[1152,3,576]{2,0,1:T(8,128)}), f32[72,3,576]{2,0,1:T(8,128)}) %reduce-scatter.19.cloned.1.call-update) | async-done | bytes 497680 | tf_op jit(solution)/shard_map/reduce_scatter | solution.py:308
  2454.6 24.5 all-reduce.7.cloned.1.call-done
  (434 shorter events, 368.7 us)
Async XLA Ops:
  7.2 5.7 copy-start
  7.2 12.6 copy-start.8
  7.2 83.5 %all-gather.10.cloned.1.call-start = ((), (), s32[]{:S(2)}) async-start(), calls=%async_computation.8 | async-start | bytes 9400320 | tf_op jit(solution)/shard_map/all_gather | solution.py:159
  7.9 141.9 %all-gather.14.cloned.1.call-start = ((), (), s32[]{:S(2)}) async-start(), calls=%async_computation.10 | async-start | bytes 4700160 | tf_op jit(solution)/shard_map/all_gather | solution.py:160
  8.7 226.8 %all-gather.12.cloned.1.call-start = ((), (), s32[]{:S(2)}) async-start(), calls=%async_computation.9 | async-start | bytes 10616832 | tf_op jit(solution)/shard_map/all_gather | solution.py:187
  19.8 123.5 %copy-start.30 = (f32[512,3]{0,1:T(4,128)}, f32[512,3]{0,1:T(4,128)S(1)}, u32[]{:S(2)}) copy-start(f32[512,3]{0,1:T(4,128)S(1)} %broadcast_multiply_fusion.1) | copy-start | bytes 18436
  147.9 243.2 %all-gather.16.cloned.1.call-start = ((), (), s32[]{:S(2)}) async-start(), calls=%async_computation.11 | async-start | bytes 1566720 | tf_op jit(solution)/shard_map/all_gather | solution.py:161
  148.5 415.5 %reduce-scatter.11.cloned.1.call-start = ((), (), s32[]{:S(2)}) async-start(), calls=%async_computation.12 | async-start | bytes 21233664 | tf_op jit(solution)/shard_map/reduce_scatter | solution.py:198
  275.0 6.2 copy-start.15
  402.3 161.8 %copy-start.9 = (bf16[512,3,1152]{2,0,1:T(8,128)(2,1)S(1)}, bf16[512,3,1152]{2,0,1:T(8,128)(2,1)}, u32[]{:S(2)}) copy-start(bf16[512,3,1152]{2,0,1:T(8,128)(2,1)} %param.22) | copy-start | bytes 10616836
  402.3 220.2 %all-gather.20.cloned.1.call-start = ((), (), s32[]{:S(2)}) async-start(), calls=%async_computation.14 | async-start | bytes 5640192 | tf_op jit(solution)/shard_map/all_gather | solution.py:162
  402.9 309.6 %all-gather.18.cloned.1.call-start = ((), (), s32[]{:S(2)}) async-start(), calls=%async_computation.13 | async-start | bytes 10616832 | tf_op jit(solution)/shard_map/all_gather | solution.py:209
  404.6 163.8 %copy-start.39 = (f32[1152]{0:T(1024)}, f32[1152]{0:T(1024)S(1)}, u32[]{:S(2)}) copy-start(f32[1152]{0:T(1024)S(1)} %get-tuple-element.323) | copy-start | bytes 13828
  571.4 8.6 copy-start.17
  575.2 9.2 copy-start.48
  575.2 195.8 %all-gather.22.cloned.1.call-start = ((), (), s32[]{:S(2)}) async-start(), calls=%async_computation.15 | async-start | bytes 5640192 | tf_op jit(solution)/shard_map/all_gather | solution.py:163
  575.9 284.5 %all-gather.24.cloned.1.call-start = ((), (), s32[]{:S(2)}) async-start(), calls=%async_computation.17 | async-start | bytes 10616832 | tf_op jit(solution)/shard_map/all_gather | solution.py:229
  577.2 160.1 %copy-start.51 = (f32[3]{0:T(128)}, f32[3]{0:T(128)S(1)}, u32[]{:S(2)}) copy-start(f32[3]{0:T(128)S(1)} %compare_convert_fusion) | copy-start | bytes 40
  584.3 504.7 %reduce-scatter.15.cloned.1.call-start = ((), (), s32[]{:S(2)}) async-start(), calls=%async_computation.18 | async-start | bytes 21233664 | tf_op jit(solution)/shard_map/reduce_scatter | solution.py:238
  584.5 343.0 %copy-start.47 = (f32[2304]{0:T(1024)}, f32[2304]{0:T(1024)S(1)}, u32[]{:S(2)}) copy-start(f32[2304]{0:T(1024)S(1)} %dynamic-slice_convert_fusion.1) | copy-start | bytes 27652
  927.4 325.4 %reduce-scatter.13.cloned.1.call-start = ((), (), s32[]{:S(2)}) async-start(), calls=%async_computation.16 | async-start | bytes 21233664 | tf_op jit(solution)/shard_map/reduce_scatter | solution.py:216
  960.0 129.0 %copy-start.25 = (f32[3,1,1152]{2,0,1:T(4,128)S(1)}, f32[3,1,1152]{2,0,1:T(4,128)}, u32[]{:S(2)}) copy-start(f32[3,1,1152]{2,0,1:T(4,128)} %copy.134) | copy-start | bytes 41476
  960.0 129.0 %copy-start.28 = (f32[512,3]{0,1:T(4,128)S(1)}, f32[512,3]{0,1:T(4,128)}, u32[]{:S(2)}) copy-start(f32[512,3]{0,1:T(4,128)} %copy-done.27) | copy-start | bytes 18436
  960.0 135.3 %copy-start.44 = (f32[512,3]{0,1:T(4,128)S(1)}, f32[512,3]{0,1:T(4,128)}, u32[]{:S(2)}) copy-start(f32[512,3]{0,1:T(4,128)} %copy-done.43) | copy-start | bytes 18436
  960.1 397.9 %all-gather.26.cloned.1.call-start = ((), (), s32[]{:S(2)}) async-start(), calls=%async_computation.19 | async-start | bytes 10616832 | tf_op jit(solution)/shard_map/all_gather | solution.py:250
  1089.0 7.0 copy-start.11
  1096.1 7.0 copy-start.36
  1096.1 156.7 %copy-start.18 = (bf16[512,3,1152]{2,0,1:T(8,128)(2,1)S(1)}, bf16[512,3,1152]{2,0,1:T(8,128)(2,1)}, u32[]{:S(2)}) copy-start(bf16[512,3,1152]{2,0,1:T(8,128)(2,1)} %param.24) | copy-start | bytes 10616836
  1096.1 156.7 %copy-start.52 = (f32[3]{0:T(128)S(1)}, f32[3]{0:T(128)}, u32[]{:S(2)}) copy-start(f32[3]{0:T(128)} %copy-done.51) | copy-start | bytes 40
  1268.6 610.6 %reduce-scatter.17.cloned.1.call-start = ((), (), s32[]{:S(2)}) async-start(), calls=%async_computation.20 | async-start | bytes 21233664 | tf_op jit(solution)/shard_map/reduce_scatter | solution.py:263
  1409.8 7.3 copy-start.2
  1409.8 7.3 copy-start.3
  1451.8 7.3 copy-start.2
  1451.8 7.3 copy-start.3
  1463.6 7.3 copy-start.5
  1515.9 7.3 copy-start.2
  1515.9 7.3 copy-start.3
  1557.9 7.3 copy-start.2
  1557.9 7.3 copy-start.3
  1569.7 7.3 copy-start.5
  1622.1 7.3 copy-start.2
  1622.1 7.3 copy-start.3
  1664.1 7.3 copy-start.2
  1664.1 7.3 copy-start.3
  1675.9 7.3 copy-start.5
  1693.9 23.6 copy-start.19
  1717.6 161.6 %copy-start.10 = (bf16[512,3,1152]{2,0,1:T(8,128)(2,1)S(1)}, bf16[512,3,1152]{2,0,1:T(8,128)(2,1)}, u32[]{:S(2)}) copy-start(bf16[512,3,1152]{2,0,1:T(8,128)(2,1)} %param.22) | copy-start | bytes 10616836
  1717.6 161.6 %copy-start.31 = (f32[512,3]{0,1:T(4,128)S(1)}, f32[512,3]{0,1:T(4,128)}, u32[]{:S(2)}) copy-start(f32[512,3]{0,1:T(4,128)} %copy-done.30) | copy-start | bytes 18436
  1717.6 317.3 %all-reduce.5.cloned.1.call-start = ((), (), s32[]{:S(2)}) async-start(), calls=%async_computation.21 | async-start | bytes 1769472 | tf_op jit(solution)/shard_map/psum | solution.py:293
  1879.2 6.0 copy-start.12
  1879.2 11.0 slice-start
  1883.8 6.4 copy-start.16
  1883.8 6.4 copy-start.26
  1883.8 6.4 copy-start.33
  1883.8 6.4 copy-start.40
  1896.7 253.4 %reduce-scatter.23.cloned.1.call-start = ((), (), s32[]{:S(2)}) async-start(), calls=%async_computation.25 | async-start | bytes 11280384 | tf_op jit(solution)/shard_map/reduce_scatter | solution.py:311
  1923.4 351.2 %reduce-scatter.21.cloned.1.call-start = ((), (), s32[]{:S(2)}) async-start(), calls=%async_computation.24 | async-start | bytes 11280384 | tf_op jit(solution)/shard_map/reduce_scatter | solution.py:310
  1947.8 11.7 copy-start.20
  1947.8 396.2 %reduce-scatter.25.cloned.1.call-start = ((), (), s32[]{:S(2)}) async-start(), calls=%async_computation.26 | async-start | bytes 3133440
  1959.5 495.1 %reduce-scatter.19.cloned.1.call-start = ((), (), s32[]{:S(2)}) async-start(), calls=%async_computation.23 | async-start | bytes 9400320 | tf_op jit(solution)/shard_map/reduce_scatter | solution.py:308
  1982.8 496.3 %all-reduce.7.cloned.1.call-start = ((), (), s32[]{:S(2)}) async-start(), calls=%async_computation.22 | async-start | bytes 294912 | tf_op jit(solution)/shard_map/psum | solution.py:306
  1992.5 42.4 %copy-start.29 = (bf16[29,1152]{1,0:T(8,128)(2,1)S(1)}, bf16[29,1152]{1,0:T(8,128)(2,1)}, u32[]{:S(2)}) copy-start(bf16[29,1152]{1,0:T(8,128)(2,1)} %param.23) | copy-start | bytes 200452
  1992.5 488.2 %copy-start.1 = (s32[29]{0:T(128)S(1)}, s32[29]{0:T(128)}, u32[]{:S(2)}) copy-start(s32[29]{0:T(128)} %param.26) | copy-start | bytes 352
  2034.9 12.7 copy-start.21
  (53 other events, 143.2 us)
Sparse Core Ops, SparseCore 0:
  10.2 80.4 all-gather.9
  92.9 49.9 all-gather.13
  148.0 87.3 all-gather.11
  237.5 39.3 all-gather.15
  402.4 161.5 reduce-scatter.10
  566.1 56.3 all-gather.19
  624.6 87.8 all-gather.17
  714.6 56.3 all-gather.21
  772.5 87.8 all-gather.23
  927.6 161.4 reduce-scatter.14
  1091.3 161.4 reduce-scatter.12
  1268.7 89.2 all-gather.25
  1717.7 161.4 reduce-scatter.16
  1896.8 128.7 all-reduce.4
  2030.1 119.9 reduce-scatter.22
  2154.6 120.0 reduce-scatter.20
  2279.0 65.0 reduce-scatter.24
  2348.6 105.9 reduce-scatter.18
  2457.5 21.5 all-reduce.6
where the time goes:
time: 2500 us; the launch traced here: 2490 us
  waiting for transfers between devices  1520 us (61%)
  matrix products  517 us (21%)
  other arithmetic  197 us (8%)
  local copies, waits for them, and re-layouts  170 us (7%)
  blocking collectives  70.1 us (3%)
    reduce_scatter x1, waiting for transfers between devices, per_device(): lax.psum_scatter(jnp.einsum('pskc,dkc->psd', part_rows, qkv_full, preferr...  162 us
    reduce_scatter x1, waiting for transfers between devices, per_device(): lax.psum_scatter(jnp.einsum('psc,cd->psd', part_rows, out_full, preferred...  150 us
    reduce_scatter x1, waiting for transfers between devices, per_device(): lax.psum_scatter(jnp.einsum('psf,fd->psd', part_rows, fc2_full, preferred...  149 us
    reduce_scatter x1, waiting for transfers between devices, per_device(): lax.psum_scatter(jnp.einsum('psf,df->psd', part_rows, fc1_full, preferred...  129 us
    reduce_scatter x1, waiting for transfers between devices, per_device(): lax.psum_scatter(grad_fc1, 'dp', scatter_dimension=0, tiled=True)  125 us
    reduce_scatter x1, waiting for transfers between devices, per_device(): lax.psum_scatter(grad_qkv, 'dp', scatter_dimension=0, tiled=True)  111 us
    reduce_scatter x1, waiting for transfers between devices, per_device(): lax.psum_scatter(grad_fc2, 'dp', scatter_dimension=1, tiled=True)  99.4 us
    all_gather x1, waiting for transfers between devices, per_device(): piece = lax.all_gather(mixed_mlp, 'tensor', axis=0, tiled=True)  90 us
  transfers between devices with their start and end apart: 19, of which 16 were waited for; matrix products, arithmetic and copies ran while one was open for 16% of the time, Pallas kernels for 0%

commit v1 on v0

v1 whole, which is shorter than its diff:
```python
from functools import partial

import jax
import jax.numpy as jnp
import numpy as np
from jax import lax
from jax.experimental import pallas as pl
from jax.experimental.pallas import tpu as pltpu
from jax.sharding import Mesh
from jax.sharding import PartitionSpec as P

HEADS = 16
HEAD_DIM = 72
EPSILON = 1e-06
WINDOW = 256
LANES = 128
LOG2E = 1.4426950408889634
VMEM_BYTES = 56 * 2**20

NN = (((1,), (0,)), ((), ()))
NT = (((1,), (1,)), ((), ()))
TN = (((0,), (0,)), ((), ()))


def dot(left, right, dims=NN):
    return lax.dot_general(left, right, dims, preferred_element_type=jnp.float32)


def norm_parts(values):
    center = values - jnp.mean(values, axis=-1, keepdims=True)
    spread = jnp.mean(center * center, axis=-1, keepdims=True)
    inverse = lax.rsqrt(spread + EPSILON)
    return center * inverse, inverse


def norm_back(normed, inverse, grad):
    mean_grad = jnp.mean(grad, axis=-1, keepdims=True)
    mean_prod = jnp.mean(grad * normed, axis=-1, keepdims=True)
    return (grad - mean_grad - normed * mean_prod) * inverse


def round_up(value, step):
    return -(-value // step) * step


def window(column, width):
    start = jnp.minimum((column // LANES) * LANES, width - WINDOW)
    low = column - start
    lane = lax.broadcasted_iota(jnp.int32, (1, WINDOW), 1)
    return pl.ds(pl.multiple_of(start, LANES), WINDOW), (lane >= low) & (lane < low + HEAD_DIM)


def forward_kernel(k_at, v_at, chunk, q_ref, kv_ref, o_ref, log_ref):
    head = pl.program_id(0)
    column = head * HEAD_DIM
    q_cols, _ = window(column, q_ref.shape[1])
    k_cols, _ = window(k_at + column, kv_ref.shape[1])
    v_cols, v_mask = window(v_at + column, kv_ref.shape[1])
    o_cols, o_mask = window(column, o_ref.shape[1])

    @pl.when(head == 0)
    def _():
        o_ref[...] = jnp.zeros_like(o_ref)

    keys = align_head(kv_ref[:, k_cols], k_at + column, kv_ref.shape[1], column, q_ref.shape[1])
    values = align_head(kv_ref[:, v_cols], v_at + column, kv_ref.shape[1], column, o_ref.shape[1])
    factor = HEAD_DIM ** (-0.5) * LOG2E
    for part in range(q_ref.shape[0] // chunk):
        rows = pl.ds(part * chunk, chunk)
        scores = dot(keys, q_ref[rows, q_cols], NT)
        peak = jnp.max(scores, axis=0, keepdims=True)
        expo = jnp.exp2((scores - peak) * factor)
        total = jnp.sum(expo, axis=0, keepdims=True)
        mixed = dot(values, expo.astype(jnp.bfloat16), TN) * (1.0 / total)
        o_ref[rows, o_cols] = o_ref[rows, o_cols] + mixed.T.astype(jnp.bfloat16)
        log_ref[pl.ds(head, 1), rows] = peak * factor + jnp.log2(total)


def align_head(block, from_column, from_width, to_column, to_width):
    from_start = jnp.minimum((from_column // LANES) * LANES, from_width - WINDOW)
    to_start = jnp.minimum((to_column // LANES) * LANES, to_width - WINDOW)
    from_low = from_column - from_start
    to_low = to_column - to_start
    shift = lax.rem(to_low - from_low + WINDOW, WINDOW)
    lane = lax.broadcasted_iota(jnp.int32, (1, WINDOW), 1)
    moved = pltpu.roll(block.astype(jnp.float32), shift, 1)
    keep = (lane >= to_low) & (lane < to_low + HEAD_DIM)
    return jnp.where(keep, moved, 0.0).astype(jnp.bfloat16)


def backward_kernel(k_at, v_at, dk_at, dv_at, chunk, joined, q_ref, kv_ref, do_ref, log_ref, *outs):
    head = pl.program_id(0)
    column = head * HEAD_DIM
    if joined:
        (dq_ref,) = outs
        dkv_ref = dq_ref
    else:
        dq_ref, dkv_ref = outs
    q_cols, q_mask = window(column, q_ref.shape[1])
    k_cols, _ = window(k_at + column, kv_ref.shape[1])
    v_cols, _ = window(v_at + column, kv_ref.shape[1])
    do_cols, _ = window(column, do_ref.shape[1])
    dq_cols, dq_mask = window(column, dq_ref.shape[1])
    dk_cols, dk_mask = window(dk_at + column, dkv_ref.shape[1])
    dv_cols, dv_mask = window(dv_at + column, dkv_ref.shape[1])

    @pl.when(head == 0)
    def _():
        for out in outs:
            out[...] = jnp.zeros_like(out)

    width = q_ref.shape[1]
    keys = align_head(kv_ref[:, k_cols], k_at + column, kv_ref.shape[1], column, width)
    values = align_head(kv_ref[:, v_cols], v_at + column, kv_ref.shape[1], column, do_ref.shape[1])
    scale = HEAD_DIM ** (-0.5)
    factor = scale * LOG2E
    dk_total = jnp.zeros((kv_ref.shape[0], WINDOW), jnp.float32)
    dv_total = jnp.zeros((kv_ref.shape[0], WINDOW), jnp.float32)
    for part in range(q_ref.shape[0] // chunk):
        rows = pl.ds(part * chunk, chunk)
        query = q_ref[rows, q_cols]
        grad = do_ref[rows, do_cols]
        scores = dot(keys, query, NT)
        probs = jnp.exp2(scores * factor - log_ref[pl.ds(head, 1), rows])
        d_probs = dot(values, grad, NT)
        inner = jnp.sum(d_probs * probs, axis=0, keepdims=True)
        d_scores = (probs * (d_probs - inner)).astype(jnp.bfloat16)
        dv_total = dv_total + dot(probs.astype(jnp.bfloat16), grad)
        dk_total = dk_total + dot(d_scores, query)
        d_query = (dot(keys, d_scores, TN) * scale).T
        moved = move_head(d_query, column, width, column, dq_ref.shape[1])
        dq_ref[rows, dq_cols] = dq_ref[rows, dq_cols] + moved
    dk_ref_add(dkv_ref, dk_cols, move_head(dk_total * scale, column, width, dk_at + column, dkv_ref.shape[1]))
    dk_ref_add(dkv_ref, dv_cols, move_head(dv_total, column, do_ref.shape[1], dv_at + column, dkv_ref.shape[1]))


def dk_ref_add(ref, cols, values):
    ref[:, cols] = ref[:, cols] + values


def move_head(block, from_column, from_width, to_column, to_width):
    return align_head(block, from_column, from_width, to_column, to_width)


def spec(shape, *index):
    return pl.BlockSpec(shape, lambda head: index, pipeline_mode=pl.Buffered(1))


def attend_forward(q, q_block, kv, kv_block, k_at, v_at, rows, keys, heads):
    width = round_up(heads * HEAD_DIM, LANES)
    return pl.pallas_call(
        partial(forward_kernel, k_at, v_at, min(256, rows)),
        grid=(heads,),
        in_specs=[
            spec((rows, q.shape[1]), q_block, 0),
            spec((keys, kv.shape[1]), kv_block, 0),
        ],
        out_specs=[spec((rows, width), 0, 0), spec((heads, rows), 0, 0)],
        out_shape=[
            jax.ShapeDtypeStruct((rows, width), jnp.bfloat16),
            jax.ShapeDtypeStruct((heads, rows), jnp.float32),
        ],
        compiler_params=pltpu.CompilerParams(vmem_limit_bytes=VMEM_BYTES),
        cost_estimate=pl.CostEstimate(
            flops=4 * heads * rows * keys * WINDOW,
            bytes_accessed=2 * (rows + keys) * 1792,
            transcendentals=heads * rows * keys,
        ),
        name="attend_forward",
    )(q, kv)


def attend_backward(q, q_block, kv, kv_block, k_at, v_at, grad, grad_block, log_total, rows, keys, heads, joined):
    slab = heads * HEAD_DIM
    if joined:
        out_specs = [spec((rows, q.shape[1]), 0, 0)]
        out_shape = [jax.ShapeDtypeStruct((rows, q.shape[1]), jnp.bfloat16)]
        dk_at, dv_at = k_at, v_at
    else:
        width = round_up(slab, LANES)
        out_specs = [spec((rows, width), 0, 0), spec((keys, 2 * slab), 0, 0)]
        out_shape = [
            jax.ShapeDtypeStruct((rows, width), jnp.bfloat16),
            jax.ShapeDtypeStruct((keys, 2 * slab), jnp.bfloat16),
        ]
        dk_at, dv_at = 0, slab
    return pl.pallas_call(
        partial(backward_kernel, k_at, v_at, dk_at, dv_at, min(256, rows), joined),
        grid=(heads,),
        in_specs=[
            spec((rows, q.shape[1]), q_block, 0),
            spec((keys, kv.shape[1]), kv_block, 0),
            spec((rows, grad.shape[1]), grad_block, 0),
            spec((heads, rows), 0, 0),
        ],
        out_specs=out_specs,
        out_shape=out_shape,
        compiler_params=pltpu.CompilerParams(vmem_limit_bytes=VMEM_BYTES),
        cost_estimate=pl.CostEstimate(
            flops=10 * heads * rows * keys * WINDOW,
            bytes_accessed=4 * (rows + keys) * 1792,
            transcendentals=heads * rows * keys,
        ),
        name="attend_backward",
    )(q, kv, grad, log_total)


def per_device(
    tokens,
    conditioning,
    cotangent,
    latent_counts,
    latent_order,
    w_ada,
    b_ada,
    w_qkv,
    b_qv,
    w_out,
    w_fc1,
    b_fc1,
    w_fc2,
    b_out2,
):
    tsize = lax.axis_size("tensor")
    t = lax.axis_index("tensor")
    c = lax.axis_index("core")
    r = lax.axis_index("dpo") * 2 + c
    dp_size = lax.axis_size("dpo") * 2
    f32, bf16 = jnp.float32, jnp.bfloat16
    rows, slots, width = tokens.shape
    latents = conditioning.shape[0]
    drows = w_ada.shape[0]
    slab = width // tsize
    half_heads = HEADS // 2
    hslab = half_heads * HEAD_DIM
    head_w = slab // 2
    fc_w = w_fc1.shape[1] // 2
    qkv_w = round_up(3 * hslab, LANES)
    out_w = round_up(hslab, LANES)
    pair = tsize == 2 and slots == 3

    def swap_core(x):
        return lax.ppermute(x, "core", [(0, 1), (1, 0)])

    def swap_tensor(x):
        return lax.ppermute(x, "tensor", [(0, 1), (1, 0)])

    def in_order(index, mine, other, axis):
        first = jnp.where(index == 0, mine, other)
        second = jnp.where(index == 0, other, mine)
        return jnp.concatenate([first, second], axis=axis)

    def at(x, index, axis):
        return lax.dynamic_index_in_dim(x, index, axis, keepdims=False)

    starts = jnp.cumsum(latent_counts) - latent_counts
    slot_all = jnp.arange(slots * dp_size, dtype=jnp.int32)
    owner, within = slot_all // slots, slot_all % slots
    live_all = (within < latent_counts[owner]).astype(f32)
    chosen = latent_order[jnp.clip(starts[owner] + within, 0, latents - 1)]
    picker = (chosen[:, None] == jnp.arange(latents, dtype=jnp.int32)[None, :]).astype(f32)
    picker_live = picker * live_all[:, None]
    cond_here = lax.dynamic_slice_in_dim(conditioning, r * drows, drows, 1).astype(f32)
    silu_here = jax.nn.silu(cond_here).astype(bf16)
    silu_slots = jnp.dot(picker, silu_here.astype(f32), precision=lax.Precision.HIGHEST).astype(bf16)

    ada_flat = w_ada.reshape(drows, 6 * slab)
    mod_part = dot(silu_slots, ada_flat)
    mod_here = lax.psum_scatter(mod_part, ("dpo", "core"), scatter_dimension=0, tiled=True)
    mod_here = mod_here.reshape(slots, 6, slab)
    if tsize == 2:
        modulation = in_order(t, mod_here, swap_tensor(mod_here), 2)
    else:
        modulation = lax.all_gather(mod_here, "tensor", axis=2, tiled=True)
    modulation = modulation + b_ada.astype(f32)[None]

    if pair:

        def take(x):
            mine = at(x, t, 1)
            other = swap_tensor(at(x, 1 - t, 1))
            return jnp.concatenate([mine, other, x[:, 2]], axis=0)

        group_slots = jnp.stack([t, t, jnp.full_like(t, 2)])
    else:

        def take(x):
            return jnp.swapaxes(x, 0, 1).reshape(slots * rows, width)

        group_slots = jnp.arange(slots, dtype=jnp.int32)
    groups = slots
    count = groups * rows
    tokens_in = take(tokens)
    cot_in = take(cotangent)
    slot_pick = group_slots[:, None] == jnp.arange(slots, dtype=jnp.int32)[None, :]
    live_here = lax.dynamic_slice_in_dim(live_all, r * slots, slots, 0)
    live = jnp.sum(jnp.where(slot_pick, live_here[None], 0.0), axis=1)
    mod_groups = jnp.sum(
        jnp.where(slot_pick[:, :, None, None], modulation[None], 0.0), axis=1
    )

    def grouped(x):
        return x.reshape(groups, rows, x.shape[-1])

    def flat(x):
        return x.reshape(count, x.shape[-1])

    shift_attn, scale_attn, gate_attn, shift_mlp, scale_mlp, gate_mlp = (
        mod_groups[:, i][:, None, :] for i in range(6)
    )

    shards = (
        w_qkv.reshape(drows, 3, 2, head_w),
        w_out.T.reshape(drows, 1, 2, head_w),
        w_fc1.reshape(drows, 1, 2, fc_w),
        w_fc2.T.reshape(drows, 1, 2, fc_w),
    )
    pads = (qkv_w - 3 * hslab, out_w - hslab, 0, 0)

    def side(which):
        return jnp.concatenate([at(x, which, 2).reshape(drows, -1) for x in shards], axis=1)

    both = in_order(c, side(c), swap_core(side(1 - c)), 0)
    if tsize == 2:
        met = swap_tensor(both)
        by_tensor = [jnp.where(t == 0, both, met), jnp.where(t == 0, met, both)]
    else:
        met = lax.all_gather(both, "tensor", axis=0, tiled=False)
        by_tensor = [met[i] for i in range(tsize)]
    gathered = []
    offset = 0
    for x, pad in zip(shards, pads):
        kinds, wide = x.shape[1], x.shape[3]
        parts = [
            y[:, offset : offset + kinds * wide].reshape(2 * drows, kinds, 1, wide) for y in by_tensor
        ]
        offset += kinds * wide
        joined = jnp.concatenate(parts, axis=2).reshape(2 * drows, kinds * tsize * wide)
        if pad:
            joined = jnp.pad(joined, ((0, 0), (0, pad)))
        own = lax.all_gather(joined, "dpo", axis=0, tiled=True)
        gathered.append((own, swap_core(own)))
    qkv_ws, out_ws, fc1_ws, fc2_ws = gathered

    def bias_halves(bias, wide):
        parts = bias.astype(f32).reshape(bias.shape[0], tsize, 2, wide)
        return [at(parts, which, 2).reshape(bias.shape[0], tsize * wide) for which in (c, 1 - c)]

    qv_halves = bias_halves(b_qv, head_w)
    qkv_bias = [
        jnp.concatenate(
            [b[0], jnp.zeros((hslab,), f32), b[1], jnp.zeros((pads[0],), f32)]
        )
        for b in qv_halves
    ]
    fc1_bias = [b[0] for b in bias_halves(b_fc1[None], fc_w)]
    bias_attn_out, bias_mlp_out = b_out2[0].astype(f32), b_out2[1].astype(f32)

    x_in = grouped(tokens_in.astype(f32))
    norm_attn, inv_attn = norm_parts(x_in)
    mixed_attn = flat((norm_attn * (1.0 + scale_attn) + shift_attn).astype(bf16))
    qkv = [(dot(mixed_attn, w) + b).astype(bf16) for w, b in zip(qkv_ws, qkv_bias)]

    if pair:
        segments = [(2, 1)]
    else:
        segments = [(g, 1) for g in range(groups)]
    seq = rows * tsize

    def gather_keys(x):
        if tsize == 2:
            return jnp.concatenate([x, swap_tensor(x)], axis=0)
        return lax.all_gather(x, "tensor", axis=0, tiled=True)

    def scatter_keys(x):
        if tsize == 2:
            return (x[:rows].astype(f32) + swap_tensor(x[rows:]).astype(f32)).astype(bf16)
        return lax.psum_scatter(x.astype(f32), "tensor", scatter_dimension=0, tiled=True).astype(bf16)

    mixed_parts, log_parts, key_parts = [], [], []
    for x in qkv:
        keys_by_segment = [
            gather_keys(x[g * rows : (g + 1) * rows, hslab : 3 * hslab]) for g, _ in segments
        ]
        outs, logs = [], []
        if pair:
            out, log = attend_forward(x, 0, x, 0, hslab, 2 * hslab, seq, seq, half_heads)
            outs.append(out)
            logs.append(log)
        for (g, _), kv in zip(segments, keys_by_segment):
            out, log = attend_forward(x, g, kv, 0, 0, hslab, rows, seq, half_heads)
            outs.append(out)
            logs.append(log)
        mixed_parts.append(jnp.concatenate(outs, axis=0))
        log_parts.append(logs)
        key_parts.append(keys_by_segment)
    branch_attn = grouped(
        sum(dot(x, w, NT) for x, w in zip(mixed_parts, out_ws)) + bias_attn_out
    )
    middle = x_in + gate_attn * branch_attn
    norm_mlp, inv_mlp = norm_parts(middle)
    mixed_mlp = flat((norm_mlp * (1.0 + scale_mlp) + shift_mlp).astype(bf16))

    grad_out = grouped(cot_in.astype(f32)) * live[:, None, None]
    d_branch_mlp = flat((grad_out * gate_mlp).astype(bf16))
    hidden, d_pre, grad_fc1, grad_fc2, d_bias_fc1 = [], [], [], [], []
    for w1, w2, b in zip(fc1_ws, fc2_ws, fc1_bias):
        pre_act = dot(mixed_mlp, w1) + b
        act = jax.nn.gelu(pre_act, approximate=True).astype(bf16)
        d_hidden = dot(d_branch_mlp, w2)
        _, gelu_back = jax.vjp(partial(jax.nn.gelu, approximate=True), pre_act)
        d_act = gelu_back(d_hidden)[0].astype(bf16)
        hidden.append(act)
        d_pre.append(d_act)
        grad_fc1.append(dot(mixed_mlp, d_act, TN).astype(bf16))
        grad_fc2.append(dot(d_branch_mlp, act, TN).astype(bf16))
        d_bias_fc1.append(jnp.sum(d_act.astype(f32), axis=0))
    branch_mlp = grouped(sum(dot(h, w, NT) for h, w in zip(hidden, fc2_ws)) + bias_mlp_out)
    out_rows = flat(((middle + gate_mlp * branch_mlp) * live[:, None, None]).astype(bf16))
    d_gate_mlp = jnp.sum(grad_out * branch_mlp, axis=1)
    d_mixed_mlp = grouped(sum(dot(g, w, NT) for g, w in zip(d_pre, fc1_ws)))
    d_shift_mlp = jnp.sum(d_mixed_mlp, axis=1)
    d_scale_mlp = jnp.sum(d_mixed_mlp * norm_mlp, axis=1)
    d_middle = grad_out + norm_back(norm_mlp, inv_mlp, d_mixed_mlp * (1.0 + scale_mlp))
    d_branch_attn = flat((d_middle * gate_attn).astype(bf16))
    d_gate_attn = jnp.sum(d_middle * branch_attn, axis=1)

    d_qkv = []
    grad_out_w = []
    for x, w, mixed, logs, keys_by_segment in zip(qkv, out_ws, mixed_parts, log_parts, key_parts):
        d_mixed = dot(d_branch_attn, w).astype(bf16)
        grad_out_w.append(dot(d_branch_attn, mixed, TN).astype(bf16))
        d_rows = []
        first = 1 if pair else 0
        for i, (g, _) in enumerate(segments):
            d_q, d_kv = attend_backward(
                x, g, keys_by_segment[i], 0, 0, hslab, d_mixed, g, logs[first + i], rows, seq, half_heads, False
            )
            d_rows.append(
                jnp.concatenate(
                    [d_q[:, :hslab], scatter_keys(d_kv), jnp.zeros((rows, pads[0]), bf16)], axis=1
                )
            )
        if pair:
            (whole,) = attend_backward(
                x, 0, x, 0, hslab, 2 * hslab, d_mixed, 0, logs[0], seq, seq, half_heads, True
            )
            d_rows.insert(0, whole)
        d_qkv.append(jnp.concatenate(d_rows, axis=0))
    grad_qkv = [dot(mixed_attn, d, TN).astype(bf16) for d in d_qkv]
    d_mixed_attn = grouped(sum(dot(d, w, NT) for d, w in zip(d_qkv, qkv_ws)))
    d_shift_attn = jnp.sum(d_mixed_attn, axis=1)
    d_scale_attn = jnp.sum(d_mixed_attn * norm_attn, axis=1)
    grad_rows = flat(
        (d_middle + norm_back(norm_attn, inv_attn, d_mixed_attn * (1.0 + scale_attn))).astype(bf16)
    )

    def give(x):
        if not pair:
            return jnp.swapaxes(x.reshape(slots, rows, width), 0, 1)
        mine, other, last = x[:rows], swap_tensor(x[rows : 2 * rows]), x[2 * rows :]
        return jnp.stack(
            [jnp.where(t == 0, mine, other), jnp.where(t == 0, other, mine), last], axis=1
        )

    out_tokens = give(out_rows)
    grad_tokens = give(grad_rows)

    def scatter_weight(halves, kinds, wide):
        own, other = halves
        total = (own.astype(f32) + swap_core(other).astype(f32)).astype(bf16)
        part = lax.optimization_barrier(
            lax.psum_scatter(total, "dpo", scatter_dimension=0, tiled=True)
        )
        part = part[:, : kinds * tsize * wide].reshape(2 * drows, kinds, tsize, wide)
        if tsize == 2:
            met = swap_tensor(at(part, 1 - t, 2))
            part = at(part, t, 2).astype(f32) + met.astype(f32)
        else:
            part = lax.psum_scatter(part.astype(f32), "tensor", scatter_dimension=2, tiled=True)
            part = part.reshape(2 * drows, kinds, wide)
        part = part.reshape(2, drows, kinds, 1, wide)
        mine = at(part, c, 0)
        met = swap_core(at(part, 1 - c, 0))
        return in_order(c, mine, met, 2).reshape(drows, kinds, 2 * wide)

    grad_w_fc1 = scatter_weight(grad_fc1, 1, fc_w).reshape(drows, 2 * fc_w)
    grad_w_fc2 = scatter_weight(grad_fc2, 1, fc_w).reshape(drows, 2 * fc_w).T
    grad_w_out = scatter_weight(grad_out_w, 1, head_w).reshape(drows, slab).T
    grad_w_qkv = scatter_weight(grad_qkv, 3, head_w)

    d_mod_groups = jnp.stack(
        [d_shift_attn, d_scale_attn, d_gate_attn, d_shift_mlp, d_scale_mlp, d_gate_mlp], axis=1
    )
    d_mod = jnp.sum(
        jnp.where(slot_pick[:, :, None, None], d_mod_groups[:, None], 0.0), axis=0
    )

    def bias_back(halves, wide):
        own, other = (x.reshape(x.shape[0], tsize, 1, wide) for x in halves)
        return in_order(c, own, other, 2).reshape(own.shape[0], tsize, 2 * wide)

    d_bias_q = [jnp.sum(d[:, :hslab].astype(f32), axis=0) for d in d_qkv]
    d_bias_v = [jnp.sum(d[:, 2 * hslab : 3 * hslab].astype(f32), axis=0) for d in d_qkv]
    d_bias_qv = bias_back([jnp.stack([q, v]) for q, v in zip(d_bias_q, d_bias_v)], head_w)
    d_bias_fc = bias_back([x[None] for x in d_bias_fc1], fc_w)
    d_bias_out = jnp.stack(
        [jnp.sum(d_branch_attn.astype(f32), axis=0), jnp.sum(d_branch_mlp.astype(f32), axis=0)]
    ).reshape(2, tsize, slab)
    small = jnp.concatenate(
        [
            jnp.swapaxes(d_mod.reshape(slots * 6, tsize, slab), 0, 1).reshape(tsize, -1),
            jnp.swapaxes(d_bias_qv, 0, 1).reshape(tsize, -1),
            jnp.swapaxes(d_bias_fc, 0, 1).reshape(tsize, -1),
            jnp.swapaxes(d_bias_out, 0, 1).reshape(tsize, -1),
        ],
        axis=1,
    )
    if tsize == 2:
        small = at(small, t, 0) + swap_tensor(at(small, 1 - t, 0))
    else:
        small = lax.psum_scatter(small, "tensor", scatter_dimension=0, tiled=True)[0]
    every = lax.all_gather(small, ("dpo", "core"), axis=0, tiled=False)
    mod_size = slots * 6 * slab
    mod_all = every[:, :mod_size].reshape(dp_size * slots, 6 * slab)
    bias_sum = jnp.sum(every[:, mod_size:], axis=0)
    d_ada_bias = jnp.sum(mod_all, axis=0)
    grad_w_ada = lax.dot_general(
        silu_slots.astype(f32), mod_all, TN, precision=lax.Precision.HIGHEST
    ).reshape(drows, 6, slab)
    d_silu_slots = lax.dot_general(
        mod_all, ada_flat.astype(f32), NT, precision=lax.Precision.HIGHEST
    )
    d_silu = lax.dot_general(picker_live, d_silu_slots, TN, precision=lax.Precision.HIGHEST)
    _, silu_back = jax.vjp(jax.nn.silu, cond_here)
    cond_part = silu_back(d_silu)[0].reshape(-1)
    shared = jnp.concatenate([d_ada_bias, bias_sum])
    share = shared.shape[0] // dp_size
    shared_part = lax.dynamic_slice_in_dim(shared, r * share, share, 0)
    last = lax.all_gather(
        jnp.concatenate([cond_part, shared_part]), ("dpo", "core", "tensor"), axis=0, tiled=False
    ).reshape(dp_size, tsize, -1)
    cond_size = latents * drows
    grad_cond = jnp.sum(last[:, :, :cond_size], axis=1).reshape(dp_size, latents, drows)
    grad_cond = jnp.swapaxes(grad_cond, 0, 1).reshape(latents, width)
    spread = jnp.swapaxes(last[:, :, cond_size:], 0, 1).reshape(tsize, dp_size * share)

    def whole(start, kinds, wide):
        part = spread[:, start : start + kinds * wide].reshape(tsize, kinds, wide)
        return jnp.swapaxes(part, 0, 1).reshape(kinds, tsize * wide)

    grad_b_ada = whole(0, 6, slab)
    grad_b_qv = whole(6 * slab, 2, slab)
    grad_b_fc1 = whole(8 * slab, 1, 2 * fc_w)[0]
    grad_b_out2 = whole(8 * slab + 2 * fc_w, 2, slab)
    return (
        out_tokens,
        grad_tokens,
        grad_cond,
        grad_w_ada,
        grad_b_ada,
        grad_w_qkv,
        grad_b_qv,
        grad_w_out,
        grad_w_fc1,
        grad_b_fc1,
        grad_w_fc2,
        grad_b_out2,
    )


def solution(mesh):
    dp_size, tensor_size = mesh.devices.shape
    split = Mesh(mesh.devices.reshape(dp_size // 2, 2, tensor_size), ("dpo", "core", "tensor"))
    dp = ("dpo", "core")
    placed = (
        P("tensor", dp, None),
        P(),
        P("tensor", dp, None),
        P(),
        P(),
        P(dp, None, "tensor"),
        P(),
        P(dp, None, "tensor"),
        P(),
        P("tensor", dp),
        P(dp, "tensor"),
        P(),
        P("tensor", dp),
        P(),
    )
    return jax.shard_map(
        per_device,
        mesh=split,
        in_specs=placed,
        out_specs=(
            P("tensor", dp, None),
            P("tensor", dp, None),
            P(),
            P(dp, None, "tensor"),
            P(),
            P(dp, None, "tensor"),
            P(),
            P("tensor", dp),
            P(dp, "tensor"),
            P(),
            P("tensor", dp),
            P(),
        ),
        check_vma=False,
    )
```

time: 2500 us -> 1270 us (0.51)
  waiting for transfers between devices: 1520 us -> 389 us
  Pallas kernels: 0 us -> 216 us
  matrix products: 517 us -> 313 us
  other arithmetic: 197 us -> 111 us
  blocking collectives: 70.1 us -> 21.3 us
    reduce_scatter x7 -> x4, waiting for transfers between devices: 924 us -> 174 us  [scatter_weight(): lax.psum_scatter(total, 'dpo', scatter_dimension=0, tiled=True)]
    all_gather x9 -> x4, waiting for transfers between devices: 494 us -> 59.2 us  [per_device(): own = lax.all_gather(joined, 'dpo', axis=0, tiled=True)]
    pallas_call x0 -> x8, Pallas kernels: none -> 216 us  [the longest x4 127 us: attend_backward(): pl.pallas_call(partial(backward_kernel, k_at, v_at, dk_at, dv_at, min(256...]
    dot_general x59 -> x29, matrix products: 517 us -> 313 us  [the longest x25 305 us: dot(): lax.dot_general(left, right, dims, preferred_element_type=jnp.float32)]
    ppermute x0 -> x28, waiting for transfers between devices: none -> 85.6 us  [the longest x15 68.1 us: swap_tensor(): return lax.ppermute(x, 'tensor', [(0, 1), (1, 0)])]
    while x117 -> x0, local copies, waits for them, and re-layouts: 46.8 us -> none
    convert_element_type x13 -> x9, other arithmetic: 76.7 us -> 30 us  [the longest x1 10.8 us: per_device(): ((middle + gate_mlp * branch_mlp) * live[:, None, None]).astype(bf16)]
    psum x1 -> x0, blocking collectives: 41 us -> none  [per_device(): lax.psum((d_mod_latent, d_bias_qv_full, d_bias_fc1_full, d_bias_out), ('d...]
  transfers between devices with their start and end apart: 19 -> 38, of which waited for: 16 -> 14; matrix products, arithmetic and copies ran while one was open for 16% -> 41% of each run, Pallas kernels for 0% -> 17%
where the time goes in v1:
time: 1270 us; the launch traced here: 1260 us
  waiting for transfers between devices  389 us (31%)
  matrix products  313 us (25%)
  Pallas kernels  216 us (17%)
  local copies, waits for them, and re-layouts  165 us (13%)
  other arithmetic  111 us (9%)
  starting transfers between devices  24.3 us (2%)
  blocking collectives  21.3 us (2%)
  between operations  17.9 us (1%)
    dot_general x25, matrix products, dot(): lax.dot_general(left, right, dims, preferred_element_type=jnp.float32)  305 us
    reduce_scatter x4, waiting for transfers between devices, scatter_weight(): lax.psum_scatter(total, 'dpo', scatter_dimension=0, tiled=True)  174 us
    pallas_call x4, Pallas kernels, attend_backward(): pl.pallas_call(partial(backward_kernel, k_at, v_at, dk_at, dv_at, min(256...  127 us
    pallas_call x4, Pallas kernels, attend_forward(): pl.pallas_call(partial(forward_kernel, k_at, v_at, min(256, rows)), grid=...  88.4 us
    unnamed x12, waiting for transfers between devices  69.9 us
    ppermute x15, waiting for transfers between devices, swap_tensor(): return lax.ppermute(x, 'tensor', [(0, 1), (1, 0)])  68.1 us
    all_gather x4, waiting for transfers between devices, per_device(): own = lax.all_gather(joined, 'dpo', axis=0, tiled=True)  59.2 us
    unnamed x175, local copies, waits for them, and re-layouts  32.9 us
  transfers between devices with their start and end apart: 38, of which 14 were waited for; matrix products, arithmetic and copies ran while one was open for 41% of the time, Pallas kernels for 17%

profile of v1, /device:TPU:0, one launch (start us, length us, event | category | flops | bytes accessed | tf_op | source)
XLA Modules:
  0.0 1257.2 jit_solution(6499041175574497211)
XLA Ops:
  17.9 3.0 collective-permute-start.3
  25.2 18.1 %collective-permute-done.3 = bf16[144,3456]{1,0:T(8,128)(2,1)} collective-permute-done((bf16[144,3456]{1,0:T(8,128)(2,1)S(1)}, bf16[144,3456]{1,0:T(8,128)(2,1)}, u32[]{:S(2)}, u32[]{:S(2)}) %collective-permute-start.3) | collective-permute-done | bytes 995360 | tf_op jit(solution)/shard_map/ppermute | solution.py:246
  57.9 3.3 dynamic-slice_bitcast_fusion.3
  62.9 4.0 dynamic-slice_bitcast_fusion.1
  72.7 69.7 %all-reduce.9.cloned.1.call-done = f32[48,3456]{1,0:T(8,128)} async-done(((f32[48,3456]{1,0:T(8,128)}), f32[48,3456]{1,0:T(8,128)}) %all-reduce.9.cloned.1.call-update) | async-done | bytes 663568
  175.0 3.2 multiply_reduce_fusion.7
  178.8 5.4 fusion.19
  184.3 3.4 fusion.68
  187.6 10.4 add_convert_fusion.1.q_ref.kv_ref
  198.0 2.5 copy-done.38
  202.9 4.5 maximum_convert_fusion
  209.3 5.3 convert_reduce_fusion.2
  215.4 25.5 %attend_forward.4 = (bf16[1024,640]{1,0:T(8,128)(2,1)}, f32[8,1024]{1,0:T(8,128)}) custom-call(bf16[1536,1792]{1,0:T(8,128)(2,1)} %copy-done.38, bf16[1536,1792]{1,0:T(8,128)(2,1)} %copy-done.38), custom_call_target="tpu_custom_call" | custom-call | flops 8589934592 | bytes 7340032 | tf_op jit(solution)/shard_map/attend_forward/pallas_call | solution.py:151
  240.9 2.6 constant_dynamic-update-slice_fusion.1
  243.4 3.3 pad_maximum_fusion.9.kv_ref
  246.7 18.8 %attend_forward.5 = (bf16[512,640]{1,0:T(8,128)(2,1)}, f32[8,512]{1,0:T(8,128)}) custom-call(bf16[1536,1792]{1,0:T(8,128)(2,1)} %copy-done.38, bf16[1024,1152]{1,0:T(8,128)(2,1)} %pad_maximum_fusion.9.kv_ref), custom_call_target="tpu_custom_call" | custom-call | flops 4294967296 | bytes 5505024 | tf_op jit(solution)/shard_map/attend_forward/pallas_call | solution.py:151
  267.6 10.2 add_convert_fusion.q_ref.kv_ref
  283.5 5.2 fusion.78
  288.8 59.2 %all-gather.14.cloned.1.call-done = bf16[1152,2304]{1,0:T(8,128)(2,1)} async-done(((bf16[144,2304]{1,0:T(8,128)(2,1)}), bf16[1152,2304]{1,0:T(8,128)(2,1)}) %all-gather.14.cloned.1.call-update) | async-done | bytes 5308432 | tf_op jit(solution)/shard_map/all_gather | solution.py:341
  348.0 25.5 %attend_forward.6 = (bf16[1024,640]{1,0:T(8,128)(2,1)}, f32[8,1024]{1,0:T(8,128)}) custom-call(bf16[1536,1792]{1,0:T(8,128)(2,1)} %copy-done.39, bf16[1536,1792]{1,0:T(8,128)(2,1)} %copy-done.39), custom_call_target="tpu_custom_call" | custom-call | flops 8589934592 | bytes 7340032 | tf_op jit(solution)/shard_map/attend_forward/pallas_call | solution.py:151
  375.0 3.2 pad_maximum_fusion.10.kv_ref
  378.2 18.6 %attend_forward.7 = (bf16[512,640]{1,0:T(8,128)(2,1)}, f32[8,512]{1,0:T(8,128)}) custom-call(bf16[1536,1792]{1,0:T(8,128)(2,1)} %copy-done.39, bf16[1024,1152]{1,0:T(8,128)(2,1)} %pad_maximum_fusion.10.kv_ref), custom_call_target="tpu_custom_call" | custom-call | flops 4294967296 | bytes 5505024 | tf_op jit(solution)/shard_map/attend_forward/pallas_call | solution.py:151
  398.0 10.7 fusion.73
  413.7 12.1 convolution_add_fusion.1
  425.8 21.3 %convert_reduce_fusion.1 = (f32[2304]{0:T(1024)}, bf16[1536,2304]{1,0:T(8,128)(2,1)S(1)}) fusion(f32[1536,2304]{1,0:T(8,128)} %convolution_add_fusion.1, bf16[1536,1152]{1,0:T(8,128)(2,1)S(1)} %copy-done.27, bf16[1152,2304]{1,0:T(8,128)(2,1)} %all-gather.14.cloned.1.call-done), kind=kOutput, calls=%fused_computation.22 | convolution fusion | flops 8231581696 | bytes 30090240 | tf_op jit(solution)/shard_map/dot_general | solution.py:26
  447.1 2.9 copy-done.66
  450.0 11.3 fusion.79
  463.3 18.9 %fusion.67 = f32[1536,1152]{1,0:T(8,128)} fusion(bf16[1152,2304]{1,0:T(8,128)(2,1)} %all-gather.14.cloned.1.call-done, f32[1536,2304]{1,0:T(8,128)} %convolution_add_fusion.1), kind=kOutput, calls=%fused_computation.287 | convolution fusion | flops 8185577472 | bytes 26542080 | tf_op jit(solution)/shard_map/dot_general | solution.py:26
  482.2 14.6 %convolution_add_fusion = f32[1536,2304]{1,0:T(8,128)} fusion(bf16[1536,1152]{1,0:T(8,128)(2,1)S(1)} %fusion.23, bf16[1152,2304]{1,0:T(8,128)(2,1)} %collective-permute-done.8, f32[2304]{0:T(1024)S(1)} %copy-done.56), kind=kOutput, calls=%fused_computation.25 | convolution fusion | flops 8157265920 | bytes 23012352 | tf_op jit(solution)/shard_map/dot_general | solution.py:26
  496.8 20.8 %convert_reduce_fusion = (f32[2304]{0:T(1024)S(1)}, bf16[1536,2304]{1,0:T(8,128)(2,1)S(1)}) fusion(f32[1536,2304]{1,0:T(8,128)} %convolution_add_fusion, bf16[1536,1152]{1,0:T(8,128)(2,1)S(1)} %copy-done.28, bf16[1152,2304]{1,0:T(8,128)(2,1)} %collective-permute-done.9), kind=kOutput, calls=%fused_computation.21 | convolution fusion | flops 8231581696 | bytes 30090240 | tf_op jit(solution)/shard_map/dot_general | solution.py:26
  517.7 18.0 %fusion.26 = (f32[1536]{0:T(1024)S(1)}, f32[1536]{0:T(1024)S(1)}, f32[1536,1152]{1,0:T(8,128)}) fusion(f32[3,1152]{1,0:T(4,128)S(1)} %bitcast.345, f32[1536]{0:T(1024)S(1)} %copy-done.41, f32[1536,1152]{1,0:T(8,128)S(1)} %bitcast.303, f32[1536]{0:T(1024)S(1)} %broadcast_multiply_fusion.4, f32[1536,1152]{1,0:T(8,128)} %fusion.79, ...), kind=kOutput, calls=%fused_computation.78 | convolution fusion | flops 8166110208 | bytes 33658368 | tf_op jit(solution)/shard_map/dot_general | solution.py:26
  537.0 8.7 convert_reduce_fusion.3
  545.8 4.1 convolution_convert_fusion.8
  550.4 5.7 convolution_convert_fusion.6.do_ref
  556.1 39.5 %attend_backward.6 = bf16[1024,1792]{1,0:T(8,128)(2,1)} custom-call(bf16[1536,1792]{1,0:T(8,128)(2,1)} %copy-done.39, bf16[1536,1792]{1,0:T(8,128)(2,1)} %copy-done.39, bf16[1536,640]{1,0:T(8,128)(2,1)} %convolution_convert_fusion.6.do_ref, f32[8,1024]{1,0:T(8,128)} %get-tuple-element.32.log_ref), custom_call_target="tpu_custom_call" | custom-call | flops 21474836480 | bytes 14680064 | tf_op jit(solution)/shard_map/attend_backward/pallas_call | solution.py:187
  595.5 24.0 %attend_backward.7 = (bf16[512,640]{1,0:T(8,128)(2,1)}, bf16[1024,1152]{1,0:T(8,128)(2,1)}) custom-call(bf16[1536,1792]{1,0:T(8,128)(2,1)} %copy-done.39, bf16[1024,1152]{1,0:T(8,128)(2,1)} %pad_maximum_fusion.10.kv_ref, bf16[1536,640]{1,0:T(8,128)(2,1)} %convolution_convert_fusion.6.do_ref, f32[8,512]{1,0:T(8,128)} %get-tuple-element.33.log_ref), custom_call_target="tpu_custom_call" | custom-call | flops 10737418240 | bytes 11010048 | tf_op jit(solution)/shard_map/attend_backward/pallas_call | solution.py:187
  622.4 6.1 convolution_convert_fusion.7.do_ref
  628.5 24.1 %attend_backward.5 = (bf16[512,640]{1,0:T(8,128)(2,1)}, bf16[1024,1152]{1,0:T(8,128)(2,1)}) custom-call(bf16[1536,1792]{1,0:T(8,128)(2,1)} %copy-done.38, bf16[1024,1152]{1,0:T(8,128)(2,1)} %pad_maximum_fusion.9.kv_ref, bf16[1536,640]{1,0:T(8,128)(2,1)} %convolution_convert_fusion.7.do_ref, f32[8,512]{1,0:T(8,128)} %get-tuple-element.29.log_ref), custom_call_target="tpu_custom_call" | custom-call | flops 10737418240 | bytes 11010048 | tf_op jit(solution)/shard_map/attend_backward/pallas_call | solution.py:187
  657.1 18.0 %fusion.17 = f32[1536,1152]{1,0:T(8,128)} fusion(f32[1536,1152]{1,0:T(8,128)} %fusion.67, bf16[1152,2304]{1,0:T(8,128)(2,1)} %collective-permute-done.9, f32[1152]{0:T(1024)S(1)} %copy-done.59, f32[1536,2304]{1,0:T(8,128)} %convolution_add_fusion), kind=kOutput, calls=%fused_computation.48 | convolution fusion | flops 8189116416 | bytes 33624576 | tf_op jit(solution)/shard_map/dot_general | solution.py:26
  675.1 39.9 %attend_backward.4 = bf16[1024,1792]{1,0:T(8,128)(2,1)} custom-call(bf16[1536,1792]{1,0:T(8,128)(2,1)} %copy-done.38, bf16[1536,1792]{1,0:T(8,128)(2,1)} %copy-done.38, bf16[1536,640]{1,0:T(8,128)(2,1)} %convolution_convert_fusion.7.do_ref, f32[8,1024]{1,0:T(8,128)} %get-tuple-element.28.log_ref), custom_call_target="tpu_custom_call" | custom-call | flops 21474836480 | bytes 14680064 | tf_op jit(solution)/shard_map/attend_backward/pallas_call | solution.py:187
  715.3 2.8 concatenate.142
  718.1 12.4 convolution_convert_fusion.4
  734.0 2.8 concatenate.140
  736.8 3.0 convert_reduce_fusion.7
  741.2 13.4 %fusion.27 = f32[1536,1152]{1,0:T(8,128)} fusion(bf16[1152,1792]{1,0:T(8,128)(2,1)} %all-gather.8.cloned.1.call-done, bf16[512,1792]{1,0:T(8,128)(2,1)} %copy-done.16, bf16[1024,1792]{1,0:T(8,128)(2,1)} %attend_backward.4), kind=kOutput, calls=%fused_computation.86 | convolution fusion | flops 6352797696 | bytes 16711680 | tf_op jit(solution)/shard_map/dot_general | solution.py:26
  754.7 15.9 %fusion.25 = (f32[1536]{0:T(1024)S(1)}, f32[1536]{0:T(1024)S(1)}, f32[1536,1152]{1,0:T(8,128)}) fusion(f32[3,1152]{1,0:T(4,128)S(1)} %bitcast.352, f32[1536]{0:T(1024)S(1)} %copy-done.45, f32[1536]{0:T(1024)S(1)} %copy-done.43, bf16[512,1152]{1,0:T(8,128)(2,1)S(1)} %copy-done.7, bf16[512,1152]{1,0:T(8,128)(2,1)S(1)} %copy-done.9, ...), kind=kOutput, calls=%fused_computation.76 | convolution fusion | flops 6375797760 | bytes 27366912 | tf_op jit(solution)/shard_map/dot_general | solution.py:26
  771.8 16.0 %multiply_reduce_fusion.1 = (f32[3,1152]{1,0:T(4,128)S(1)}, f32[3,1152]{1,0:T(4,128)S(1)}, f32[3,1152]{1,0:T(4,128)S(1)}, f32[3,1152]{1,0:T(4,128)S(1)}, f32[3,1...) fusion(f32[3,512,1152]{2,1,0:T(8,128)} %bitcast.308, f32[3,512]{1,0:T(4,128)} %rsqrt.26, ...), kind=kLoop, calls=%fused_computation.63 | loop fusion | flops 53063424 | bytes 46179852 | tf_op jit(solution)/shard_map/reduce_sum | solution.py:423
  811.2 3.3 collective-permute-done.15
  815.4 21.3 %all-gather.2 = f32[16,1,14976]{2,1,0:T(1,128)S(1)} all-gather(f32[1,1,14976]{2,1,0:T(1,128)S(1)} %reshape.900), channel_id=2, replica_groups=mesh['dpo'=8,'core'=2,'tensor'=2] {'dpo','core'}, dimensions={0}, use_global_device_ids=true | all-gather | bytes 1018368 | tf_op jit(solution)/shard_map/all_gather | solution.py:523
  851.1 7.1 fusion.30
  858.3 12.7 %add_convert_fusion.4 = bf16[1152,1792]{1,0:T(8,128)(2,1)} fusion(bf16[1152,1792]{1,0:T(8,128)(2,1)} %collective-permute-done.16, bf16[1536,1152]{1,0:T(8,128)(2,1)} %fusion.19, bf16[512,1792]{1,0:T(8,128)(2,1)} %copy-done.16, bf16[1024,1792]{1,0:T(8,128)(2,1)} %attend_backward.4), kind=kOutput, calls=%fused_computation.49 | convolution fusion | flops 6363119616 | bytes 17301504 | tf_op jit(solution)/shard_map/dot_general | solution.py:26
  871.2 14.1 %convolution_convert_fusion = bf16[1152,2304]{1,0:T(8,128)(2,1)S(1)} fusion(bf16[1536,1152]{1,0:T(8,128)(2,1)} %get-tuple-element.63, f32[1536,2304]{1,0:T(8,128)} %convolution_add_fusion), kind=kOutput, calls=%fused_computation.27 | convolution fusion | flops 8188231680 | bytes 23003136 | tf_op jit(solution)/shard_map/dot_general | solution.py:26
  885.9 8.4 collective-permute-done.25
  894.3 14.9 %add_convert_fusion.2 = bf16[1152,2304]{1,0:T(8,128)(2,1)} fusion(bf16[1152,2304]{1,0:T(8,128)(2,1)S(1)} %collective-permute-done.25, bf16[1536,1152]{1,0:T(8,128)(2,1)S(1)} %copy-done.29, f32[1536,2304]{1,0:T(8,128)} %convolution_add_fusion.1), kind=kOutput, calls=%fused_computation.41 | convolution fusion | flops 8198848512 | bytes 28311552 | tf_op jit(solution)/shard_map/dot_general | solution.py:26
  909.6 13.0 %convolution_convert_fusion.2 = bf16[1152,2304]{1,0:T(8,128)(2,1)S(1)} fusion(bf16[1536,1152]{1,0:T(8,128)(2,1)} %copy-done.24, bf16[1536,2304]{1,0:T(8,128)(2,1)} %copy-done.17), kind=kOutput, calls=%fused_computation.30 | convolution fusion | flops 8156381184 | bytes 15925248 | tf_op jit(solution)/shard_map/dot_general | solution.py:26
  922.9 8.4 collective-permute-done.22
  931.3 13.3 %add_convert_fusion.3 = bf16[1152,2304]{1,0:T(8,128)(2,1)} fusion(bf16[1152,2304]{1,0:T(8,128)(2,1)S(1)} %collective-permute-done.22, bf16[1536,1152]{1,0:T(8,128)(2,1)S(1)} %copy-done.25, bf16[1536,2304]{1,0:T(8,128)(2,1)} %copy-done.66), kind=kOutput, calls=%fused_computation.42 | convolution fusion | flops 8166998016 | bytes 21233664 | tf_op jit(solution)/shard_map/dot_general | solution.py:26
  944.7 10.8 multiply_convert_fusion.2
  961.0 25.9 %collective-permute-done.10 = bf16[512,1152]{1,0:T(8,128)(2,1)S(1)} collective-permute-done((bf16[512,1152]{1,0:T(8,128)(2,1)S(1)}, bf16[512,1152]{1,0:T(8,128)(2,1)S(1)}, u32[]{:S(2)}, u32[]{:S(2)}) %collective-permute-start.10) | collective-permute-done | bytes 1179680 | tf_op jit(solution)/shard_map/ppermute | solution.py:246
  993.2 2.8 fusion.31
  1035.6 6.8 collective-permute-done.17
  1044.9 72.9 %reduce-scatter.11.cloned.1.call-done = bf16[144,2304]{1,0:T(8,128)(2,1)} async-done(((bf16[1152,2304]{1,0:T(8,128)(2,1)}), bf16[144,2304]{1,0:T(8,128)(2,1)}) %reduce-scatter.11.cloned.1.call-update) | async-done | bytes 663568 | tf_op jit(solution)/shard_map/reduce_scatter | solution.py:473
  1124.0 101.4 %reduce-scatter.9.cloned.1.call-done = bf16[144,2304]{1,0:T(8,128)(2,1)} async-done(((bf16[1152,2304]{1,0:T(8,128)(2,1)}), bf16[144,2304]{1,0:T(8,128)(2,1)}) %reduce-scatter.9.cloned.1.call-update) | async-done | bytes 663568 | tf_op jit(solution)/shard_map/reduce_scatter | solution.py:473
  1230.9 13.7 %collective-permute-done.23 = bf16[144,1,1152]{2,1,0:T(2,128)(2,1)S(1)} collective-permute-done((bf16[144,1,1152]{2,1,0:T(2,128)(2,1)S(1)}, bf16[144,1,1152]{2,1,0:T(2,128)(2,1)S(1)}, u32[]{:S(2)}, u32[]{:S(2)}) %collective-permute-start.23) | collective-permute-done | bytes 331808 | tf_op jit(solution)/shard_map/ppermute | solution.py:246
  (449 shorter events, 216.5 us)
Async XLA Ops:
  8.0 134.4 %all-reduce.9.cloned.1.call-start = ((), (), s32[]{:S(2)}) async-start(), calls=%async_computation.13 | async-start | bytes 1327104
  14.6 2.1 collective-permute-start.2
  16.3 28.6 %copy-start.21 = (bf16[72,3456]{1,0:T(8,128)(2,1)}, bf16[72,3456]{1,0:T(8,128)(2,1)S(1)}, u32[]{:S(2)}) copy-start(bf16[72,3456]{1,0:T(8,128)(2,1)S(1)} %reshape.799) | copy-start | bytes 1492996
  17.9 25.4 %collective-permute-start.3 = (bf16[144,3456]{1,0:T(8,128)(2,1)S(1)}, bf16[144,3456]{1,0:T(8,128)(2,1)}, u32[]{:S(2)}, u32[]{:S(2)}) collective-permute-start(bf16[144,3456]{1,0:T(8,128)(2,1)S(1)} %pad_maximum_fusion.11), channel_id=1, source_target_pairs={{0,1},{1,0},{2,3},{3,2},{4,5},{5,4},{6,7},{7,6},{8,9},{9,8},{10,11... | collective-permute-start | bytes 2985992 | tf_op jit(solution)/shard_map/ppermute | solution.py:246
  25.1 162.5 %all-gather.8.cloned.1.call-start = ((), (), s32[]{:S(2)}) async-start(), calls=%async_computation.4 | async-start | bytes 4644864 | tf_op jit(solution)/shard_map/all_gather | solution.py:341
  52.8 162.5 %all-gather.10.cloned.1.call-start = ((), (), s32[]{:S(2)}) async-start(), calls=%async_computation.5 | async-start | bytes 1658880 | tf_op jit(solution)/shard_map/all_gather | solution.py:341
  54.2 234.5 %all-gather.12.cloned.1.call-start = ((), (), s32[]{:S(2)}) async-start(), calls=%async_computation.6 | async-start | bytes 5971968 | tf_op jit(solution)/shard_map/all_gather | solution.py:341
  57.4 290.6 %all-gather.14.cloned.1.call-start = ((), (), s32[]{:S(2)}) async-start(), calls=%async_computation.7 | async-start | bytes 5971968 | tf_op jit(solution)/shard_map/all_gather | solution.py:341
  61.2 336.8 %copy-start.4 = (bf16[512,1152]{1,0:T(8,128)(2,1)}, bf16[512,1152]{1,0:T(8,128)(2,1)S(1)}, u32[]{:S(2)}) copy-start(bf16[512,1152]{1,0:T(8,128)(2,1)S(1)} %get-tuple-element.82) | copy-start | bytes 3538948
  61.2 336.8 %copy-start.6 = (bf16[512,1152]{1,0:T(8,128)(2,1)}, bf16[512,1152]{1,0:T(8,128)(2,1)S(1)}, u32[]{:S(2)}) copy-start(bf16[512,1152]{1,0:T(8,128)(2,1)S(1)} %get-tuple-element.83) | copy-start | bytes 3538948
  61.2 85.9 %copy-start.54 = (bf16[2,1152]{1,0:T(2,128)(2,1)S(1)}, bf16[2,1152]{1,0:T(2,128)(2,1)}, u32[]{:S(2)}) copy-start(bf16[2,1152]{1,0:T(2,128)(2,1)} %param.27) | copy-start | bytes 13828
  61.2 109.0 %collective-permute-start = (bf16[512,1152]{1,0:T(8,128)(2,1)}, bf16[512,1152]{1,0:T(8,128)(2,1)S(1)}, u32[]{:S(2)}, u32[]{:S(2)}) collective-permute-start(bf16[512,1152]{1,0:T(8,128)(2,1)} %get-tuple-element.84), channel_id=1, source_target_pairs={{0,1},{1,0},{2,3},{3,2},{4,5},{5,4},{6,7},{7,6},{8,9},{9,8},{10,11... | collective-permute-start | bytes 3538952 | tf_op jit(solution)/shard_map/ppermute | solution.py:246
  66.9 136.0 %collective-permute-start.11 = (bf16[512,1152]{1,0:T(8,128)(2,1)}, bf16[512,1152]{1,0:T(8,128)(2,1)}, u32[]{:S(2)}, u32[]{:S(2)}) collective-permute-start(bf16[512,1152]{1,0:T(8,128)(2,1)} %get-tuple-element.79), channel_id=1, source_target_pairs={{0,1},{1,0},{2,3},{3,2},{4,5},{5,4},{6,7},{7,6},{8,9},{9,8},{10,11... | collective-permute-start | bytes 3538952 | tf_op jit(solution)/shard_map/ppermute | solution.py:246
  145.5 18.4 %collective-permute-start.1 = (f32[3,6,576]{2,1,0:T(8,128)}, f32[3,6,576]{2,1,0:T(8,128)}, u32[]{:S(2)}, u32[]{:S(2)}) collective-permute-start(f32[3,6,576]{2,1,0:T(8,128)} %reshape.800), channel_id=1, source_target_pairs={{0,1},{1,0},{2,3},{3,2},{4,5},{5,4},{6,7},{7,6},{8,9},{9,8},{10,11... | collective-permute-start | bytes 124424 | tf_op jit(solution)/shard_map/ppermute | solution.py:246
  170.2 227.7 %copy-start.8 = (bf16[512,1152]{1,0:T(8,128)(2,1)}, bf16[512,1152]{1,0:T(8,128)(2,1)S(1)}, u32[]{:S(2)}) copy-start(bf16[512,1152]{1,0:T(8,128)(2,1)S(1)} %collective-permute-done) | copy-start | bytes 3538948
  172.3 36.4 %copy-start.42 = (f32[1536]{0:T(1024)}, f32[1536]{0:T(1024)S(1)}, u32[]{:S(2)}) copy-start(f32[1536]{0:T(1024)S(1)} %broadcast_multiply_fusion.5) | copy-start | bytes 18436
  175.0 821.1 %all-reduce.7.cloned.1.call-start = ((), (), s32[]{:S(2)}) async-start(), calls=%async_computation.12 | async-start | bytes 663552
  187.6 79.9 %collective-permute-start.5 = (bf16[1152,1792]{1,0:T(8,128)(2,1)}, bf16[1152,1792]{1,0:T(8,128)(2,1)}, u32[]{:S(2)}, u32[]{:S(2)}) collective-permute-start(bf16[1152,1792]{1,0:T(8,128)(2,1)} %all-gather.8.cloned.1.call-done), channel_id=1, source_target_pairs={{0,2},{2,0},{1,3},{3,1},{4,6},{6,4},{5,7},{7,5},{8,10},{10,8},{9,1... | collective-permute-start | bytes 12386312 | tf_op jit(solution)/shard_map/ppermute | solution.py:243
  202.3 41.1 %collective-permute-start.4 = (bf16[512,1152]{1,0:T(8,128)(2,1)}, bf16[512,1152]{1,0:T(8,128)(2,1)}, u32[]{:S(2)}, u32[]{:S(2)}) collective-permute-start(bf16[512,1152]{1,0:T(8,128)(2,1)} %slice.233), channel_id=1, source_target_pairs={{0,1},{1,0},{2,3},{3,2},{4,5},{5,4},{6,7},{7,6},{8,9},{9,8},{10,11... | collective-permute-start | bytes 3538952 | tf_op jit(solution)/shard_map/ppermute | solution.py:246
  215.3 182.6 %collective-permute-start.7 = (bf16[1152,640]{1,0:T(8,128)(2,1)}, bf16[1152,640]{1,0:T(8,128)(2,1)}, u32[]{:S(2)}, u32[]{:S(2)}) collective-permute-start(bf16[1152,640]{1,0:T(8,128)(2,1)} %all-gather.10.cloned.1.call-done), channel_id=1, source_target_pairs={{0,2},{2,0},{1,3},{3,1},{4,6},{6,4},{5,7},{7,5},{8,10},{10,8},{9,1... | collective-permute-start | bytes 4423688 | tf_op jit(solution)/shard_map/ppermute | solution.py:243
  246.7 20.9 %copy-start.23 = (bf16[1536,1152]{1,0:T(8,128)(2,1)S(1)}, bf16[1536,1152]{1,0:T(8,128)(2,1)}, u32[]{:S(2)}) copy-start(bf16[1536,1152]{1,0:T(8,128)(2,1)} %fusion.19) | copy-start | bytes 10616836
  246.7 20.9 %copy-start.60 = (f32[1792]{0:T(1024)S(1)}, f32[1792]{0:T(1024)}, u32[]{:S(2)}) copy-start(f32[1792]{0:T(1024)} %concatenate.134) | copy-start | bytes 21508
  282.0 92.9 %collective-permute-start.6 = (bf16[512,1152]{1,0:T(8,128)(2,1)}, bf16[512,1152]{1,0:T(8,128)(2,1)}, u32[]{:S(2)}, u32[]{:S(2)}) collective-permute-start(bf16[512,1152]{1,0:T(8,128)(2,1)} %slice.236), channel_id=1, source_target_pairs={{0,1},{1,0},{2,3},{3,2},{4,5},{5,4},{6,7},{7,6},{8,9},{9,8},{10,11... | collective-permute-start | bytes 3538952 | tf_op jit(solution)/shard_map/ppermute | solution.py:246
  288.7 193.5 %collective-permute-start.8 = (bf16[1152,2304]{1,0:T(8,128)(2,1)}, bf16[1152,2304]{1,0:T(8,128)(2,1)}, u32[]{:S(2)}, u32[]{:S(2)}) collective-permute-start(bf16[1152,2304]{1,0:T(8,128)(2,1)} %all-gather.12.cloned.1.call-done), channel_id=1, source_target_pairs={{0,2},{2,0},{1,3},{3,1},{4,6},{6,4},{5,7},{7,5},{8,10},{10,8},{9,1... | collective-permute-start | bytes 15925256 | tf_op jit(solution)/shard_map/ppermute | solution.py:243
  348.0 148.8 %collective-permute-start.9 = (bf16[1152,2304]{1,0:T(8,128)(2,1)}, bf16[1152,2304]{1,0:T(8,128)(2,1)}, u32[]{:S(2)}, u32[]{:S(2)}) collective-permute-start(bf16[1152,2304]{1,0:T(8,128)(2,1)} %all-gather.14.cloned.1.call-done), channel_id=1, source_target_pairs={{0,2},{2,0},{1,3},{3,1},{4,6},{6,4},{5,7},{7,5},{8,10},{10,8},{9,1... | collective-permute-start | bytes 15925256 | tf_op jit(solution)/shard_map/ppermute | solution.py:243
  378.2 19.8 %copy-start.33 = (f32[3,1,1152]{2,0,1:T(4,128)S(1)}, f32[3,1,1152]{2,0,1:T(4,128)}, u32[]{:S(2)}) copy-start(f32[3,1,1152]{2,0,1:T(4,128)} %copy.145) | copy-start | bytes 41476
  378.2 19.8 %copy-start.51 = (f32[1152]{0:T(1024)S(1)}, f32[1152]{0:T(1024)}, u32[]{:S(2)}) copy-start(f32[1152]{0:T(1024)} %get-tuple-element.59) | copy-start | bytes 13828
  413.7 68.4 %copy-start.24 = (bf16[1536,1152]{1,0:T(8,128)(2,1)}, bf16[1536,1152]{1,0:T(8,128)(2,1)S(1)}, u32[]{:S(2)}) copy-start(bf16[1536,1152]{1,0:T(8,128)(2,1)S(1)} %fusion.23) | copy-start | bytes 10616836
  482.2 35.4 %slice-start = ((s8[7077888]{0:T(1024)(128)(4,1)}), s8[4194304]{0:T(1024)(128)(4,1)S(1)}, s32[]{:S(2)}) async-start(s8[7077888]{0:T(1024)(128)(4,1)} %bitcast.302), calls=%async_computation.14 | async-start | bytes 8388608
  496.8 20.8 %slice-start.1 = ((s8[7077888]{0:T(1024)(128)(4,1)}), s8[2883584]{0:T(1024)(128)(4,1)S(1)}, s32[]{:S(2)}) async-start(s8[7077888]{0:T(1024)(128)(4,1)} %bitcast.302), calls=%async_computation.15 | async-start | bytes 5767168
  496.8 20.8 %copy-start.36 = (f32[3,1,1152]{2,0,1:T(4,128)S(1)}, f32[3,1,1152]{2,0,1:T(4,128)}, u32[]{:S(2)}) copy-start(f32[3,1,1152]{2,0,1:T(4,128)} %copy.141) | copy-start | bytes 41476
  496.8 20.8 %copy-start.41 = (f32[1536]{0:T(1024)S(1)}, f32[1536]{0:T(1024)}, u32[]{:S(2)}) copy-start(f32[1536]{0:T(1024)} %copy-done.40) | copy-start | bytes 18436
  517.7 19.3 %copy-start.11 = (bf16[512,1152]{1,0:T(8,128)(2,1)S(1)}, bf16[512,1152]{1,0:T(8,128)(2,1)}, u32[]{:S(2)}) copy-start(bf16[512,1152]{1,0:T(8,128)(2,1)} %get-tuple-element.77) | copy-start | bytes 3538948
  517.7 19.3 %copy-start.13 = (bf16[512,1152]{1,0:T(8,128)(2,1)S(1)}, bf16[512,1152]{1,0:T(8,128)(2,1)}, u32[]{:S(2)}) copy-start(bf16[512,1152]{1,0:T(8,128)(2,1)} %get-tuple-element.78) | copy-start | bytes 3538948
  545.7 76.7 %copy-start.26 = (bf16[1536,1152]{1,0:T(8,128)(2,1)}, bf16[1536,1152]{1,0:T(8,128)(2,1)S(1)}, u32[]{:S(2)}) copy-start(bf16[1536,1152]{1,0:T(8,128)(2,1)S(1)} %get-tuple-element.61) | copy-start | bytes 10616836
  549.9 301.2 %collective-permute-start.19 = (bf16[1152,640]{1,0:T(8,128)(2,1)}, bf16[1152,640]{1,0:T(8,128)(2,1)}, u32[]{:S(2)}, u32[]{:S(2)}) collective-permute-start(bf16[1152,640]{1,0:T(8,128)(2,1)} %convolution_convert_fusion.8), channel_id=1, source_target_pairs={{0,2},{2,0},{1,3},{3,1},{4,6},{6,4},{5,7},{7,5},{8,10},{10,8},{9,1... | collective-permute-start | bytes 4423688 | tf_op jit(solution)/shard_map/ppermute | solution.py:243
  620.9 94.1 %collective-permute-start.13 = (bf16[512,1152]{1,0:T(8,128)(2,1)S(1)}, bf16[512,1152]{1,0:T(8,128)(2,1)S(1)}, u32[]{:S(2)}, u32[]{:S(2)}) collective-permute-start(bf16[512,1152]{1,0:T(8,128)(2,1)S(1)} %slice.202), channel_id=1, source_target_pairs={{0,1},{1,0},{2,3},{3,2},{4,5},{5,4},{6,7},{7,6},{8,9},{9,8},{10,11... | collective-permute-start | bytes 3538952 | tf_op jit(solution)/shard_map/ppermute | solution.py:246
  628.5 27.0 %copy-start.58 = (f32[2304]{0:T(1024)S(1)}, f32[2304]{0:T(1024)}, u32[]{:S(2)}) copy-start(f32[2304]{0:T(1024)} %get-tuple-element.64) | copy-start | bytes 27652
  628.5 27.8 %copy-start.53 = (f32[1,2,576]{2,0,1:T(1,128)S(1)}, f32[1,2,576]{2,0,1:T(1,128)}, u32[]{:S(2)}) copy-start(f32[1,2,576]{2,0,1:T(1,128)} %stack.103) | copy-start | bytes 13828
  628.5 28.5 %copy-start.59 = (f32[1152]{0:T(1024)S(1)}, f32[1152]{0:T(1024)}, u32[]{:S(2)}) copy-start(f32[1152]{0:T(1024)} %get-tuple-element.58) | copy-start | bytes 13828
  655.0 77.1 %collective-permute-start.12 = (bf16[512,1152]{1,0:T(8,128)(2,1)}, bf16[512,1152]{1,0:T(8,128)(2,1)}, u32[]{:S(2)}, u32[]{:S(2)}) collective-permute-start(bf16[512,1152]{1,0:T(8,128)(2,1)} %slice.199), channel_id=1, source_target_pairs={{0,1},{1,0},{2,3},{3,2},{4,5},{5,4},{6,7},{7,6},{8,9},{9,8},{10,11... | collective-permute-start | bytes 3538952 | tf_op jit(solution)/shard_map/ppermute | solution.py:246
  675.1 39.9 %copy-start.30 = (bf16[1024,1152]{1,0:T(8,128)(2,1)S(1)}, bf16[1024,1152]{1,0:T(8,128)(2,1)}, u32[]{:S(2)}) copy-start(bf16[1024,1152]{1,0:T(8,128)(2,1)} %get-tuple-element.35) | copy-start | bytes 7077892
  730.5 127.7 %collective-permute-start.16 = (bf16[1152,1792]{1,0:T(8,128)(2,1)}, bf16[1152,1792]{1,0:T(8,128)(2,1)}, u32[]{:S(2)}, u32[]{:S(2)}) collective-permute-start(bf16[1152,1792]{1,0:T(8,128)(2,1)} %convolution_convert_fusion.4), channel_id=1, source_target_pairs={{0,2},{2,0},{1,3},{3,1},{4,6},{6,4},{5,7},{7,5},{8,10},{10,8},{9,1... | collective-permute-start | bytes 12386312 | tf_op jit(solution)/shard_map/ppermute | solution.py:243
  771.8 29.9 %copy-start.55 = (f32[1,2,1,288]{3,2,0,1:T(1,128)S(1)}, f32[1,2,1,288]{3,2,0,1:T(1,128)}, u32[]{:S(2)}) copy-start(f32[1,2,1,288]{3,2,0,1:T(1,128)} %stack.97) | copy-start | bytes 6916
  809.7 4.7 collective-permute-start.15
  850.6 177.0 %reduce-scatter.7.cloned.1.call-start = ((), (), s32[]{:S(2)}) async-start(), calls=%async_computation.9 | async-start | bytes 1658880 | tf_op jit(solution)/shard_map/reduce_scatter | solution.py:473
  858.2 172.3 %reduce-scatter.5.cloned.1.call-start = ((), (), s32[]{:S(2)}) async-start(), calls=%async_computation.8 | async-start | bytes 4644864 | tf_op jit(solution)/shard_map/reduce_scatter | solution.py:473
  871.0 246.9 %reduce-scatter.11.cloned.1.call-start = ((), (), s32[]{:S(2)}) async-start(), calls=%async_computation.11 | async-start | bytes 5971968 | tf_op jit(solution)/shard_map/reduce_scatter | solution.py:473
  871.2 23.1 %copy-start.29 = (bf16[1536,1152]{1,0:T(8,128)(2,1)S(1)}, bf16[1536,1152]{1,0:T(8,128)(2,1)}, u32[]{:S(2)}) copy-start(bf16[1536,1152]{1,0:T(8,128)(2,1)} %get-tuple-element.63) | copy-start | bytes 10616836
  885.4 8.9 collective-permute-start.25
  909.3 316.1 %reduce-scatter.9.cloned.1.call-start = ((), (), s32[]{:S(2)}) async-start(), calls=%async_computation.10 | async-start | bytes 5971968 | tf_op jit(solution)/shard_map/reduce_scatter | solution.py:473
  909.5 21.8 %copy-start.25 = (bf16[1536,1152]{1,0:T(8,128)(2,1)S(1)}, bf16[1536,1152]{1,0:T(8,128)(2,1)}, u32[]{:S(2)}) copy-start(bf16[1536,1152]{1,0:T(8,128)(2,1)} %copy-done.24) | copy-start | bytes 10616836
  922.5 22.2 %copy-start.62 = (f32[3]{0:T(128)S(1)}, f32[3]{0:T(128)}, u32[]{:S(2)}) copy-start(f32[3]{0:T(128)} %select_reduce_fusion.2) | copy-start | bytes 40
  922.5 8.8 collective-permute-start.22
  957.3 29.6 %collective-permute-start.10 = (bf16[512,1152]{1,0:T(8,128)(2,1)S(1)}, bf16[512,1152]{1,0:T(8,128)(2,1)S(1)}, u32[]{:S(2)}, u32[]{:S(2)}) collective-permute-start(bf16[512,1152]{1,0:T(8,128)(2,1)S(1)} %get-tuple-element.80), channel_id=1, source_target_pairs={{0,1},{1,0},{2,3},{3,2},{4,5},{5,4},{6,7},{7,6},{8,9},{9,8},{10,11... | collective-permute-start | bytes 3538952 | tf_op jit(solution)/shard_map/ppermute | solution.py:246
  960.5 63.4 %collective-permute-start.14 = (bf16[512,1152]{1,0:T(8,128)(2,1)}, bf16[512,1152]{1,0:T(8,128)(2,1)}, u32[]{:S(2)}, u32[]{:S(2)}) collective-permute-start(bf16[512,1152]{1,0:T(8,128)(2,1)} %get-tuple-element.75), channel_id=1, source_target_pairs={{0,1},{1,0},{2,3},{3,2},{4,5},{5,4},{6,7},{7,6},{8,9},{9,8},{10,11... | collective-permute-start | bytes 3538952 | tf_op jit(solution)/shard_map/ppermute | solution.py:246
  1029.0 6.2 collective-permute-start.20
  1034.2 8.2 collective-permute-start.17
  1035.5 7.3 collective-permute-start.21
  1042.8 1.7 collective-permute-start.18
  1120.5 109.2 %collective-permute-start.26 = (bf16[144,1,1152]{2,1,0:T(2,128)(2,1)S(1)}, bf16[144,1,1152]{2,1,0:T(2,128)(2,1)S(1)}, u32[]{:S(2)}, u32[]{:S(2)}) collective-permute-start(bf16[144,1,1152]{2,1,0:T(2,128)(2,1)S(1)} %dynamic-slice_bitcast_fusion.4), channel_id=1, source_target_pairs={{0,1},{1,0},{2,3},{3,2},{4,5},{5,4},{6,7},{7,6},{8,9},{9,8},{10,11... | collective-permute-start | bytes 995336 | tf_op jit(solution)/shard_map/ppermute | solution.py:246
  1228.2 16.4 %collective-permute-start.23 = (bf16[144,1,1152]{2,1,0:T(2,128)(2,1)S(1)}, bf16[144,1,1152]{2,1,0:T(2,128)(2,1)S(1)}, u32[]{:S(2)}, u32[]{:S(2)}) collective-permute-start(bf16[144,1,1152]{2,1,0:T(2,128)(2,1)S(1)} %dynamic-slice_bitcast_fusion.5), channel_id=1, source_target_pairs={{0,1},{1,0},{2,3},{3,2},{4,5},{5,4},{6,7},{7,6},{8,9},{9,8},{10,11... | collective-permute-start | bytes 995336 | tf_op jit(solution)/shard_map/ppermute | solution.py:246
  1230.8 14.9 %collective-permute-start.27 = (f32[72,1,1,1152]{3,2,0,1:T(1,128)S(1)}, f32[72,1,1,1152]{3,2,0,1:T(1,128)S(1)}, u32[]{:S(2)}, u32[]{:S(2)}) collective-permute-start(f32[72,1,1,1152]{3,2,0,1:T(1,128)S(1)} %dynamic-slice_bitcast_fusion.6), channel_id=1, source_target_pairs={{0,2},{2,0},{1,3},{3,1},{4,6},{6,4},{5,7},{7,5},{8,10},{10,8},{9,1... | collective-permute-start | bytes 995336 | tf_op jit(solution)/shard_map/ppermute | solution.py:243
  1245.6 2.1 collective-permute-start.24
  (45 other events, 418.0 us)
Sparse Core Ops, SparseCore 0:
  25.3 117.1 all-reduce.8
  850.7 133.1 all-reduce.6
Sparse Core Ops, SparseCore 1:
  52.9 74.4 all-gather.7
  130.0 42.2 all-gather.9
  174.9 85.3 all-gather.11
  263.0 84.9 all-gather.13
  858.3 60.8 reduce-scatter.6
  923.1 87.5 reduce-scatter.4
  1014.1 103.7 reduce-scatter.10
  1121.8 103.6 reduce-scatter.8

commit v2 on v1

--- a/solution.py
+++ b/solution.py
@@ -265,7 +265,7 @@
     silu_slots = jnp.dot(picker, silu_here.astype(f32), precision=lax.Precision.HIGHEST).astype(bf16)
 
     ada_flat = w_ada.reshape(drows, 6 * slab)
-    mod_part = dot(silu_slots, ada_flat)
+    mod_part = dot(silu_slots, ada_flat).reshape(dp_size, slots * 6, slab)
     mod_here = lax.psum_scatter(mod_part, ("dpo", "core"), scatter_dimension=0, tiled=True)
     mod_here = mod_here.reshape(slots, 6, slab)
     if tsize == 2:
@@ -317,30 +317,42 @@
     )
     pads = (qkv_w - 3 * hslab, out_w - hslab, 0, 0)
 
-    def side(which):
-        return jnp.concatenate([at(x, which, 2).reshape(drows, -1) for x in shards], axis=1)
-
-    both = in_order(c, side(c), swap_core(side(1 - c)), 0)
-    if tsize == 2:
-        met = swap_tensor(both)
-        by_tensor = [jnp.where(t == 0, both, met), jnp.where(t == 0, met, both)]
-    else:
+    def quad(some):
+        def side(which):
+            parts = [at(x, which, 2).reshape(drows, -1) for x in some]
+            return parts[0] if len(parts) == 1 else jnp.concatenate(parts, axis=1)
+
+        both = in_order(c, side(c), swap_core(side(1 - c)), 0)
+        if tsize == 2:
+            met = swap_tensor(both)
+            return [jnp.where(t == 0, both, met), jnp.where(t == 0, met, both)]
         met = lax.all_gather(both, "tensor", axis=0, tiled=False)
-        by_tensor = [met[i] for i in range(tsize)]
-    gathered = []
-    offset = 0
-    for x, pad in zip(shards, pads):
-        kinds, wide = x.shape[1], x.shape[3]
+        return [met[i] for i in range(tsize)]
+
+    def columns(by_tensor, offset, kinds, wide, pad):
         parts = [
             y[:, offset : offset + kinds * wide].reshape(2 * drows, kinds, 1, wide) for y in by_tensor
         ]
-        offset += kinds * wide
         joined = jnp.concatenate(parts, axis=2).reshape(2 * drows, kinds * tsize * wide)
-        if pad:
-            joined = jnp.pad(joined, ((0, 0), (0, pad)))
-        own = lax.all_gather(joined, "dpo", axis=0, tiled=True)
-        gathered.append((own, swap_core(own)))
-    qkv_ws, out_ws, fc1_ws, fc2_ws = gathered
+        return jnp.pad(joined, ((0, 0), (0, pad))) if pad else joined
+
+    def gather(x):
+        own = lax.all_gather(x, "dpo", axis=0, tiled=True)
+        return own, swap_core(own)
+
+    qkv_ws = gather(columns(quad(shards[:1]), 0, 3, head_w, pads[0]))
+    rest = quad(shards[1:])
+    out_fc1 = jnp.concatenate(
+        [columns(rest, 0, 1, head_w, pads[1]), columns(rest, head_w, 1, fc_w, 0)], axis=1
+    )
+    out_fc1_ws = gather(out_fc1)
+    out_ws = [w[:, :out_w] for w in out_fc1_ws]
+    fc1_ws = [w[:, out_w:] for w in out_fc1_ws]
+    first_w, fc2_cols = lax.optimization_barrier(
+        (qkv_ws[0], columns(rest, head_w + fc_w, 1, fc_w, 0))
+    )
+    qkv_ws = (first_w, qkv_ws[1])
+    fc2_ws = gather(fc2_cols)
 
     def bias_halves(bias, wide):
         parts = bias.astype(f32).reshape(bias.shape[0], tsize, 2, wide)
@@ -403,7 +415,7 @@
 
     grad_out = grouped(cot_in.astype(f32)) * live[:, None, None]
     d_branch_mlp = flat((grad_out * gate_mlp).astype(bf16))
-    hidden, d_pre, grad_fc1, grad_fc2, d_bias_fc1 = [], [], [], [], []
+    hidden, d_pre, d_bias_fc1 = [], [], []
     for w1, w2, b in zip(fc1_ws, fc2_ws, fc1_bias):
         pre_act = dot(mixed_mlp, w1) + b
         act = jax.nn.gelu(pre_act, approximate=True).astype(bf16)
@@ -412,9 +424,17 @@
         d_act = gelu_back(d_hidden)[0].astype(bf16)
         hidden.append(act)
         d_pre.append(d_act)
-        grad_fc1.append(dot(mixed_mlp, d_act, TN).astype(bf16))
-        grad_fc2.append(dot(d_branch_mlp, act, TN).astype(bf16))
         d_bias_fc1.append(jnp.sum(d_act.astype(f32), axis=0))
+
+    def both_cores(left, rights):
+        met = swap_core(dot(left, rights[1], TN).astype(bf16))
+        return (dot(left, rights[0], TN).astype(bf16).astype(f32) + met.astype(f32)).astype(bf16)
+
+    total_fc2 = both_cores(d_branch_mlp, hidden)
+    total_fc1 = both_cores(mixed_mlp, d_pre)
+    hidden, d_pre, total_fc1, total_fc2 = lax.optimization_barrier(
+        (hidden, d_pre, total_fc1, total_fc2)
+    )
     branch_mlp = grouped(sum(dot(h, w, NT) for h, w in zip(hidden, fc2_ws)) + bias_mlp_out)
     out_rows = flat(((middle + gate_mlp * branch_mlp) * live[:, None, None]).astype(bf16))
     d_gate_mlp = jnp.sum(grad_out * branch_mlp, axis=1)
@@ -425,11 +445,11 @@
     d_branch_attn = flat((d_middle * gate_attn).astype(bf16))
     d_gate_attn = jnp.sum(d_middle * branch_attn, axis=1)
 
+    total_out = both_cores(d_branch_attn, mixed_parts)
+    d_branch_attn, total_out = lax.optimization_barrier((d_branch_attn, total_out))
     d_qkv = []
-    grad_out_w = []
-    for x, w, mixed, logs, keys_by_segment in zip(qkv, out_ws, mixed_parts, log_parts, key_parts):
+    for x, w, logs, keys_by_segment in reversed(list(zip(qkv, out_ws, log_parts, key_parts))):
         d_mixed = dot(d_branch_attn, w).astype(bf16)
-        grad_out_w.append(dot(d_branch_attn, mixed, TN).astype(bf16))
         d_rows = []
         first = 1 if pair else 0
         for i, (g, _) in enumerate(segments):
@@ -447,7 +467,9 @@
             )
             d_rows.insert(0, whole)
         d_qkv.append(jnp.concatenate(d_rows, axis=0))
-    grad_qkv = [dot(mixed_attn, d, TN).astype(bf16) for d in d_qkv]
+    d_qkv.reverse()
+    total_qkv = both_cores(mixed_attn, d_qkv)
+    d_qkv, total_qkv = lax.optimization_barrier((d_qkv, total_qkv))
     d_mixed_attn = grouped(sum(dot(d, w, NT) for d, w in zip(d_qkv, qkv_ws)))
     d_shift_attn = jnp.sum(d_mixed_attn, axis=1)
     d_scale_attn = jnp.sum(d_mixed_attn * norm_attn, axis=1)
@@ -466,9 +488,7 @@
     out_tokens = give(out_rows)
     grad_tokens = give(grad_rows)
 
-    def scatter_weight(halves, kinds, wide):
-        own, other = halves
-        total = (own.astype(f32) + swap_core(other).astype(f32)).astype(bf16)
+    def scatter_weight(total, kinds, wide):
         part = lax.optimization_barrier(
             lax.psum_scatter(total, "dpo", scatter_dimension=0, tiled=True)
         )
@@ -484,10 +504,10 @@
         met = swap_core(at(part, 1 - c, 0))
         return in_order(c, mine, met, 2).reshape(drows, kinds, 2 * wide)
 
-    grad_w_fc1 = scatter_weight(grad_fc1, 1, fc_w).reshape(drows, 2 * fc_w)
-    grad_w_fc2 = scatter_weight(grad_fc2, 1, fc_w).reshape(drows, 2 * fc_w).T
-    grad_w_out = scatter_weight(grad_out_w, 1, head_w).reshape(drows, slab).T
-    grad_w_qkv = scatter_weight(grad_qkv, 3, head_w)
+    grad_w_fc1 = scatter_weight(total_fc1, 1, fc_w).reshape(drows, 2 * fc_w)
+    grad_w_fc2 = scatter_weight(total_fc2, 1, fc_w).reshape(drows, 2 * fc_w).T
+    grad_w_out = scatter_weight(total_out, 1, head_w).reshape(drows, slab).T
+    grad_w_qkv = scatter_weight(total_qkv, 3, head_w)
 
     d_mod_groups = jnp.stack(
         [d_shift_attn, d_scale_attn, d_gate_attn, d_shift_mlp, d_scale_mlp, d_gate_mlp], axis=1
@@ -537,13 +557,15 @@
     shared = jnp.concatenate([d_ada_bias, bias_sum])
     share = shared.shape[0] // dp_size
     shared_part = lax.dynamic_slice_in_dim(shared, r * share, share, 0)
-    last = lax.all_gather(
-        jnp.concatenate([cond_part, shared_part]), ("dpo", "core", "tensor"), axis=0, tiled=False
-    ).reshape(dp_size, tsize, -1)
+    mine = jnp.concatenate([cond_part, shared_part])
+    mine = jnp.pad(mine, (0, -mine.shape[0] % (8 * LANES))).reshape(1, -1, LANES)
+    last = lax.all_gather(mine, ("dpo", "core", "tensor"), axis=0, tiled=True)
+    last = last.reshape(dp_size, tsize, -1)
     cond_size = latents * drows
     grad_cond = jnp.sum(last[:, :, :cond_size], axis=1).reshape(dp_size, latents, drows)
     grad_cond = jnp.swapaxes(grad_cond, 0, 1).reshape(latents, width)
-    spread = jnp.swapaxes(last[:, :, cond_size:], 0, 1).reshape(tsize, dp_size * share)
+    spread = jnp.swapaxes(last[:, :, cond_size : cond_size + share], 0, 1)
+    spread = spread.reshape(tsize, dp_size * share)
 
     def whole(start, kinds, wide):
         part = spread[:, start : start + kinds * wide].reshape(tsize, kinds, wide)

time: 1270 us -> 1110 us (0.87)
  waiting for transfers between devices: 389 us -> 159 us
  blocking collectives: 21.3 us -> 99.2 us
    reduce_scatter x4, waiting for transfers between devices: 174 us -> 0.01 us  [scatter_weight(): lax.psum_scatter(total, 'dpo', scatter_dimension=0, tiled=True)]
    all_gather x0 -> x1, blocking collectives: none -> 72.1 us  [per_device(): last = lax.all_gather(mine, ('dpo', 'core', 'tensor'), axis=0, tiled=True)]
    unnamed x12 -> x9, waiting for transfers between devices: 69.9 us -> 34.6 us
    ppermute x13, waiting for transfers between devices: 17.5 us -> 4.36 us  [swap_core(): return lax.ppermute(x, 'core', [(0, 1), (1, 0)])]
    ppermute x15 -> x16, waiting for transfers between devices: 68.1 us -> 58.5 us  [swap_tensor(): return lax.ppermute(x, 'tensor', [(0, 1), (1, 0)])]
    unnamed x175 -> x220, local copies, waits for them, and re-layouts: 32.9 us -> 28.9 us
    all_gather x4 -> x3, waiting for transfers between devices: 59.2 us -> 61.7 us  [gather(): own = lax.all_gather(x, 'dpo', axis=0, tiled=True)]
  transfers between devices with their start and end apart: 38 -> 37, of which waited for: 14 -> 14; matrix products, arithmetic and copies ran while one was open for 41% -> 41% of each run, Pallas kernels for 17% -> 20%
where the time goes in v2:
time: 1110 us; the launch traced here: 1100 us
  matrix products  306 us (28%)
  Pallas kernels  216 us (19%)
  local copies, waits for them, and re-layouts  164 us (15%)
  waiting for transfers between devices  159 us (14%)
  other arithmetic  118 us (11%)
  blocking collectives  99.2 us (9%)
  starting transfers between devices  24.6 us (2%)
  between operations  17.6 us (2%)
    dot_general x25, matrix products, dot(): lax.dot_general(left, right, dims, preferred_element_type=jnp.float32)  298 us
    pallas_call x4, Pallas kernels, attend_backward(): pl.pallas_call(partial(backward_kernel, k_at, v_at, dk_at, dv_at, min(256...  128 us
    pallas_call x4, Pallas kernels, attend_forward(): pl.pallas_call(partial(forward_kernel, k_at, v_at, min(256, rows)), grid=...  88.5 us
    all_gather x1, blocking collectives, per_device(): last = lax.all_gather(mine, ('dpo', 'core', 'tensor'), axis=0, tiled=True)  72.1 us
    all_gather x3, waiting for transfers between devices, gather(): own = lax.all_gather(x, 'dpo', axis=0, tiled=True)  61.7 us
    ppermute x16, waiting for transfers between devices, swap_tensor(): return lax.ppermute(x, 'tensor', [(0, 1), (1, 0)])  58.5 us
    unnamed x9, waiting for transfers between devices  34.6 us
    unnamed x220, local copies, waits for them, and re-layouts  28.9 us
  transfers between devices with their start and end apart: 37, of which 14 were waited for; matrix products, arithmetic and copies ran while one was open for 41% of the time, Pallas kernels for 20%

profile of v2, /device:TPU:0, one launch (start us, length us, event | category | flops | bytes accessed | tf_op | source)
XLA Modules:
  0.0 1105.0 jit_solution(7961116616487963621)
XLA Ops:
  21.3 6.9 collective-permute-done.3
  38.6 17.6 %collective-permute-done.5 = bf16[144,2592]{1,0:T(8,128)(2,1)S(1)} collective-permute-done((bf16[144,2592]{1,0:T(8,128)(2,1)S(1)}, bf16[144,2592]{1,0:T(8,128)(2,1)S(1)}, u32[]{:S(2)}, u32[]{:S(2)}) %collective-permute-start.5) | collective-permute-done | bytes 746528 | tf_op jit(solution)/shard_map/ppermute | solution.py:246
  80.1 33.7 %reduce-scatter.16.cloned.1.call-done = f32[1,18,576]{2,1,0:T(8,128)} async-done(((f32[16,18,576]{2,1,0:T(8,128)}), f32[1,18,576]{2,1,0:T(8,128)}) %reduce-scatter.16.cloned.1.call-update) | async-done | bytes 41488
  119.7 2.7 collective-permute-done.1
  127.1 3.2 multiply_reduce_fusion.7
  131.1 3.7 fusion.18
  134.8 10.9 add_convert_fusion.1.q_ref.kv_ref
  167.4 5.8 convert_reduce_fusion.2
  173.2 25.5 %attend_forward.4 = (bf16[1024,640]{1,0:T(8,128)(2,1)}, f32[8,1024]{1,0:T(8,128)}) custom-call(bf16[1536,1792]{1,0:T(8,128)(2,1)} %copy-done.47, bf16[1536,1792]{1,0:T(8,128)(2,1)} %copy-done.47), custom_call_target="tpu_custom_call" | custom-call | flops 8589934592 | bytes 7340032 | tf_op jit(solution)/shard_map/attend_forward/pallas_call | solution.py:151
  201.2 3.2 pad_maximum_fusion.5.kv_ref
  204.4 10.7 all-gather.8.cloned.1.call-done
  215.1 10.4 add_convert_fusion.q_ref.kv_ref
  231.3 18.5 %attend_forward.5 = (bf16[512,640]{1,0:T(8,128)(2,1)}, f32[8,512]{1,0:T(8,128)}) custom-call(bf16[1536,1792]{1,0:T(8,128)(2,1)} %copy-done.47, bf16[1024,1152]{1,0:T(8,128)(2,1)} %pad_maximum_fusion.5.kv_ref), custom_call_target="tpu_custom_call" | custom-call | flops 4294967296 | bytes 5505024 | tf_op jit(solution)/shard_map/attend_forward/pallas_call | solution.py:151
  251.8 51.1 %all-gather.10.cloned.1.call-done = bf16[1152,2304]{1,0:T(8,128)(2,1)} async-done(((bf16[144,2304]{1,0:T(8,128)(2,1)}), bf16[1152,2304]{1,0:T(8,128)(2,1)}) %all-gather.10.cloned.1.call-update) | async-done | bytes 5308432 | tf_op jit(solution)/shard_map/all_gather | solution.py:340
  302.9 25.6 %attend_forward.6 = (bf16[1024,640]{1,0:T(8,128)(2,1)}, f32[8,1024]{1,0:T(8,128)}) custom-call(bf16[1536,1792]{1,0:T(8,128)(2,1)} %copy-done.48, bf16[1536,1792]{1,0:T(8,128)(2,1)} %copy-done.48), custom_call_target="tpu_custom_call" | custom-call | flops 8589934592 | bytes 7340032 | tf_op jit(solution)/shard_map/attend_forward/pallas_call | solution.py:151
  329.9 3.2 pad_maximum_fusion.6.kv_ref
  333.1 18.9 %attend_forward.7 = (bf16[512,640]{1,0:T(8,128)(2,1)}, f32[8,512]{1,0:T(8,128)}) custom-call(bf16[1536,1792]{1,0:T(8,128)(2,1)} %copy-done.48, bf16[1024,1152]{1,0:T(8,128)(2,1)} %pad_maximum_fusion.6.kv_ref), custom_call_target="tpu_custom_call" | custom-call | flops 4294967296 | bytes 5505024 | tf_op jit(solution)/shard_map/attend_forward/pallas_call | solution.py:151
  353.4 6.0 fusion.42
  359.5 12.0 %fusion.87 = f32[1536,2304]{1,0:T(8,128)} fusion(bf16[1536,1152]{1,0:T(8,128)(2,1)S(1)} %copy-done.32, bf16[1152,2304]{1,0:T(8,128)(2,1)S(1)} %bitcast.370), kind=kOutput, calls=%fused_computation.306 | convolution fusion | flops 8153726976 | bytes 23003136 | tf_op jit(solution)/shard_map/dot_general | solution.py:26
  371.5 9.1 fusion.82
  385.1 14.5 %fusion.88 = f32[1536,2304]{1,0:T(8,128)} fusion(bf16[1536,1152]{1,0:T(8,128)(2,1)S(1)} %copy-done.33, bf16[1152,2304]{1,0:T(8,128)(2,1)} %collective-permute-done.11), kind=kOutput, calls=%fused_computation.307 | convolution fusion | flops 8153726976 | bytes 23003136 | tf_op jit(solution)/shard_map/dot_general | solution.py:26
  399.6 24.0 %convert_reduce_fusion = (f32[2304]{0:T(1024)}, bf16[1536,2304]{1,0:T(8,128)(2,1)}, bf16[1536,2304]{1,0:T(8,128)(2,1)S(1)}) fusion(f32[1536,2304]{1,0:T(8,128)} %fusion.88, f32[2304]{0:T(1024)S(1)} %copy-done.70, bf16[1536,1152]{1,0:T(8,128)(2,1)S(1)} %fusion.22, bf16[1152,2944]{1,0:T(8,128)(2,1)} %collective-permute-done.9), kind=kOutput, calls=%fused_computation.21 | convolution fusion | flops 8242198528 | bytes 37177344 | tf_op jit(solution)/shard_map/dot_general | solution.py:26
  423.6 15.8 %convolution_convert_fusion.2 = bf16[1152,2304]{1,0:T(8,128)(2,1)} fusion(bf16[1536,1152]{1,0:T(8,128)(2,1)S(1)} %fusion.22, bf16[1536,2304]{1,0:T(8,128)(2,1)} %get-tuple-element.46), kind=kOutput, calls=%fused_computation.30 | convolution fusion | flops 8156381184 | bytes 15925248 | tf_op jit(solution)/shard_map/dot_general | solution.py:26
  439.9 10.5 convolution_convert_fusion
  450.4 26.3 %convert_reduce_fusion.1 = (f32[2304]{0:T(1024)}, bf16[1536,2304]{1,0:T(8,128)(2,1)S(1)}, bf16[1536,2304]{1,0:T(8,128)(2,1)}) fusion(f32[1536,2304]{1,0:T(8,128)} %fusion.87, f32[2304]{0:T(1024)S(1)} %copy-done.68, bf16[1536,1152]{1,0:T(8,128)(2,1)S(1)} %fusion.22, bf16[1152,2944]{1,0:T(8,128)(2,1)S(1)} %bitcast.315), kind=kOutput, calls=%fused_computation.22 | convolution fusion | flops 8242198528 | bytes 37180416 | tf_op jit(solution)/shard_map/dot_general | solution.py:26
  476.7 2.8 copy-done.21
  479.5 11.8 %add_convert_fusion.3 = bf16[1152,2304]{1,0:T(8,128)(2,1)} fusion(bf16[1152,2304]{1,0:T(8,128)(2,1)} %collective-permute-done.12, bf16[1536,1152]{1,0:T(8,128)(2,1)S(1)} %fusion.22, bf16[1536,2304]{1,0:T(8,128)(2,1)S(1)} %get-tuple-element.45), kind=kOutput, calls=%fused_computation.42 | convolution fusion | flops 8166998016 | bytes 21233664 | tf_op jit(solution)/shard_map/dot_general | solution.py:26
  491.3 15.6 %add_convert_fusion.2 = bf16[1152,2304]{1,0:T(8,128)(2,1)} fusion(bf16[1152,2304]{1,0:T(8,128)(2,1)} %collective-permute-done.13, bf16[1536,1152]{1,0:T(8,128)(2,1)} %get-tuple-element.87, bf16[1536,2304]{1,0:T(8,128)(2,1)} %get-tuple-element.43), kind=kOutput, calls=%fused_computation.41 | convolution fusion | flops 8166998016 | bytes 21233664 | tf_op jit(solution)/shard_map/dot_general | solution.py:26
  506.9 15.1 %fusion.26 = f32[1536,1152]{1,0:T(8,128)} fusion(bf16[1536,2304]{1,0:T(8,128)(2,1)} %get-tuple-element.46, bf16[1152,2944]{1,0:T(8,128)(2,1)} %collective-permute-done.9), kind=kOutput, calls=%fused_computation.80 | convolution fusion | flops 8153726976 | bytes 19464192 | tf_op jit(solution)/shard_map/dot_general | solution.py:26
  522.1 14.9 %fusion.25 = (f32[1536]{0:T(1024)S(1)}, f32[1536]{0:T(1024)S(1)}, f32[1536,1152]{1,0:T(8,128)S(1)}) fusion(f32[3,1152]{1,0:T(4,128)S(1)} %bitcast.347, f32[1536]{0:T(1024)S(1)} %add_rsqrt_fusion, f32[1536,1152]{1,0:T(8,128)S(1)} %bitcast.301, f32[1536]{0:T(1024)S(1)} %broadcast_multiply_fusion.4, f32[1536,1152]{1,0:T(8,128)} %fusion.26, ...), kind=kOutput, calls=%fused_computation.76 | convolution fusion | flops 8166110208 | bytes 33658368 | tf_op jit(solution)/shard_map/dot_general | solution.py:26
  537.1 6.9 fusion.20
  544.0 3.0 convolution_convert_fusion.8
  547.6 2.9 collective-permute-done.15
  550.5 5.7 fusion.37
  561.2 3.4 fusion.78
  564.6 4.7 maximum_convert_fusion
  572.4 13.6 %fusion.89 = f32[1536,1152]{1,0:T(8,128)S(1)} fusion(bf16[1536,2304]{1,0:T(8,128)(2,1)} %copy-done.84, bf16[1152,2304]{1,0:T(8,128)(2,1)} %collective-permute-done.11), kind=kOutput, calls=%fused_computation.308 | convolution fusion | flops 8153726976 | bytes 19464192 | tf_op jit(solution)/shard_map/dot_general | solution.py:26
  586.1 13.4 %add_add_fusion = f32[1536,1152]{1,0:T(8,128)} fusion(f32[1536,1152]{1,0:T(8,128)S(1)} %fusion.89, f32[1152]{0:T(1024)S(1)} %copy-done.72, bf16[1536,2304]{1,0:T(8,128)(2,1)} %get-tuple-element.43, bf16[1152,2304]{1,0:T(8,128)(2,1)S(1)} %bitcast.372), kind=kOutput, calls=%fused_computation.70 | convolution fusion | flops 8157265920 | bytes 26546688 | tf_op jit(solution)/shard_map/dot_general | solution.py:26
  599.5 8.7 multiply_convert_fusion.2
  611.5 6.9 convolution_convert_fusion.7.do_ref
  618.3 24.7 %attend_backward.5 = (bf16[512,640]{1,0:T(8,128)(2,1)}, bf16[1024,1152]{1,0:T(8,128)(2,1)}) custom-call(bf16[1536,1792]{1,0:T(8,128)(2,1)} %copy-done.47, bf16[1024,1152]{1,0:T(8,128)(2,1)} %pad_maximum_fusion.5.kv_ref, bf16[1536,640]{1,0:T(8,128)(2,1)} %convolution_convert_fusion.7.do_ref, f32[8,512]{1,0:T(8,128)} %get-tuple-element.49.log_ref), custom_call_target="tpu_custom_call" | custom-call | flops 10737418240 | bytes 11010048 | tf_op jit(solution)/shard_map/attend_backward/pallas_call | solution.py:187
  646.0 5.7 convolution_convert_fusion.6.do_ref
  651.7 24.1 %attend_backward.7 = (bf16[512,640]{1,0:T(8,128)(2,1)}, bf16[1024,1152]{1,0:T(8,128)(2,1)}) custom-call(bf16[1536,1792]{1,0:T(8,128)(2,1)} %copy-done.48, bf16[1024,1152]{1,0:T(8,128)(2,1)} %pad_maximum_fusion.6.kv_ref, bf16[1536,640]{1,0:T(8,128)(2,1)} %convolution_convert_fusion.6.do_ref, f32[8,512]{1,0:T(8,128)} %get-tuple-element.53.log_ref), custom_call_target="tpu_custom_call" | custom-call | flops 10737418240 | bytes 11010048 | tf_op jit(solution)/shard_map/attend_backward/pallas_call | solution.py:187
  678.7 39.7 %attend_backward.6 = bf16[1024,1792]{1,0:T(8,128)(2,1)} custom-call(bf16[1536,1792]{1,0:T(8,128)(2,1)} %copy-done.48, bf16[1536,1792]{1,0:T(8,128)(2,1)} %copy-done.48, bf16[1536,640]{1,0:T(8,128)(2,1)} %convolution_convert_fusion.6.do_ref, f32[8,1024]{1,0:T(8,128)} %get-tuple-element.52.log_ref), custom_call_target="tpu_custom_call" | custom-call | flops 21474836480 | bytes 14680064 | tf_op jit(solution)/shard_map/attend_backward/pallas_call | solution.py:187
  720.5 4.2 concatenate.150
  724.6 12.1 %convolution_convert_fusion.4 = bf16[1152,1792]{1,0:T(8,128)(2,1)} fusion(bf16[1536,1152]{1,0:T(8,128)(2,1)} %copy-done.29, bf16[512,1792]{1,0:T(8,128)(2,1)} %concatenate.150, bf16[1024,1792]{1,0:T(8,128)(2,1)} %attend_backward.6), kind=kOutput, calls=%fused_computation.47 | convolution fusion | flops 6354862080 | bytes 13172736 | tf_op jit(solution)/shard_map/dot_general | solution.py:26
  736.8 39.4 %attend_backward.4 = bf16[1024,1792]{1,0:T(8,128)(2,1)} custom-call(bf16[1536,1792]{1,0:T(8,128)(2,1)} %copy-done.47, bf16[1536,1792]{1,0:T(8,128)(2,1)} %copy-done.47, bf16[1536,640]{1,0:T(8,128)(2,1)} %convolution_convert_fusion.7.do_ref, f32[8,1024]{1,0:T(8,128)} %get-tuple-element.48.log_ref), custom_call_target="tpu_custom_call" | custom-call | flops 21474836480 | bytes 14680064 | tf_op jit(solution)/shard_map/attend_backward/pallas_call | solution.py:187
  778.2 5.7 pad_maximum_fusion.1
  788.2 2.8 concatenate.148
  791.0 3.1 collective-permute-done.23
  795.7 4.8 pad_maximum_fusion
  801.8 12.9 %add_convert_fusion.4 = bf16[1152,1792]{1,0:T(8,128)(2,1)} fusion(bf16[1152,1792]{1,0:T(8,128)(2,1)} %collective-permute-done.18, bf16[1536,1152]{1,0:T(8,128)(2,1)} %copy-done.29, bf16[512,1792]{1,0:T(8,128)(2,1)S(1)} %concatenate.148, bf16[1024,1792]{1,0:T(8,128)(2,1)} %attend_backward.4), kind=kOutput, calls=%fused_computation.46 | convolution fusion | flops 6363119616 | bytes 17301504 | tf_op jit(solution)/shard_map/dot_general | solution.py:26
  814.7 12.5 %fusion.90 = f32[1536,1152]{1,0:T(8,128)} fusion(bf16[1536,1792]{1,0:T(8,128)(2,1)} %pad_maximum_fusion, bf16[1152,1792]{1,0:T(8,128)(2,1)} %all-gather.6.cloned.1.call-done), kind=kOutput, calls=%fused_computation.309 | convolution fusion | flops 6341787648 | bytes 16711680 | tf_op jit(solution)/shard_map/dot_general | solution.py:26
  827.2 15.5 %fusion.24 = (f32[1536]{0:T(1024)S(1)}, f32[1536]{0:T(1024)S(1)}, f32[1536,1152]{1,0:T(8,128)}) fusion(f32[3,1152]{1,0:T(4,128)S(1)} %bitcast.354, f32[1536]{0:T(1024)S(1)} %copy-done.55, f32[1536]{0:T(1024)S(1)} %copy-done.50, bf16[512,1152]{1,0:T(8,128)(2,1)S(1)} %copy-done.10, bf16[512,1152]{1,0:T(8,128)(2,1)S(1)} %copy-done.13, ...), kind=kOutput, calls=%fused_computation.74 | convolution fusion | flops 6364787712 | bytes 27366912 | tf_op jit(solution)/shard_map/dot_general | solution.py:26
  844.0 16.0 %multiply_reduce_fusion.1 = (f32[3,1152]{1,0:T(4,128)S(1)}, f32[3,1152]{1,0:T(4,128)S(1)}, f32[3,1152]{1,0:T(4,128)S(1)}, f32[3,1152]{1,0:T(4,128)S(1)}, f32[3,1...) fusion(f32[3,512,1152]{2,1,0:T(8,128)} %bitcast.306, f32[3,512]{1,0:T(4,128)} %rsqrt.26, ...), kind=kLoop, calls=%fused_computation.60 | loop fusion | flops 53063424 | bytes 46179852 | tf_op jit(solution)/shard_map/reduce_sum | solution.py:443
  871.8 4.0 convert_reduce_fusion.5
  889.6 27.0 %all-gather.1 = f32[16,1,14976]{2,1,0:T(1,128)S(1)} all-gather(f32[1,1,14976]{2,1,0:T(1,128)S(1)} %reshape.904), channel_id=2, replica_groups=mesh['dpo'=8,'core'=2,'tensor'=2] {'dpo','core'}, dimensions={0}, use_global_device_ids=true | all-gather | bytes 1018368 | tf_op jit(solution)/shard_map/all_gather | solution.py:543
  929.8 72.1 %all_gather.23 = f32[32,24,128]{2,1,0:T(8,128)} all-gather(f32[1,24,128]{2,1,0:T(8,128)S(1)} %fusion.57), channel_id=1, replica_groups=mesh['dpo'=8,'core'=2,'tensor'=2] {'dpo','core','tensor'}, dimensions={0}, use_global_device_ids=true | all-gather | bytes 405504 | tf_op jit(solution)/shard_map/all_gather | solution.py:562
  1034.6 2.9 fusion.45
  1037.6 3.9 select_bitcast_fusion.1
  1049.1 3.1 pad_maximum_fusion.4
  1054.9 10.3 collective-permute-done.25
  1067.4 8.2 collective-permute-done.27
  1084.0 8.8 collective-permute-done.21
  (498 shorter events, 224.9 us)
Async XLA Ops:
  8.0 105.8 %reduce-scatter.16.cloned.1.call-start = ((), (), s32[]{:S(2)}) async-start(), calls=%async_computation.12 | async-start | bytes 1044480
  10.4 8.3 collective-permute-start.2
  14.9 15.7 %copy-start.27 = (bf16[72,3456]{1,0:T(8,128)(2,1)}, bf16[72,3456]{1,0:T(8,128)(2,1)S(1)}, u32[]{:S(2)}) copy-start(bf16[72,3456]{1,0:T(8,128)(2,1)S(1)} %reshape.805) | copy-start | bytes 1492996
  18.3 101.2 %all-gather.6.cloned.1.call-start = ((), (), s32[]{:S(2)}) async-start(), calls=%async_computation.5 | async-start | bytes 4644864 | tf_op jit(solution)/shard_map/all_gather | solution.py:340
  18.7 9.5 collective-permute-start.3
  31.9 183.1 %all-gather.8.cloned.1.call-start = ((), (), s32[]{:S(2)}) async-start(), calls=%async_computation.6 | async-start | bytes 7630848 | tf_op jit(solution)/shard_map/all_gather | solution.py:340
  34.9 1.8 collective-permute-start.4
  36.8 19.4 %collective-permute-start.5 = (bf16[144,2592]{1,0:T(8,128)(2,1)S(1)}, bf16[144,2592]{1,0:T(8,128)(2,1)S(1)}, u32[]{:S(2)}, u32[]{:S(2)}) collective-permute-start(bf16[144,2592]{1,0:T(8,128)(2,1)S(1)} %pad_maximum_fusion.8), channel_id=1, source_target_pairs={{0,1},{1,0},{2,3},{3,2},{4,5},{5,4},{6,7},{7,6},{8,9},{9,8},{10,11... | collective-permute-start | bytes 2239496 | tf_op jit(solution)/shard_map/ppermute | solution.py:246
  66.2 236.7 %all-gather.10.cloned.1.call-start = ((), (), s32[]{:S(2)}) async-start(), calls=%async_computation.7 | async-start | bytes 5971968 | tf_op jit(solution)/shard_map/all_gather | solution.py:340
  68.2 99.1 %collective-permute-start.10 = (bf16[512,1152]{1,0:T(8,128)(2,1)}, bf16[512,1152]{1,0:T(8,128)(2,1)}, u32[]{:S(2)}, u32[]{:S(2)}) collective-permute-start(bf16[512,1152]{1,0:T(8,128)(2,1)} %get-tuple-element.107), channel_id=1, source_target_pairs={{0,1},{1,0},{2,3},{3,2},{4,5},{5,4},{6,7},{7,6},{8,9},{9,8},{10,11... | collective-permute-start | bytes 3538952 | tf_op jit(solution)/shard_map/ppermute | solution.py:246
  71.3 300.2 %copy-start.5 = (bf16[512,1152]{1,0:T(8,128)(2,1)}, bf16[512,1152]{1,0:T(8,128)(2,1)S(1)}, u32[]{:S(2)}) copy-start(bf16[512,1152]{1,0:T(8,128)(2,1)S(1)} %get-tuple-element.108) | copy-start | bytes 3538948
  71.3 300.2 %copy-start.8 = (bf16[512,1152]{1,0:T(8,128)(2,1)}, bf16[512,1152]{1,0:T(8,128)(2,1)S(1)}, u32[]{:S(2)}) copy-start(bf16[512,1152]{1,0:T(8,128)(2,1)S(1)} %get-tuple-element.109) | copy-start | bytes 3538948
  71.3 53.7 %collective-permute-start = (bf16[512,1152]{1,0:T(8,128)(2,1)}, bf16[512,1152]{1,0:T(8,128)(2,1)S(1)}, u32[]{:S(2)}, u32[]{:S(2)}) collective-permute-start(bf16[512,1152]{1,0:T(8,128)(2,1)} %get-tuple-element.110), channel_id=1, source_target_pairs={{0,1},{1,0},{2,3},{3,2},{4,5},{5,4},{6,7},{7,6},{8,9},{9,8},{10,11... | collective-permute-start | bytes 3538952 | tf_op jit(solution)/shard_map/ppermute | solution.py:246
  79.3 51.1 %copy-start.79 = (f32[64]{0:T(128)}, f32[64]{0:T(128)S(1)}, u32[]{:S(2)}) copy-start(f32[64]{0:T(128)S(1)} %broadcast.361) | copy-start | bytes 772
  80.1 50.3 %copy-start.77 = (pred[3,3]{1,0:T(4,128)(4,1)}, pred[3,3]{1,0:T(4,128)(4,1)S(1)}, u32[]{:S(2)}) copy-start(pred[3,3]{1,0:T(4,128)(4,1)S(1)} %iota_compare_fusion.5) | copy-start | bytes 31
  115.3 7.1 collective-permute-start.1
  119.5 664.4 %reduce-scatter.10.cloned.1.call-start = ((), (), s32[]{:S(2)}) async-start(), calls=%async_computation.9 | async-start | bytes 1658880 | tf_op jit(solution)/shard_map/reduce_scatter | solution.py:493
  125.0 246.5 %copy-start.11 = (bf16[512,1152]{1,0:T(8,128)(2,1)}, bf16[512,1152]{1,0:T(8,128)(2,1)S(1)}, u32[]{:S(2)}) copy-start(bf16[512,1152]{1,0:T(8,128)(2,1)S(1)} %collective-permute-done) | copy-start | bytes 3538948
  130.4 84.7 %collective-permute-start.7 = (bf16[1152,1792]{1,0:T(8,128)(2,1)}, bf16[1152,1792]{1,0:T(8,128)(2,1)}, u32[]{:S(2)}, u32[]{:S(2)}) collective-permute-start(bf16[1152,1792]{1,0:T(8,128)(2,1)} %all-gather.6.cloned.1.call-done), channel_id=1, source_target_pairs={{0,2},{2,0},{1,3},{3,1},{4,6},{6,4},{5,7},{7,5},{8,10},{10,8},{9,1... | collective-permute-start | bytes 12386312 | tf_op jit(solution)/shard_map/ppermute | solution.py:243
  134.8 15.5 %copy-start.83 = (f32[3]{0:T(128)S(1)}, f32[3]{0:T(128)}, u32[]{:S(2)}) copy-start(f32[3]{0:T(128)} %dynamic_slice.141) | copy-start | bytes 40
  148.5 52.7 %collective-permute-start.6 = (bf16[512,1152]{1,0:T(8,128)(2,1)}, bf16[512,1152]{1,0:T(8,128)(2,1)}, u32[]{:S(2)}, u32[]{:S(2)}) collective-permute-start(bf16[512,1152]{1,0:T(8,128)(2,1)} %slice.241), channel_id=1, source_target_pairs={{0,1},{1,0},{2,3},{3,2},{4,5},{5,4},{6,7},{7,6},{8,9},{9,8},{10,11... | collective-permute-start | bytes 3538952 | tf_op jit(solution)/shard_map/ppermute | solution.py:246
  152.4 46.3 %copy-start.62 = (f32[1536]{0:T(1024)}, f32[1536]{0:T(1024)S(1)}, u32[]{:S(2)}) copy-start(f32[1536]{0:T(1024)S(1)} %mul.377) | copy-start | bytes 18436
  198.7 16.4 %copy-start.74 = (f32[1792]{0:T(1024)S(1)}, f32[1792]{0:T(1024)}, u32[]{:S(2)}) copy-start(f32[1792]{0:T(1024)} %concatenate.144) | copy-start | bytes 21508
  215.0 156.4 %collective-permute-start.9 = (bf16[1152,2944]{1,0:T(8,128)(2,1)}, bf16[1152,2944]{1,0:T(8,128)(2,1)}, u32[]{:S(2)}, u32[]{:S(2)}) collective-permute-start(bf16[1152,2944]{1,0:T(8,128)(2,1)} %all-gather.8.cloned.1.call-done), channel_id=1, source_target_pairs={{0,2},{2,0},{1,3},{3,1},{4,6},{6,4},{5,7},{7,5},{8,10},{10,8},{9,1... | collective-permute-start | bytes 20348936 | tf_op jit(solution)/shard_map/ppermute | solution.py:243
  229.8 100.1 %collective-permute-start.8 = (bf16[512,1152]{1,0:T(8,128)(2,1)}, bf16[512,1152]{1,0:T(8,128)(2,1)}, u32[]{:S(2)}, u32[]{:S(2)}) collective-permute-start(bf16[512,1152]{1,0:T(8,128)(2,1)} %slice.247), channel_id=1, source_target_pairs={{0,1},{1,0},{2,3},{3,2},{4,5},{5,4},{6,7},{7,6},{8,9},{9,8},{10,11... | collective-permute-start | bytes 3538952 | tf_op jit(solution)/shard_map/ppermute | solution.py:246
  302.9 81.0 %collective-permute-start.11 = (bf16[1152,2304]{1,0:T(8,128)(2,1)}, bf16[1152,2304]{1,0:T(8,128)(2,1)}, u32[]{:S(2)}, u32[]{:S(2)}) collective-permute-start(bf16[1152,2304]{1,0:T(8,128)(2,1)} %all-gather.10.cloned.1.call-done), channel_id=1, source_target_pairs={{0,2},{2,0},{1,3},{3,1},{4,6},{6,4},{5,7},{7,5},{8,10},{10,8},{9,1... | collective-permute-start | bytes 15925256 | tf_op jit(solution)/shard_map/ppermute | solution.py:243
  353.4 18.1 %copy-start.22 = (bf16[1536,640]{1,0:T(8,128)(2,1)}, bf16[1536,640]{1,0:T(8,128)(2,1)S(1)}, u32[]{:S(2)}) copy-start(bf16[1536,640]{1,0:T(8,128)(2,1)S(1)} %constant_dynamic-update-slice_fusion.2) | copy-start | bytes 5898244
  381.5 155.5 %copy-start.51 = (f32[1536]{0:T(1024)}, f32[1536]{0:T(1024)S(1)}, u32[]{:S(2)}) copy-start(f32[1536]{0:T(1024)S(1)} %add_rsqrt_fusion) | copy-start | bytes 18436
  383.9 15.7 %copy-start.70 = (f32[2304]{0:T(1024)S(1)}, f32[2304]{0:T(1024)}, u32[]{:S(2)}) copy-start(f32[2304]{0:T(1024)} %add.413) | copy-start | bytes 27652
  423.6 16.3 %copy-start.84 = (bf16[1536,2304]{1,0:T(8,128)(2,1)}, bf16[1536,2304]{1,0:T(8,128)(2,1)S(1)}, u32[]{:S(2)}) copy-start(bf16[1536,2304]{1,0:T(8,128)(2,1)S(1)} %get-tuple-element.44) | copy-start | bytes 21233668
  423.6 26.8 %slice-start.4 = ((s8[6782976]{0:T(1024)(128)(4,1)}), s8[4194304]{0:T(1024)(128)(4,1)S(1)}, s32[]{:S(2)}) async-start(s8[6782976]{0:T(1024)(128)(4,1)} %bitcast.314), calls=%async_computation.17 | async-start | bytes 8388608
  439.4 37.3 %collective-permute-start.12 = (bf16[1152,2304]{1,0:T(8,128)(2,1)}, bf16[1152,2304]{1,0:T(8,128)(2,1)}, u32[]{:S(2)}, u32[]{:S(2)}) collective-permute-start(bf16[1152,2304]{1,0:T(8,128)(2,1)} %convolution_convert_fusion.2), channel_id=1, source_target_pairs={{0,2},{2,0},{1,3},{3,1},{4,6},{6,4},{5,7},{7,5},{8,10},{10,8},{9,1... | collective-permute-start | bytes 15925256 | tf_op jit(solution)/shard_map/ppermute | solution.py:243
  450.4 40.9 %collective-permute-start.13 = (bf16[1152,2304]{1,0:T(8,128)(2,1)}, bf16[1152,2304]{1,0:T(8,128)(2,1)}, u32[]{:S(2)}, u32[]{:S(2)}) collective-permute-start(bf16[1152,2304]{1,0:T(8,128)(2,1)} %convolution_convert_fusion), channel_id=1, source_target_pairs={{0,2},{2,0},{1,3},{3,1},{4,6},{6,4},{5,7},{7,5},{8,10},{10,8},{9,1... | collective-permute-start | bytes 15925256 | tf_op jit(solution)/shard_map/ppermute | solution.py:243
  491.3 30.7 %slice-start = ((s8[7077888]{0:T(1024)(128)(4,1)}), s8[2883584]{0:T(1024)(128)(4,1)S(1)}, s32[]{:S(2)}) async-start(s8[7077888]{0:T(1024)(128)(4,1)} %bitcast.300), calls=%async_computation.13 | async-start | bytes 5767168
  506.9 15.1 %slice-start.1 = ((s8[7077888]{0:T(1024)(128)(4,1)}), s8[4194304]{0:T(1024)(128)(4,1)S(1)}, s32[]{:S(2)}) async-start(s8[7077888]{0:T(1024)(128)(4,1)} %bitcast.300), calls=%async_computation.14 | async-start | bytes 8388608
  522.0 15.0 %copy-start.14 = (bf16[512,1152]{1,0:T(8,128)(2,1)S(1)}, bf16[512,1152]{1,0:T(8,128)(2,1)}, u32[]{:S(2)}) copy-start(bf16[512,1152]{1,0:T(8,128)(2,1)} %get-tuple-element.105) | copy-start | bytes 3538948
  522.0 15.0 %copy-start.16 = (bf16[512,1152]{1,0:T(8,128)(2,1)S(1)}, bf16[512,1152]{1,0:T(8,128)(2,1)}, u32[]{:S(2)}) copy-start(bf16[512,1152]{1,0:T(8,128)(2,1)} %get-tuple-element.106) | copy-start | bytes 3538948
  522.0 15.0 %copy-start.41 = (f32[3,1,1152]{2,0,1:T(4,128)S(1)}, f32[3,1,1152]{2,0,1:T(4,128)}, u32[]{:S(2)}) copy-start(f32[3,1,1152]{2,0,1:T(4,128)} %copy.145) | copy-start | bytes 41476
  547.0 3.4 collective-permute-start.15
  556.2 487.3 %reduce-scatter.12.cloned.1.call-start = ((), (), s32[]{:S(2)}) async-start(), calls=%async_computation.10 | async-start | bytes 5971968 | tf_op jit(solution)/shard_map/reduce_scatter | solution.py:493
  556.9 495.2 %reduce-scatter.14.cloned.1.call-start = ((), (), s32[]{:S(2)}) async-start(), calls=%async_computation.11 | async-start | bytes 5971968 | tf_op jit(solution)/shard_map/reduce_scatter | solution.py:493
  564.6 21.4 %slice-start.8 = ((s8[5308416]{0:T(1024)(128)(4,1)}), s8[1114112]{0:T(1024)(128)(4,1)S(1)}, s32[]{:S(2)}) async-start(s8[5308416]{0:T(1024)(128)(4,1)} %bitcast.371), calls=%async_computation.21 | async-start | bytes 2228224
  609.9 427.6 %collective-permute-start.14 = (bf16[512,1152]{1,0:T(8,128)(2,1)}, bf16[512,1152]{1,0:T(8,128)(2,1)}, u32[]{:S(2)}, u32[]{:S(2)}) collective-permute-start(bf16[512,1152]{1,0:T(8,128)(2,1)} %get-tuple-element.103), channel_id=1, source_target_pairs={{0,1},{1,0},{2,3},{3,2},{4,5},{5,4},{6,7},{7,6},{8,9},{9,8},{10,11... | collective-permute-start | bytes 3538952 | tf_op jit(solution)/shard_map/ppermute | solution.py:246
  611.4 467.3 %reduce-scatter.8.cloned.1.call-start = ((), (), s32[]{:S(2)}) async-start(), calls=%async_computation.8 | async-start | bytes 4644864 | tf_op jit(solution)/shard_map/reduce_scatter | solution.py:493
  618.3 27.7 %copy-start.20 = (bf16[1536,1152]{1,0:T(8,128)(2,1)S(1)}, bf16[1536,1152]{1,0:T(8,128)(2,1)}, u32[]{:S(2)}) copy-start(bf16[1536,1152]{1,0:T(8,128)(2,1)} %copy-done.19) | copy-start | bytes 10616836
  645.4 141.2 %collective-permute-start.16 = (bf16[512,1152]{1,0:T(8,128)(2,1)}, bf16[512,1152]{1,0:T(8,128)(2,1)}, u32[]{:S(2)}, u32[]{:S(2)}) collective-permute-start(bf16[512,1152]{1,0:T(8,128)(2,1)} %slice.207), channel_id=1, source_target_pairs={{0,1},{1,0},{2,3},{3,2},{4,5},{5,4},{6,7},{7,6},{8,9},{9,8},{10,11... | collective-permute-start | bytes 3538952 | tf_op jit(solution)/shard_map/ppermute | solution.py:246
  677.2 41.3 %collective-permute-start.17 = (bf16[512,1152]{1,0:T(8,128)(2,1)S(1)}, bf16[512,1152]{1,0:T(8,128)(2,1)S(1)}, u32[]{:S(2)}, u32[]{:S(2)}) collective-permute-start(bf16[512,1152]{1,0:T(8,128)(2,1)S(1)} %slice.210), channel_id=1, source_target_pairs={{0,1},{1,0},{2,3},{3,2},{4,5},{5,4},{6,7},{7,6},{8,9},{9,8},{10,11... | collective-permute-start | bytes 3538952 | tf_op jit(solution)/shard_map/ppermute | solution.py:246
  678.7 39.7 %copy-start.37 = (bf16[1024,1152]{1,0:T(8,128)(2,1)S(1)}, bf16[1024,1152]{1,0:T(8,128)(2,1)}, u32[]{:S(2)}) copy-start(bf16[1024,1152]{1,0:T(8,128)(2,1)} %get-tuple-element.55) | copy-start | bytes 7077892
  736.8 65.0 %collective-permute-start.18 = (bf16[1152,1792]{1,0:T(8,128)(2,1)}, bf16[1152,1792]{1,0:T(8,128)(2,1)}, u32[]{:S(2)}, u32[]{:S(2)}) collective-permute-start(bf16[1152,1792]{1,0:T(8,128)(2,1)} %convolution_convert_fusion.4), channel_id=1, source_target_pairs={{0,2},{2,0},{1,3},{3,1},{4,6},{6,4},{5,7},{7,5},{8,10},{10,8},{9,1... | collective-permute-start | bytes 12386312 | tf_op jit(solution)/shard_map/ppermute | solution.py:243
  786.0 8.2 collective-permute-start.23
  795.6 4.9 collective-permute-start.24
  801.8 25.4 %slice-start.2 = ((s8[5505024]{0:T(1024)(128)(4,1)}), s8[1310720]{0:T(1024)(128)(4,1)S(1)}, s32[]{:S(2)}) async-start(s8[5505024]{0:T(1024)(128)(4,1)} %bitcast.307), calls=%async_computation.15 | async-start | bytes 2621440
  827.2 16.8 %copy-start.67 = (f32[3,512]{1,0:T(4,128)S(1)}, f32[3,512]{1,0:T(4,128)}, u32[]{:S(2)}) copy-start(f32[3,512]{1,0:T(4,128)} %rsqrt.27) | copy-start | bytes 18436
  844.0 21.3 %copy-start.78 = (pred[3,3]{1,0:T(4,128)(4,1)S(1)}, pred[3,3]{1,0:T(4,128)(4,1)}, u32[]{:S(2)}) copy-start(pred[3,3]{1,0:T(4,128)(4,1)} %copy-done.77) | copy-start | bytes 31
  885.1 4.5 collective-permute-start.20
  885.7 38.6 %copy-start.81 = (s32[48]{0:T(128)S(1)}, s32[48]{0:T(128)}, u32[]{:S(2)}) copy-start(s32[48]{0:T(128)} %copy-done.80) | copy-start | bytes 580
  887.2 150.3 %collective-permute-start.19 = (bf16[512,1152]{1,0:T(8,128)(2,1)}, bf16[512,1152]{1,0:T(8,128)(2,1)}, u32[]{:S(2)}, u32[]{:S(2)}) collective-permute-start(bf16[512,1152]{1,0:T(8,128)(2,1)} %get-tuple-element.101), channel_id=1, source_target_pairs={{0,1},{1,0},{2,3},{3,2},{4,5},{5,4},{6,7},{7,6},{8,9},{9,8},{10,11... | collective-permute-start | bytes 3538952 | tf_op jit(solution)/shard_map/ppermute | solution.py:246
  916.8 117.9 %copy-start.65 = (bf16[48,72]{1,0:T(8,128)(2,1)S(1)}, bf16[48,72]{1,0:T(8,128)(2,1)}, u32[]{:S(2)}) copy-start(bf16[48,72]{1,0:T(8,128)(2,1)} %copy-done.64) | copy-start | bytes 20740
  1047.0 18.2 %collective-permute-start.25 = (bf16[144,1,1152]{2,1,0:T(2,128)(2,1)}, bf16[144,1,1152]{2,1,0:T(2,128)(2,1)}, u32[]{:S(2)}, u32[]{:S(2)}) collective-permute-start(bf16[144,1,1152]{2,1,0:T(2,128)(2,1)} %dynamic-slice_bitcast_fusion.5), channel_id=1, source_target_pairs={{0,1},{1,0},{2,3},{3,2},{4,5},{5,4},{6,7},{7,6},{8,9},{9,8},{10,11... | collective-permute-start | bytes 995336 | tf_op jit(solution)/shard_map/ppermute | solution.py:246
  1054.8 20.8 %collective-permute-start.27 = (bf16[144,1,1152]{2,1,0:T(2,128)(2,1)S(1)}, bf16[144,1,1152]{2,1,0:T(2,128)(2,1)S(1)}, u32[]{:S(2)}, u32[]{:S(2)}) collective-permute-start(bf16[144,1,1152]{2,1,0:T(2,128)(2,1)S(1)} %dynamic-slice_bitcast_fusion.4), channel_id=1, source_target_pairs={{0,1},{1,0},{2,3},{3,2},{4,5},{5,4},{6,7},{7,6},{8,9},{9,8},{10,11... | collective-permute-start | bytes 995336 | tf_op jit(solution)/shard_map/ppermute | solution.py:246
  1067.4 9.3 collective-permute-start.26
  1076.6 7.0 collective-permute-start.28
  1082.6 10.2 collective-permute-start.21
  1093.2 1.7 collective-permute-start.22
  (68 other events, 494.3 us)
Sparse Core Ops, SparseCore 0:
  18.4 95.4 reduce-scatter.15
Sparse Core Ops, SparseCore 1:
  32.0 76.7 all-gather.5
  111.1 103.9 all-gather.7
  217.9 84.9 all-gather.9
  556.3 61.3 reduce-scatter.9
  621.7 102.9 reduce-scatter.11
  728.3 103.6 reduce-scatter.13
  880.6 90.9 reduce-scatter.7

commit v3 on v2

--- a/solution.py
+++ b/solution.py
@@ -15,7 +15,9 @@
 WINDOW = 256
 LANES = 128
 LOG2E = 1.4426950408889634
+SQRT_2_PI = 0.7978845608028654
 VMEM_BYTES = 56 * 2**20
+SMALL_COST = pl.CostEstimate(flops=10**9, bytes_accessed=10**6, transcendentals=0)
 
 NN = (((1,), (0,)), ((), ()))
 NT = (((1,), (1,)), ((), ()))
@@ -196,13 +198,105 @@
         out_specs=out_specs,
         out_shape=out_shape,
         compiler_params=pltpu.CompilerParams(vmem_limit_bytes=VMEM_BYTES),
-        cost_estimate=pl.CostEstimate(
-            flops=10 * heads * rows * keys * WINDOW,
-            bytes_accessed=4 * (rows + keys) * 1792,
-            transcendentals=heads * rows * keys,
-        ),
+        cost_estimate=SMALL_COST,
         name="attend_backward",
     )(q, kv, grad, log_total)
+
+
+def mlp_kernel(x_ref, g_ref, w1_ref, w2_ref, b_ref, hidden_ref, d_ref, bias_ref):
+    value = dot(x_ref[...], w1_ref[...]) + b_ref[...]
+    grad = dot(g_ref[...], w2_ref[...])
+    square = value * value
+    curve = jnp.tanh(SQRT_2_PI * value * (1.0 + 0.044715 * square))
+    left = 0.5 + 0.5 * curve
+    hidden_ref[...] = (value * left).astype(jnp.bfloat16)
+    slope = left + (0.5 * SQRT_2_PI) * value * (1.0 - curve * curve) * (1.0 + 0.134145 * square)
+    d_pre = (grad * slope).astype(jnp.bfloat16)
+    d_ref[...] = d_pre
+    sums = jnp.sum(d_pre.astype(jnp.float32), axis=0, keepdims=True)
+
+    @pl.when(pl.program_id(1) == 0)
+    def _():
+        bias_ref[...] = sums
+
+    @pl.when(pl.program_id(1) != 0)
+    def _():
+        bias_ref[...] = bias_ref[...] + sums
+
+
+def mlp_middle(x, grad, w1, w2, bias):
+    count, width = x.shape
+    wide = bias.shape[0]
+    rows = count // 3 if (count // 3) % 16 == 0 else count
+    cols = wide // 3 if (wide // 3) % LANES == 0 else wide
+    by_row = pl.BlockSpec((rows, width), lambda j, i: (i, 0))
+    by_col = pl.BlockSpec((width, cols), lambda j, i: (0, j))
+    by_both = pl.BlockSpec((rows, cols), lambda j, i: (i, j))
+    one_row = pl.BlockSpec((1, cols), lambda j, i: (0, j))
+    hidden, d_pre, sums = pl.pallas_call(
+        mlp_kernel,
+        grid=(wide // cols, count // rows),
+        in_specs=[by_row, by_row, by_col, by_col, one_row],
+        out_specs=[by_both, by_both, one_row],
+        out_shape=[
+            jax.ShapeDtypeStruct((count, wide), jnp.bfloat16),
+            jax.ShapeDtypeStruct((count, wide), jnp.bfloat16),
+            jax.ShapeDtypeStruct((1, wide), jnp.float32),
+        ],
+        compiler_params=pltpu.CompilerParams(vmem_limit_bytes=VMEM_BYTES),
+        cost_estimate=pl.CostEstimate(
+            flops=4 * count * width * wide,
+            bytes_accessed=4 * (count + wide) * width + 4 * count * wide,
+            transcendentals=count * wide,
+        ),
+        name="mlp_middle",
+    )(x, grad, w1, w2, bias[None])
+    return hidden, d_pre, sums[0]
+
+
+def back_kernel(a0_ref, a1_ref, w0_ref, w1_ref, x_ref, base_ref, scale_ref, out_ref, sum_ref, prod_ref):
+    grad = dot(a0_ref[...], w0_ref[...], NT) + dot(a1_ref[...], w1_ref[...], NT)
+    normed, inverse = norm_parts(x_ref[...].astype(jnp.float32))
+    back = norm_back(normed, inverse, grad * (1.0 + scale_ref[0]))
+    out_ref[...] = (base_ref[...] + back).astype(out_ref.dtype)
+    sums = jnp.sum(grad, axis=0, keepdims=True)
+    prods = jnp.sum(grad * normed, axis=0, keepdims=True)
+
+    @pl.when(pl.program_id(1) == 0)
+    def _():
+        sum_ref[0] = sums
+        prod_ref[0] = prods
+
+    @pl.when(pl.program_id(1) != 0)
+    def _():
+        sum_ref[0] = sum_ref[0] + sums
+        prod_ref[0] = prod_ref[0] + prods
+
+
+def matmul_norm_back(halves, weights, deep, x, base, scale, kind):
+    count, width = x.shape
+    groups = scale.shape[0]
+    rows = count // groups
+    block = 256 if rows % 256 == 0 else rows
+    steps = rows // block
+
+    def by_row(wide):
+        return pl.BlockSpec((block, wide), lambda g, i: (g * steps + i, 0))
+
+    weight = pl.BlockSpec((width, deep), lambda g, i: (0, 0), pipeline_mode=pl.Buffered(1))
+    one_row = pl.BlockSpec((1, 1, width), lambda g, i: (g, 0, 0))
+    one_sum = jax.ShapeDtypeStruct((groups, 1, width), jnp.float32)
+    out, sums, prods = pl.pallas_call(
+        back_kernel,
+        grid=(groups, steps),
+        in_specs=[by_row(deep), by_row(deep), weight, weight, by_row(width), by_row(width), one_row],
+        out_specs=[by_row(width), one_row, one_row],
+        out_shape=[jax.ShapeDtypeStruct((count, width), kind), one_sum, one_sum],
+        compiler_params=pltpu.CompilerParams(vmem_limit_bytes=VMEM_BYTES),
+        cost_estimate=SMALL_COST,
+        name="matmul_norm_back",
+    )(halves[0], halves[1], weights[0], weights[1], x, base, scale)
+    return out, sums[:, 0], prods[:, 0]
 
 
 def per_device(
@@ -253,6 +347,46 @@
     def at(x, index, axis):
         return lax.dynamic_index_in_dim(x, index, axis, keepdims=False)
 
+    bits = [("core", 0)]
+    while 2 ** len(bits) < dp_size:
+        bits.append(("dpo", len(bits) - 1))
+    dpo_size = dp_size // 2
+
+    def hop(x, axis, bit):
+        size = 2 if axis == "core" else dpo_size
+        return lax.ppermute(x, axis, [(i, i ^ (1 << bit)) for i in range(size)])
+
+    def bit_of(axis, bit):
+        return (lax.axis_index(axis) >> bit) & 1
+
+    def sum_scatter_dp(x):
+        for axis, bit in bits:
+            x = x.reshape((x.shape[0] // 2, 2) + x.shape[1:])
+            here = bit_of(axis, bit)
+            x = at(x, here, 1) + hop(at(x, 1 - here, 1), axis, bit)
+        return x[0]
+
+    def gather_dp(x, tie=None):
+        x = x[None]
+        for step, (axis, bit) in enumerate(reversed(bits)):
+            if step == 1 and tie is not None:
+                x, tie = lax.optimization_barrier((x, tie))
+            here = bit_of(axis, bit)
+            other = hop(x, axis, bit)
+            x = jnp.stack([jnp.where(here == 0, x, other), jnp.where(here == 0, other, x)], axis=1)
+            x = x.reshape((-1,) + x.shape[2:])
+        return x if tie is None else (x, tie)
+
+    def sum_tensor(x):
+        if tsize == 2:
+            return at(x, t, 0) + swap_tensor(at(x, 1 - t, 0))
+        return lax.psum_scatter(x, "tensor", scatter_dimension=0, tiled=True)[0]
+
+    def all_tensor(x):
+        if tsize == 2:
+            return in_order(t, x[None], swap_tensor(x)[None], 0)
+        return lax.all_gather(x, "tensor", axis=0, tiled=False)
+
     starts = jnp.cumsum(latent_counts) - latent_counts
     slot_all = jnp.arange(slots * dp_size, dtype=jnp.int32)
     owner, within = slot_all // slots, slot_all % slots
@@ -266,8 +400,7 @@
 
     ada_flat = w_ada.reshape(drows, 6 * slab)
     mod_part = dot(silu_slots, ada_flat).reshape(dp_size, slots * 6, slab)
-    mod_here = lax.psum_scatter(mod_part, ("dpo", "core"), scatter_dimension=0, tiled=True)
-    mod_here = mod_here.reshape(slots, 6, slab)
+    mod_here = sum_scatter_dp(mod_part).reshape(slots, 6, slab)
     if tsize == 2:
         modulation = in_order(t, mod_here, swap_tensor(mod_here), 2)
     else:
@@ -343,16 +476,16 @@
     qkv_ws = gather(columns(quad(shards[:1]), 0, 3, head_w, pads[0]))
     rest = quad(shards[1:])
     out_fc1 = jnp.concatenate(
-        [columns(rest, 0, 1, head_w, pads[1]), columns(rest, head_w, 1, fc_w, 0)], axis=1
+        [columns(rest, head_w, 1, fc_w, 0), columns(rest, 0, 1, head_w, pads[1])], axis=1
     )
     out_fc1_ws = gather(out_fc1)
-    out_ws = [w[:, :out_w] for w in out_fc1_ws]
-    fc1_ws = [w[:, out_w:] for w in out_fc1_ws]
+    fc_all = fc_w * tsize
+    out_ws = [w[:, fc_all:] for w in out_fc1_ws]
     first_w, fc2_cols = lax.optimization_barrier(
         (qkv_ws[0], columns(rest, head_w + fc_w, 1, fc_w, 0))
     )
     qkv_ws = (first_w, qkv_ws[1])
-    fc2_ws = gather(fc2_cols)
+    fc2_own = lax.all_gather(fc2_cols, "dpo", axis=0, tiled=True)
 
     def bias_halves(bias, wide):
         parts = bias.astype(f32).reshape(bias.shape[0], tsize, 2, wide)
@@ -406,6 +539,8 @@
         mixed_parts.append(jnp.concatenate(outs, axis=0))
         log_parts.append(logs)
         key_parts.append(keys_by_segment)
+    fc2_own, mixed_parts = lax.optimization_barrier((fc2_own, mixed_parts))
+    fc2_ws = (fc2_own, swap_core(fc2_own))
     branch_attn = grouped(
         sum(dot(x, w, NT) for x, w in zip(mixed_parts, out_ws)) + bias_attn_out
     )
@@ -416,19 +551,20 @@
     grad_out = grouped(cot_in.astype(f32)) * live[:, None, None]
     d_branch_mlp = flat((grad_out * gate_mlp).astype(bf16))
     hidden, d_pre, d_bias_fc1 = [], [], []
-    for w1, w2, b in zip(fc1_ws, fc2_ws, fc1_bias):
-        pre_act = dot(mixed_mlp, w1) + b
-        act = jax.nn.gelu(pre_act, approximate=True).astype(bf16)
-        d_hidden = dot(d_branch_mlp, w2)
-        _, gelu_back = jax.vjp(partial(jax.nn.gelu, approximate=True), pre_act)
-        d_act = gelu_back(d_hidden)[0].astype(bf16)
+    for w1, w2, b in zip(out_fc1_ws, fc2_ws, fc1_bias):
+        act, d_act, d_b = mlp_middle(mixed_mlp, d_branch_mlp, w1, w2, b)
         hidden.append(act)
         d_pre.append(d_act)
-        d_bias_fc1.append(jnp.sum(d_act.astype(f32), axis=0))
+        d_bias_fc1.append(d_b)
 
     def both_cores(left, rights):
         met = swap_core(dot(left, rights[1], TN).astype(bf16))
         return (dot(left, rights[0], TN).astype(bf16).astype(f32) + met.astype(f32)).astype(bf16)
+
+    def scatter_dpo(total):
+        return lax.optimization_barrier(
+            lax.psum_scatter(total, "dpo", scatter_dimension=0, tiled=True)
+        )
 
     total_fc2 = both_cores(d_branch_mlp, hidden)
     total_fc1 = both_cores(mixed_mlp, d_pre)
@@ -438,15 +574,17 @@
     branch_mlp = grouped(sum(dot(h, w, NT) for h, w in zip(hidden, fc2_ws)) + bias_mlp_out)
     out_rows = flat(((middle + gate_mlp * branch_mlp) * live[:, None, None]).astype(bf16))
     d_gate_mlp = jnp.sum(grad_out * branch_mlp, axis=1)
-    d_mixed_mlp = grouped(sum(dot(g, w, NT) for g, w in zip(d_pre, fc1_ws)))
-    d_shift_mlp = jnp.sum(d_mixed_mlp, axis=1)
-    d_scale_mlp = jnp.sum(d_mixed_mlp * norm_mlp, axis=1)
-    d_middle = grad_out + norm_back(norm_mlp, inv_mlp, d_mixed_mlp * (1.0 + scale_mlp))
+    d_middle, d_shift_mlp, d_scale_mlp = matmul_norm_back(
+        d_pre, out_fc1_ws, fc_all, flat(middle), flat(grad_out), scale_mlp, f32
+    )
+    d_middle = grouped(d_middle)
     d_branch_attn = flat((d_middle * gate_attn).astype(bf16))
     d_gate_attn = jnp.sum(d_middle * branch_attn, axis=1)
 
     total_out = both_cores(d_branch_attn, mixed_parts)
-    d_branch_attn, total_out = lax.optimization_barrier((d_branch_attn, total_out))
+    total_fc1_out = jnp.concatenate([total_fc1, total_out], axis=1)
+    d_branch_attn, total_fc1_out = lax.optimization_barrier((d_branch_attn, total_fc1_out))
+    part_fc2, part_fc1_out = scatter_dpo(total_fc2), scatter_dpo(total_fc1_out)
     d_qkv = []
     for x, w, logs, keys_by_segment in reversed(list(zip(qkv, out_ws, log_parts, key_parts))):
         d_mixed = dot(d_branch_attn, w).astype(bf16)
@@ -468,13 +606,11 @@
             d_rows.insert(0, whole)
         d_qkv.append(jnp.concatenate(d_rows, axis=0))
     d_qkv.reverse()
+    d_qkv, part_fc2, part_fc1_out = lax.optimization_barrier((d_qkv, part_fc2, part_fc1_out))
     total_qkv = both_cores(mixed_attn, d_qkv)
     d_qkv, total_qkv = lax.optimization_barrier((d_qkv, total_qkv))
-    d_mixed_attn = grouped(sum(dot(d, w, NT) for d, w in zip(d_qkv, qkv_ws)))
-    d_shift_attn = jnp.sum(d_mixed_attn, axis=1)
-    d_scale_attn = jnp.sum(d_mixed_attn * norm_attn, axis=1)
-    grad_rows = flat(
-        (d_middle + norm_back(norm_attn, inv_attn, d_mixed_attn * (1.0 + scale_attn))).astype(bf16)
+    grad_rows, d_shift_attn, d_scale_attn = matmul_norm_back(
+        d_qkv, qkv_ws, qkv_w, tokens_in, flat(d_middle), scale_attn, bf16
     )
 
     def give(x):
@@ -488,10 +624,7 @@
     out_tokens = give(out_rows)
     grad_tokens = give(grad_rows)
 
-    def scatter_weight(total, kinds, wide):
-        part = lax.optimization_barrier(
-            lax.psum_scatter(total, "dpo", scatter_dimension=0, tiled=True)
-        )
+    def finish_weight(part, kinds, wide):
         part = part[:, : kinds * tsize * wide].reshape(2 * drows, kinds, tsize, wide)
         if tsize == 2:
             met = swap_tensor(at(part, 1 - t, 2))
@@ -504,77 +637,77 @@
         met = swap_core(at(part, 1 - c, 0))
         return in_order(c, mine, met, 2).reshape(drows, kinds, 2 * wide)
 
-    grad_w_fc1 = scatter_weight(total_fc1, 1, fc_w).reshape(drows, 2 * fc_w)
-    grad_w_fc2 = scatter_weight(total_fc2, 1, fc_w).reshape(drows, 2 * fc_w).T
-    grad_w_out = scatter_weight(total_out, 1, head_w).reshape(drows, slab).T
-    grad_w_qkv = scatter_weight(total_qkv, 3, head_w)
-
-    d_mod_groups = jnp.stack(
-        [d_shift_attn, d_scale_attn, d_gate_attn, d_shift_mlp, d_scale_mlp, d_gate_mlp], axis=1
-    )
-    d_mod = jnp.sum(
-        jnp.where(slot_pick[:, :, None, None], d_mod_groups[:, None], 0.0), axis=0
-    )
+    def by_slot(parts):
+        stacked = jnp.stack(parts, axis=1)
+        return jnp.sum(jnp.where(slot_pick[:, :, None, None], stacked[:, None], 0.0), axis=0)
+
+    def by_tensor_index(x):
+        parts = x.reshape(-1, tsize, x.shape[-1] // tsize)
+        return jnp.swapaxes(parts, 0, 1).reshape(tsize, -1)
 
     def bias_back(halves, wide):
         own, other = (x.reshape(x.shape[0], tsize, 1, wide) for x in halves)
-        return in_order(c, own, other, 2).reshape(own.shape[0], tsize, 2 * wide)
-
+        return in_order(c, own, other, 2).reshape(own.shape[0], tsize * 2 * wide)
+
+    def shared(parts, tie=None):
+        mine = sum_tensor(jnp.concatenate([by_tensor_index(x) for x in parts], axis=1))
+        return gather_dp(mine, tie)
+
+    d_bias_fc = bias_back([x[None] for x in d_bias_fc1], fc_w)
+    d_bias_out = jnp.stack(
+        [jnp.sum(d_branch_attn.astype(f32), axis=0), jnp.sum(d_branch_mlp.astype(f32), axis=0)]
+    )
+    early = shared(
+        [by_slot([d_gate_attn, d_shift_mlp, d_scale_mlp, d_gate_mlp]), d_bias_fc, d_bias_out]
+    )
     d_bias_q = [jnp.sum(d[:, :hslab].astype(f32), axis=0) for d in d_qkv]
     d_bias_v = [jnp.sum(d[:, 2 * hslab : 3 * hslab].astype(f32), axis=0) for d in d_qkv]
     d_bias_qv = bias_back([jnp.stack([q, v]) for q, v in zip(d_bias_q, d_bias_v)], head_w)
-    d_bias_fc = bias_back([x[None] for x in d_bias_fc1], fc_w)
-    d_bias_out = jnp.stack(
-        [jnp.sum(d_branch_attn.astype(f32), axis=0), jnp.sum(d_branch_mlp.astype(f32), axis=0)]
-    ).reshape(2, tsize, slab)
-    small = jnp.concatenate(
-        [
-            jnp.swapaxes(d_mod.reshape(slots * 6, tsize, slab), 0, 1).reshape(tsize, -1),
-            jnp.swapaxes(d_bias_qv, 0, 1).reshape(tsize, -1),
-            jnp.swapaxes(d_bias_fc, 0, 1).reshape(tsize, -1),
-            jnp.swapaxes(d_bias_out, 0, 1).reshape(tsize, -1),
-        ],
-        axis=1,
-    )
+    late, part_qkv = shared(
+        [by_slot([d_shift_attn, d_scale_attn]), d_bias_qv], scatter_dpo(total_qkv)
+    )
+
+    def split_mod(x, kinds):
+        size = slots * kinds * slab
+        return x[:, :size].reshape(dp_size * slots, kinds * slab), jnp.sum(x[:, size:], axis=0)
+
+    mod_late, bias_late = split_mod(late, 2)
+    mod_early, bias_early = split_mod(early, 4)
+    silu_f32 = silu_slots.astype(f32)
+    ada_f32 = ada_flat.astype(f32)
+
+    def exact(left, right, dims):
+        return lax.dot_general(left, right, dims, precision=lax.Precision.HIGHEST)
+
+    grad_w_ada = jnp.concatenate(
+        [exact(silu_f32, mod_late, TN), exact(silu_f32, mod_early, TN)], axis=1
+    ).reshape(drows, 6, slab)
+    d_silu_slots = exact(mod_late, ada_f32[:, : 2 * slab], NT) + exact(
+        mod_early, ada_f32[:, 2 * slab :], NT
+    )
+    d_silu = exact(picker_live, d_silu_slots, TN)
     if tsize == 2:
-        small = at(small, t, 0) + swap_tensor(at(small, 1 - t, 0))
+        d_silu = d_silu + swap_tensor(d_silu)
     else:
-        small = lax.psum_scatter(small, "tensor", scatter_dimension=0, tiled=True)[0]
-    every = lax.all_gather(small, ("dpo", "core"), axis=0, tiled=False)
-    mod_size = slots * 6 * slab
-    mod_all = every[:, :mod_size].reshape(dp_size * slots, 6 * slab)
-    bias_sum = jnp.sum(every[:, mod_size:], axis=0)
-    d_ada_bias = jnp.sum(mod_all, axis=0)
-    grad_w_ada = lax.dot_general(
-        silu_slots.astype(f32), mod_all, TN, precision=lax.Precision.HIGHEST
-    ).reshape(drows, 6, slab)
-    d_silu_slots = lax.dot_general(
-        mod_all, ada_flat.astype(f32), NT, precision=lax.Precision.HIGHEST
-    )
-    d_silu = lax.dot_general(picker_live, d_silu_slots, TN, precision=lax.Precision.HIGHEST)
+        d_silu = lax.psum(d_silu, "tensor")
     _, silu_back = jax.vjp(jax.nn.silu, cond_here)
-    cond_part = silu_back(d_silu)[0].reshape(-1)
-    shared = jnp.concatenate([d_ada_bias, bias_sum])
-    share = shared.shape[0] // dp_size
-    shared_part = lax.dynamic_slice_in_dim(shared, r * share, share, 0)
-    mine = jnp.concatenate([cond_part, shared_part])
-    mine = jnp.pad(mine, (0, -mine.shape[0] % (8 * LANES))).reshape(1, -1, LANES)
-    last = lax.all_gather(mine, ("dpo", "core", "tensor"), axis=0, tiled=True)
-    last = last.reshape(dp_size, tsize, -1)
-    cond_size = latents * drows
-    grad_cond = jnp.sum(last[:, :, :cond_size], axis=1).reshape(dp_size, latents, drows)
-    grad_cond = jnp.swapaxes(grad_cond, 0, 1).reshape(latents, width)
-    spread = jnp.swapaxes(last[:, :, cond_size : cond_size + share], 0, 1)
-    spread = spread.reshape(tsize, dp_size * share)
+    grad_cond = jnp.swapaxes(gather_dp(silu_back(d_silu)[0]), 0, 1).reshape(latents, width)
+    biases = all_tensor(
+        jnp.concatenate([jnp.sum(mod_late, axis=0), jnp.sum(mod_early, axis=0), bias_late, bias_early])
+    )
 
     def whole(start, kinds, wide):
-        part = spread[:, start : start + kinds * wide].reshape(tsize, kinds, wide)
+        part = biases[:, start : start + kinds * wide].reshape(tsize, kinds, wide)
         return jnp.swapaxes(part, 0, 1).reshape(kinds, tsize * wide)
 
     grad_b_ada = whole(0, 6, slab)
     grad_b_qv = whole(6 * slab, 2, slab)
     grad_b_fc1 = whole(8 * slab, 1, 2 * fc_w)[0]
     grad_b_out2 = whole(8 * slab + 2 * fc_w, 2, slab)
+    grad_w_fc1 = finish_weight(part_fc1_out[:, :fc_all], 1, fc_w).reshape(drows, 2 * fc_w)
+    grad_w_fc2 = finish_weight(part_fc2, 1, fc_w).reshape(drows, 2 * fc_w).T
+    grad_w_out = finish_weight(part_fc1_out[:, fc_all:], 1, head_w).reshape(drows, slab).T
+    grad_w_qkv = finish_weight(part_qkv, 3, head_w)
     return (
         out_tokens,
         grad_tokens,

time: 1110 us -> 947 us (0.85)
  matrix products: 306 us -> 166 us
  Pallas kernels: 216 us -> 324 us
  blocking collectives: 99.2 us -> 0 us
  local copies, waits for them, and re-layouts: 164 us -> 97.9 us
  waiting for transfers between devices: 159 us -> 187 us
  starting transfers between devices: 24.6 us -> 43.9 us
  other arithmetic: 118 us -> 103 us
    dot_general x25 -> x17, matrix products: 298 us -> 161 us  [dot(): lax.dot_general(left, right, dims, preferred_element_type=jnp.float32)]
    pallas_call x0 -> x4, Pallas kernels: none -> 107 us  [the longest x2 53.6 us: matmul_norm_back(): pl.pallas_call(back_kernel, grid=(groups, steps), in_specs=[by_row(deep),...]
    all_gather x2 -> x0, blocking collectives: 99.2 us -> none  [the longest x1 72.1 us: per_device(): last = lax.all_gather(mine, ('dpo', 'core', 'tensor'), axis=0, tiled=True)]
    ppermute x16 -> x19, waiting for transfers between devices: 58.5 us -> 104 us  [swap_tensor(): return lax.ppermute(x, 'tensor', [(0, 1), (1, 0)])]
    unnamed x9 -> x6, waiting for transfers between devices: 34.6 us -> 0.1 us
    all_gather x3 -> x2, waiting for transfers between devices: 61.7 us -> 34.1 us  [gather(): own = lax.all_gather(x, 'dpo', axis=0, tiled=True)]
    ppermute x0 -> x16, waiting for transfers between devices: none -> 25.9 us  [hop(): return lax.ppermute(x, axis, [(i, i ^ 1 << bit) for i in range(size)])]
    reshape x21 -> x26, local copies, waits for them, and re-layouts: 31.9 us -> 14.2 us  [the longest x4 4.81 us: finish_weight(): part = part[:, :kinds * tsize * wide].reshape(2 * drows, kinds, tsize, wide)]
  transfers between devices with their start and end apart: 37 -> 54, of which waited for: 14 -> 23; matrix products, arithmetic and copies ran while one was open for 41% -> 33% of each run, Pallas kernels for 20% -> 29%
where the time goes in v3:
time: 947 us; the launch traced here: 937 us
  Pallas kernels  324 us (34%)
  waiting for transfers between devices  187 us (20%)
  matrix products  166 us (18%)
  other arithmetic  103 us (11%)
  local copies, waits for them, and re-layouts  97.9 us (10%)
  starting transfers between devices  43.9 us (5%)
  between operations  16.5 us (2%)
    dot_general x17, matrix products, dot(): lax.dot_general(left, right, dims, preferred_element_type=jnp.float32)  161 us
    pallas_call x4, Pallas kernels, attend_backward(): pl.pallas_call(partial(backward_kernel, k_at, v_at, dk_at, dv_at, min(256...  128 us
    ppermute x19, waiting for transfers between devices, swap_tensor(): return lax.ppermute(x, 'tensor', [(0, 1), (1, 0)])  104 us
    pallas_call x4, Pallas kernels, attend_forward(): pl.pallas_call(partial(forward_kernel, k_at, v_at, min(256, rows)), grid=...  88.7 us
    pallas_call x2, Pallas kernels, matmul_norm_back(): pl.pallas_call(back_kernel, grid=(groups, steps), in_specs=[by_row(deep),...  53.6 us
    pallas_call x2, Pallas kernels, mlp_middle(): pl.pallas_call(mlp_kernel, grid=(wide // cols, count // rows), in_specs=[...  53.5 us
    all_gather x2, waiting for transfers between devices, gather(): own = lax.all_gather(x, 'dpo', axis=0, tiled=True)  34.1 us
    ppermute x16, waiting for transfers between devices, hop(): return lax.ppermute(x, axis, [(i, i ^ 1 << bit) for i in range(size)])  25.9 us
  transfers between devices with their start and end apart: 54, of which 23 were waited for; matrix products, arithmetic and copies ran while one was open for 33% of the time, Pallas kernels for 29%

profile of v3, /device:TPU:0, one launch (start us, length us, event | category | flops | bytes accessed | tf_op | source)
XLA Modules:
  0.0 937.5 jit_solution(10124027560386453695)
XLA Ops:
  11.1 2.9 collective-permute-start.7
  14.0 6.5 collective-permute-done.7
  30.5 17.6 %collective-permute-done.9 = bf16[144,2592]{1,0:T(8,128)(2,1)S(1)} collective-permute-done((bf16[144,2592]{1,0:T(8,128)(2,1)S(1)}, bf16[144,2592]{1,0:T(8,128)(2,1)S(1)}, u32[]{:S(2)}, u32[]{:S(2)}) %collective-permute-start.9) | collective-permute-done | bytes 746528 | tf_op jit(solution)/shard_map/ppermute | solution.py:340
  60.4 9.1 collective-permute-done.2
  71.9 3.9 dynamic-slice_bitcast_fusion.3
  77.3 2.7 collective-permute-done.3
  81.9 4.6 collective-permute-done.4
  89.8 14.7 %collective-permute-done.5 = f32[3,6,576]{2,1,0:T(8,128)S(1)} collective-permute-done((f32[3,6,576]{2,1,0:T(8,128)S(1)}, f32[3,6,576]{2,1,0:T(8,128)S(1)}, u32[]{:S(2)}, u32[]{:S(2)}) %collective-permute-start.5) | collective-permute-done | bytes 41504 | tf_op jit(solution)/shard_map/ppermute | solution.py:340
  112.4 2.5 fusion.7
  115.0 7.9 add_convert_fusion.1.q_ref.kv_ref
  130.8 25.7 %attend_forward.4 = (bf16[1024,640]{1,0:T(8,128)(2,1)}, f32[8,1024]{1,0:T(8,128)}) custom-call(bf16[1536,1792]{1,0:T(8,128)(2,1)} %copy-done.5, bf16[1536,1792]{1,0:T(8,128)(2,1)} %copy-done.5), custom_call_target="tpu_custom_call" | custom-call | flops 8589934592 | bytes 7340032 | tf_op jit(solution)/shard_map/attend_forward/pallas_call | solution.py:153
  156.5 3.4 pad_maximum_fusion.6.kv_ref
  159.9 9.7 %add_convert_fusion.q_ref.kv_ref = bf16[1536,1792]{1,0:T(8,128)(2,1)S(1)} fusion(bf16[1536,1152]{1,0:T(8,128)(2,1)S(1)} %copy-done.21, bf16[1152,1792]{1,0:T(8,128)(2,1)} %collective-permute-done.11.w1_ref, f32[1792]{0:T(1024)S(1)} %copy-done.53), kind=kOutput, calls=%fused_computation.9 | convolution fusion | flops 6347292672 | bytes 13179904 | tf_op jit(solution)/shard_map/dot_general | solution.py:28
  174.6 34.1 %all-gather.8.cloned.1.call-done.w1_ref.w0_ref = bf16[1152,2944]{1,0:T(8,128)(2,1)} async-done(((bf16[144,2944]{1,0:T(8,128)(2,1)}), bf16[1152,2944]{1,0:T(8,128)(2,1)}) %all-gather.8.cloned.1.call-update) | async-done | bytes 6782992 | tf_op jit(solution)/shard_map/all_gather | solution.py:473
  208.7 18.6 %attend_forward.5 = (bf16[512,640]{1,0:T(8,128)(2,1)}, f32[8,512]{1,0:T(8,128)}) custom-call(bf16[1536,1792]{1,0:T(8,128)(2,1)} %copy-done.5, bf16[1024,1152]{1,0:T(8,128)(2,1)} %pad_maximum_fusion.6.kv_ref), custom_call_target="tpu_custom_call" | custom-call | flops 4294967296 | bytes 5505024 | tf_op jit(solution)/shard_map/attend_forward/pallas_call | solution.py:153
  227.4 2.5 pad_maximum_fusion.8
  229.9 25.7 %attend_forward.6 = (bf16[1024,640]{1,0:T(8,128)(2,1)}, f32[8,1024]{1,0:T(8,128)}) custom-call(bf16[1536,1792]{1,0:T(8,128)(2,1)} %copy-done.6, bf16[1536,1792]{1,0:T(8,128)(2,1)} %copy-done.6), custom_call_target="tpu_custom_call" | custom-call | flops 8589934592 | bytes 7340032 | tf_op jit(solution)/shard_map/attend_forward/pallas_call | solution.py:153
  255.6 3.3 pad_maximum_fusion.7.kv_ref
  258.9 18.7 %attend_forward.7 = (bf16[512,640]{1,0:T(8,128)(2,1)}, f32[8,512]{1,0:T(8,128)}) custom-call(bf16[1536,1792]{1,0:T(8,128)(2,1)} %copy-done.6, bf16[1024,1152]{1,0:T(8,128)(2,1)} %pad_maximum_fusion.7.kv_ref), custom_call_target="tpu_custom_call" | custom-call | flops 4294967296 | bytes 5505024 | tf_op jit(solution)/shard_map/attend_forward/pallas_call | solution.py:153
  277.5 2.5 pad_maximum_fusion.9
  280.1 16.6 %all-gather.6.cloned.1.call-done.w2_ref = bf16[1152,2304]{1,0:T(8,128)(2,1)} async-done(((bf16[144,2304]{1,0:T(8,128)(2,1)}), bf16[1152,2304]{1,0:T(8,128)(2,1)}) %all-gather.6.cloned.1.call-update) | async-done | bytes 5308432 | tf_op jit(solution)/shard_map/all_gather | solution.py:488
  296.7 3.9 dynamic-slice_bitcast_fusion.1
  311.4 17.9 %collective-permute-done.14 = bf16[512,1152]{1,0:T(8,128)(2,1)} collective-permute-done((bf16[512,1152]{1,0:T(8,128)(2,1)}, bf16[512,1152]{1,0:T(8,128)(2,1)}, u32[]{:S(2)}, u32[]{:S(2)}) %collective-permute-start.14) | collective-permute-done | bytes 1179680 | tf_op jit(solution)/shard_map/ppermute | solution.py:340
  329.3 6.3 convert_reduce_fusion
  335.6 4.6 fusion.15
  340.3 7.8 fusion.56
  350.8 4.1 fusion.6.x_ref
  355.0 26.8 %mlp_middle.3 = (bf16[1536,2304]{1,0:T(8,128)(2,1)}, bf16[1536,2304]{1,0:T(8,128)(2,1)}, f32[1,2304]{1,0:T(1,128)}) custom-call(bf16[1536,1152]{1,0:T(8,128)(2,1)} %fusion.6.x_ref, bf16[1536,1152]{1,0:T(8,128)(2,1)} %get-tuple-element.193.g_ref, bf16[1152,2944]{1,0:T(8,128)(2,1)} %collective-permute-done.13.w1_ref, ...), custom_call_target="tpu_custom_call" | custom-call | flops 16307453952 | bytes 31850496 | tf_op jit(solution)/shard_map/mlp_middle/pallas_call | solution.py:236
  381.9 13.7 %convolution_convert_fusion = bf16[1152,2304]{1,0:T(8,128)(2,1)} fusion(bf16[1536,1152]{1,0:T(8,128)(2,1)S(1)} %copy-done.25, bf16[1536,2304]{1,0:T(8,128)(2,1)} %get-tuple-element.72), kind=kOutput, calls=%fused_computation.3 | convolution fusion | flops 8156381184 | bytes 15925248 | tf_op jit(solution)/shard_map/dot_general | solution.py:28
  395.6 10.6 %convolution_convert_fusion.2 = bf16[1152,2304]{1,0:T(8,128)(2,1)} fusion(bf16[1536,1152]{1,0:T(8,128)(2,1)S(1)} %copy-done.23, bf16[1536,2304]{1,0:T(8,128)(2,1)S(1)} %copy-done.13), kind=kOutput, calls=%fused_computation.6 | convolution fusion | flops 8156381184 | bytes 15925248 | tf_op jit(solution)/shard_map/dot_general | solution.py:28
  407.3 5.3 maximum_convert_fusion
  412.6 26.7 %mlp_middle.2 = (bf16[1536,2304]{1,0:T(8,128)(2,1)}, bf16[1536,2304]{1,0:T(8,128)(2,1)}, f32[1,2304]{1,0:T(1,128)}) custom-call(bf16[1536,1152]{1,0:T(8,128)(2,1)} %fusion.6.x_ref, bf16[1536,1152]{1,0:T(8,128)(2,1)} %get-tuple-element.193.g_ref, bf16[1152,2944]{1,0:T(8,128)(2,1)} %all-gather.8.cloned.1.call-done.w1_ref.w0_ref, ...), custom_call_target="tpu_custom_call" | custom-call | flops 16307453952 | bytes 31850496 | tf_op jit(solution)/shard_map/mlp_middle/pallas_call | solution.py:236
  444.7 15.5 %add_convert_fusion.2 = bf16[1152,2304]{1,0:T(8,128)(2,1)} fusion(bf16[1152,2304]{1,0:T(8,128)(2,1)} %collective-permute-done.17, bf16[1536,1152]{1,0:T(8,128)(2,1)} %get-tuple-element.193.g_ref, bf16[1536,2304]{1,0:T(8,128)(2,1)} %get-tuple-element.71), kind=kOutput, calls=%fused_computation.13 | convolution fusion | flops 8166998016 | bytes 21233664 | tf_op jit(solution)/shard_map/dot_general | solution.py:28
  460.2 15.3 %add_convert_fusion.3 = bf16[1152,2304]{1,0:T(8,128)(2,1)} fusion(bf16[1152,2304]{1,0:T(8,128)(2,1)} %collective-permute-done.16, bf16[1536,1152]{1,0:T(8,128)(2,1)} %fusion.6.x_ref, bf16[1536,2304]{1,0:T(8,128)(2,1)} %get-tuple-element.73.a0_ref), kind=kOutput, calls=%fused_computation.14 | convolution fusion | flops 8166998016 | bytes 21233664 | tf_op jit(solution)/shard_map/dot_general | solution.py:28
  475.5 29.2 %matmul_norm_back.2 = (f32[1536,1152]{1,0:T(8,128)}, f32[3,1,1152]{2,1,0:T(1,128)}, f32[3,1,1152]{2,1,0:T(1,128)}) custom-call(bf16[1536,2304]{1,0:T(8,128)(2,1)} %get-tuple-element.73.a0_ref, bf16[1536,2304]{1,0:T(8,128)(2,1)} %get-tuple-element.74.a1_ref, bf16[1152,2944]{1,0:T(8,128)(2,1)} %all-gather.8.cloned.1.call-done.w1_ref.w0_ref, ...), custom_call_target="tpu_custom_call" | custom-call | flops 1000000000 | bytes 1000000 | tf_op jit(solution)/shard_map/matmul_norm_back/pallas_call | solution.py:289
  504.7 3.7 fusion.4
  508.4 4.1 convolution_convert_fusion.8
  512.7 14.9 %fusion.60 = f32[1536,1152]{1,0:T(8,128)} fusion(bf16[1536,2304]{1,0:T(8,128)(2,1)} %get-tuple-element.72, bf16[1152,2304]{1,0:T(8,128)(2,1)} %collective-permute-done.15.w2_ref), kind=kOutput, calls=%fused_computation.318 | convolution fusion | flops 8153726976 | bytes 19464192 | tf_op jit(solution)/shard_map/dot_general | solution.py:28
  527.6 16.2 %add_add_fusion = f32[1536,1152]{1,0:T(8,128)} fusion(f32[1536,1152]{1,0:T(8,128)} %fusion.60, f32[1152]{0:T(1024)S(1)} %copy-done.51, bf16[1536,2304]{1,0:T(8,128)(2,1)} %get-tuple-element.71, bf16[1152,2304]{1,0:T(8,128)(2,1)} %all-gather.6.cloned.1.call-done.w2_ref), kind=kOutput, calls=%fused_computation.35 | convolution fusion | flops 8157265920 | bytes 26546688 | tf_op jit(solution)/shard_map/dot_general | solution.py:28
  543.9 8.4 multiply_reduce_fusion
  558.7 3.2 slice_bitcast_fusion.1
  563.4 5.1 fusion.10
  568.4 5.8 pad_maximum_fusion
  579.1 5.7 convolution_convert_fusion.6.do_ref
  584.8 24.0 %attend_backward.7 = (bf16[512,640]{1,0:T(8,128)(2,1)}, bf16[1024,1152]{1,0:T(8,128)(2,1)}) custom-call(bf16[1536,1792]{1,0:T(8,128)(2,1)} %copy-done.6, bf16[1024,1152]{1,0:T(8,128)(2,1)} %pad_maximum_fusion.7.kv_ref, bf16[1536,640]{1,0:T(8,128)(2,1)} %convolution_convert_fusion.6.do_ref, f32[8,512]{1,0:T(8,128)} %get-tuple-element.83.log_ref), custom_call_target="tpu_custom_call" | custom-call | flops 1000000000 | bytes 1000000 | tf_op jit(solution)/shard_map/attend_backward/pallas_call | solution.py:189
  615.3 5.8 convolution_convert_fusion.7.do_ref
  621.8 24.0 %attend_backward.5 = (bf16[512,640]{1,0:T(8,128)(2,1)}, bf16[1024,1152]{1,0:T(8,128)(2,1)}) custom-call(bf16[1536,1792]{1,0:T(8,128)(2,1)} %copy-done.5, bf16[1024,1152]{1,0:T(8,128)(2,1)} %pad_maximum_fusion.6.kv_ref, bf16[1536,640]{1,0:T(8,128)(2,1)} %convolution_convert_fusion.7.do_ref, f32[8,512]{1,0:T(8,128)} %get-tuple-element.79.log_ref), custom_call_target="tpu_custom_call" | custom-call | flops 1000000000 | bytes 1000000 | tf_op jit(solution)/shard_map/attend_backward/pallas_call | solution.py:189
  650.1 39.8 %attend_backward.6 = bf16[1024,1792]{1,0:T(8,128)(2,1)} custom-call(bf16[1536,1792]{1,0:T(8,128)(2,1)} %copy-done.6, bf16[1536,1792]{1,0:T(8,128)(2,1)} %copy-done.6, bf16[1536,640]{1,0:T(8,128)(2,1)} %convolution_convert_fusion.6.do_ref, f32[8,1024]{1,0:T(8,128)} %get-tuple-element.82.log_ref), custom_call_target="tpu_custom_call" | custom-call | flops 1000000000 | bytes 1000000 | tf_op jit(solution)/shard_map/attend_backward/pallas_call | solution.py:189
  689.9 39.9 %attend_backward.4 = bf16[1024,1792]{1,0:T(8,128)(2,1)} custom-call(bf16[1536,1792]{1,0:T(8,128)(2,1)} %copy-done.5, bf16[1536,1792]{1,0:T(8,128)(2,1)} %copy-done.5, bf16[1536,640]{1,0:T(8,128)(2,1)} %convolution_convert_fusion.7.do_ref, f32[8,1024]{1,0:T(8,128)} %get-tuple-element.78.log_ref), custom_call_target="tpu_custom_call" | custom-call | flops 1000000000 | bytes 1000000 | tf_op jit(solution)/shard_map/attend_backward/pallas_call | solution.py:189
  733.4 2.8 concatenate.160
  738.1 4.0 concatenate.158
  742.1 4.9 pad_maximum_fusion.2.a1_ref
  747.0 3.0 pad_maximum_fusion.1.a0_ref
  750.8 11.1 %convolution_convert_fusion.4 = bf16[1152,1792]{1,0:T(8,128)(2,1)} fusion(bf16[1536,1152]{1,0:T(8,128)(2,1)S(1)} %copy-done.22, bf16[1536,1792]{1,0:T(8,128)(2,1)} %pad_maximum_fusion.2.a1_ref), kind=kOutput, calls=%fused_computation.18 | convolution fusion | flops 6343852032 | bytes 13172736 | tf_op jit(solution)/shard_map/dot_general | solution.py:28
  775.3 4.6 collective-permute-done.42
  783.8 12.8 %add_convert_fusion.4 = bf16[1152,1792]{1,0:T(8,128)(2,1)} fusion(bf16[1152,1792]{1,0:T(8,128)(2,1)} %collective-permute-done.22, bf16[1536,1152]{1,0:T(8,128)(2,1)} %copy-done.20, bf16[1536,1792]{1,0:T(8,128)(2,1)} %pad_maximum_fusion.1.a0_ref), kind=kOutput, calls=%fused_computation.17 | convolution fusion | flops 6352109568 | bytes 17301504 | tf_op jit(solution)/shard_map/dot_general | solution.py:28
  799.3 8.3 collective-permute-done.44
  811.9 2.8 convert_reduce_fusion.3
  815.3 24.4 %matmul_norm_back.3 = (bf16[1536,1152]{1,0:T(8,128)(2,1)}, f32[3,1,1152]{2,1,0:T(1,128)}, f32[3,1,1152]{2,1,0:T(1,128)}) custom-call(bf16[1536,1792]{1,0:T(8,128)(2,1)} %pad_maximum_fusion.1.a0_ref, bf16[1536,1792]{1,0:T(8,128)(2,1)} %pad_maximum_fusion.2.a1_ref, bf16[1152,1792]{1,0:T(8,128)(2,1)} %all-gather.4.cloned.1.call-done.w0_ref, ...), custom_call_target="tpu_custom_call" | custom-call | flops 1000000000 | bytes 1000000 | tf_op jit(solution)/shard_map/matmul_norm_back/pallas_call | solution.py:289
  851.9 25.0 %collective-permute-done.23 = bf16[512,1152]{1,0:T(8,128)(2,1)S(1)} collective-permute-done((bf16[512,1152]{1,0:T(8,128)(2,1)S(1)}, bf16[512,1152]{1,0:T(8,128)(2,1)S(1)}, u32[]{:S(2)}, u32[]{:S(2)}) %collective-permute-start.23) | collective-permute-done | bytes 1179680 | tf_op jit(solution)/shard_map/ppermute | solution.py:340
  887.2 2.5 reshape.809
  895.7 6.8 collective-permute-done.40
  916.8 2.6 collective-permute-done.36
  920.1 3.6 collective-permute-done.37
  (529 shorter events, 180.2 us)
Async XLA Ops:
  7.2 45.8 %copy-start = (s32[29]{0:T(128)S(1)}, s32[29]{0:T(128)}, u32[]{:S(2)}) copy-start(s32[29]{0:T(128)} %param.18) | copy-start | bytes 352
  7.2 103.9 %all-gather.4.cloned.1.call-start = ((), (), s32[]{:S(2)}) async-start(), calls=%async_computation.3 | async-start | bytes 4644864 | tf_op jit(solution)/shard_map/all_gather | solution.py:473
  9.5 1.5 collective-permute-start.6
  11.1 9.5 %collective-permute-start.7 = (bf16[144,864]{1,0:T(8,128)(2,1)S(1)}, bf16[144,864]{1,0:T(8,128)(2,1)S(1)}, u32[]{:S(2)}, u32[]{:S(2)}) collective-permute-start(bf16[144,864]{1,0:T(8,128)(2,1)S(1)} %pad_maximum_fusion.21), channel_id=1, source_target_pairs={{0,1},{1,0},{2,3},{3,2},{4,5},{5,4},{6,7},{7,6},{8,9},{9,8},{10,11... | collective-permute-start | bytes 746504 | tf_op jit(solution)/shard_map/ppermute | solution.py:340
  24.4 184.4 %all-gather.8.cloned.1.call-start = ((), (), s32[]{:S(2)}) async-start(), calls=%async_computation.5 | async-start | bytes 7630848 | tf_op jit(solution)/shard_map/all_gather | solution.py:473
  26.8 1.8 collective-permute-start.8
  28.7 19.4 %collective-permute-start.9 = (bf16[144,2592]{1,0:T(8,128)(2,1)S(1)}, bf16[144,2592]{1,0:T(8,128)(2,1)S(1)}, u32[]{:S(2)}, u32[]{:S(2)}) collective-permute-start(bf16[144,2592]{1,0:T(8,128)(2,1)S(1)} %pad_maximum_fusion.12), channel_id=1, source_target_pairs={{0,1},{1,0},{2,3},{3,2},{4,5},{5,4},{6,7},{7,6},{8,9},{9,8},{10,11... | collective-permute-start | bytes 2239496 | tf_op jit(solution)/shard_map/ppermute | solution.py:340
  51.1 245.6 %all-gather.6.cloned.1.call-start = ((), (), s32[]{:S(2)}) async-start(), calls=%async_computation.4 | async-start | bytes 5971968 | tf_op jit(solution)/shard_map/all_gather | solution.py:488
  56.2 1.8 collective-permute-start.1
  58.6 10.9 %collective-permute-start.2 = (f32[4,18,576]{2,0,1:T(4,128)S(1)}, f32[4,18,576]{2,0,1:T(4,128)S(1)}, u32[]{:S(2)}, u32[]{:S(2)}) collective-permute-start(f32[4,18,576]{2,0,1:T(4,128)S(1)} %bitcast.382), channel_id=1, source_target_pairs={{0,4},{4,0},{8,12},{12,8},{16,20},{20,16},{24,28},{28,24},{1,5},{5... | collective-permute-start | bytes 497672 | tf_op jit(solution)/shard_map/ppermute | solution.py:357
  70.0 10.1 %collective-permute-start.3 = (f32[2,18,576]{2,0,1:T(2,128)S(1)}, f32[2,18,576]{2,0,1:T(2,128)S(1)}, u32[]{:S(2)}, u32[]{:S(2)}) collective-permute-start(f32[2,18,576]{2,0,1:T(2,128)S(1)} %bitcast.388), channel_id=1, source_target_pairs={{0,8},{4,12},{8,0},{12,4},{16,24},{20,28},{24,16},{28,20},{1,9},{5... | collective-permute-start | bytes 248840 | tf_op jit(solution)/shard_map/ppermute | solution.py:357
  75.8 32.4 %collective-permute-start = (bf16[512,1152]{1,0:T(8,128)(2,1)}, bf16[512,1152]{1,0:T(8,128)(2,1)S(1)}, u32[]{:S(2)}, u32[]{:S(2)}) collective-permute-start(bf16[512,1152]{1,0:T(8,128)(2,1)} %get-tuple-element.214), channel_id=1, source_target_pairs={{0,1},{1,0},{2,3},{3,2},{4,5},{5,4},{6,7},{7,6},{8,9},{9,8},{10,11... | collective-permute-start | bytes 3538952 | tf_op jit(solution)/shard_map/ppermute | solution.py:340
  80.2 6.3 collective-permute-start.4
  86.7 17.8 %collective-permute-start.5 = (f32[3,6,576]{2,1,0:T(8,128)S(1)}, f32[3,6,576]{2,1,0:T(8,128)S(1)}, u32[]{:S(2)}, u32[]{:S(2)}) collective-permute-start(f32[3,6,576]{2,1,0:T(8,128)S(1)} %reshape_squeeze.3), channel_id=1, source_target_pairs={{0,1},{1,0},{2,3},{3,2},{4,5},{5,4},{6,7},{7,6},{8,9},{9,8},{10,11... | collective-permute-start | bytes 124424 | tf_op jit(solution)/shard_map/ppermute | solution.py:340
  111.1 432.7 %copy-start.3 = (bf16[1536,1152]{1,0:T(8,128)(2,1)}, bf16[1536,1152]{1,0:T(8,128)(2,1)S(1)}, u32[]{:S(2)}) copy-start(bf16[1536,1152]{1,0:T(8,128)(2,1)S(1)} %get-tuple-element.197.x_ref) | copy-start | bytes 10616836
  111.2 638.9 %reduce-scatter.4.cloned.1.call-start = ((), (), s32[]{:S(2)}) async-start(), calls=%async_computation.6 | async-start | bytes 5971968 | tf_op jit(solution)/shard_map/reduce_scatter | solution.py:566
  112.3 47.5 %collective-permute-start.11 = (bf16[1152,1792]{1,0:T(8,128)(2,1)}, bf16[1152,1792]{1,0:T(8,128)(2,1)}, u32[]{:S(2)}, u32[]{:S(2)}) collective-permute-start(bf16[1152,1792]{1,0:T(8,128)(2,1)} %all-gather.4.cloned.1.call-done.w0_ref), channel_id=1, source_target_pairs={{0,2},{2,0},{1,3},{3,1},{4,6},{6,4},{5,7},{7,5},{8,10},{10,8},{9,1... | collective-permute-start | bytes 12386312 | tf_op jit(solution)/shard_map/ppermute | solution.py:337
  127.1 29.4 %collective-permute-start.10 = (bf16[512,1152]{1,0:T(8,128)(2,1)}, bf16[512,1152]{1,0:T(8,128)(2,1)}, u32[]{:S(2)}, u32[]{:S(2)}) collective-permute-start(bf16[512,1152]{1,0:T(8,128)(2,1)} %slice.238), channel_id=1, source_target_pairs={{0,1},{1,0},{2,3},{3,2},{4,5},{5,4},{6,7},{7,6},{8,9},{9,8},{10,11... | collective-permute-start | bytes 3538952 | tf_op jit(solution)/shard_map/ppermute | solution.py:340
  173.8 81.8 %collective-permute-start.12 = (bf16[512,1152]{1,0:T(8,128)(2,1)}, bf16[512,1152]{1,0:T(8,128)(2,1)}, u32[]{:S(2)}, u32[]{:S(2)}) collective-permute-start(bf16[512,1152]{1,0:T(8,128)(2,1)} %slice.239), channel_id=1, source_target_pairs={{0,1},{1,0},{2,3},{3,2},{4,5},{5,4},{6,7},{7,6},{8,9},{9,8},{10,11... | collective-permute-start | bytes 3538952 | tf_op jit(solution)/shard_map/ppermute | solution.py:340
  208.7 131.5 %collective-permute-start.13 = (bf16[1152,2944]{1,0:T(8,128)(2,1)}, bf16[1152,2944]{1,0:T(8,128)(2,1)}, u32[]{:S(2)}, u32[]{:S(2)}) collective-permute-start(bf16[1152,2944]{1,0:T(8,128)(2,1)} %all-gather.8.cloned.1.call-done.w1_ref.w0_ref), channel_id=1, source_target_pairs={{0,2},{2,0},{1,3},{3,1},{4,6},{6,4},{5,7},{7,5},{8,10},{10,8},{9,1... | collective-permute-start | bytes 20348936 | tf_op jit(solution)/shard_map/ppermute | solution.py:337
  296.7 58.3 %collective-permute-start.15 = (bf16[1152,2304]{1,0:T(8,128)(2,1)}, bf16[1152,2304]{1,0:T(8,128)(2,1)}, u32[]{:S(2)}, u32[]{:S(2)}) collective-permute-start(bf16[1152,2304]{1,0:T(8,128)(2,1)} %all-gather.6.cloned.1.call-done.w2_ref), channel_id=1, source_target_pairs={{0,2},{2,0},{1,3},{3,1},{4,6},{6,4},{5,7},{7,5},{8,10},{10,8},{9,1... | collective-permute-start | bytes 15925256 | tf_op jit(solution)/shard_map/ppermute | solution.py:337
  300.6 28.7 %collective-permute-start.14 = (bf16[512,1152]{1,0:T(8,128)(2,1)}, bf16[512,1152]{1,0:T(8,128)(2,1)}, u32[]{:S(2)}, u32[]{:S(2)}) collective-permute-start(bf16[512,1152]{1,0:T(8,128)(2,1)} %get-tuple-element.211), channel_id=1, source_target_pairs={{0,1},{1,0},{2,3},{3,2},{4,5},{5,4},{6,7},{7,6},{8,9},{9,8},{10,11... | collective-permute-start | bytes 3538952 | tf_op jit(solution)/shard_map/ppermute | solution.py:340
  303.7 31.9 %copy-start.60 = (f32[3]{0:T(128)}, f32[3]{0:T(128)S(1)}, u32[]{:S(2)}) copy-start(f32[3]{0:T(128)S(1)} %select_reduce_fusion.3) | copy-start | bytes 40
  309.2 31.1 %copy-start.34 = (f32[3,1,1152]{2,0,1:T(4,128)}, f32[3,1,1152]{2,0,1:T(4,128)S(1)}, u32[]{:S(2)}) copy-start(f32[3,1,1152]{2,0,1:T(4,128)S(1)} %copy.230) | copy-start | bytes 41476
  311.4 24.2 %copy-start.37 = (f32[3,1,1152]{2,0,1:T(4,128)}, f32[3,1,1152]{2,0,1:T(4,128)S(1)}, u32[]{:S(2)}) copy-start(f32[3,1,1152]{2,0,1:T(4,128)S(1)} %copy.227) | copy-start | bytes 41476
  355.0 26.9 %copy-start.25 = (bf16[1536,1152]{1,0:T(8,128)(2,1)S(1)}, bf16[1536,1152]{1,0:T(8,128)(2,1)}, u32[]{:S(2)}) copy-start(bf16[1536,1152]{1,0:T(8,128)(2,1)} %get-tuple-element.193.g_ref) | copy-start | bytes 10616836
  395.6 49.1 %collective-permute-start.17 = (bf16[1152,2304]{1,0:T(8,128)(2,1)}, bf16[1152,2304]{1,0:T(8,128)(2,1)}, u32[]{:S(2)}, u32[]{:S(2)}) collective-permute-start(bf16[1152,2304]{1,0:T(8,128)(2,1)} %convolution_convert_fusion), channel_id=1, source_target_pairs={{0,2},{2,0},{1,3},{3,1},{4,6},{6,4},{5,7},{7,5},{8,10},{10,8},{9,1... | collective-permute-start | bytes 15925256 | tf_op jit(solution)/shard_map/ppermute | solution.py:337
  406.2 54.0 %collective-permute-start.16 = (bf16[1152,2304]{1,0:T(8,128)(2,1)}, bf16[1152,2304]{1,0:T(8,128)(2,1)}, u32[]{:S(2)}, u32[]{:S(2)}) collective-permute-start(bf16[1152,2304]{1,0:T(8,128)(2,1)} %convolution_convert_fusion.2), channel_id=1, source_target_pairs={{0,2},{2,0},{1,3},{3,1},{4,6},{6,4},{5,7},{7,5},{8,10},{10,8},{9,1... | collective-permute-start | bytes 15925256 | tf_op jit(solution)/shard_map/ppermute | solution.py:337
  412.6 26.7 %copy-start.50 = (f32[1,2304]{1,0:T(1,128)S(1)}, f32[1,2304]{1,0:T(1,128)}, u32[]{:S(2)}) copy-start(f32[1,2304]{1,0:T(1,128)} %get-tuple-element.100) | copy-start | bytes 27652
  475.5 29.2 %copy-start.35 = (f32[3,1,1152]{2,0,1:T(4,128)S(1)}, f32[3,1,1152]{2,0,1:T(4,128)}, u32[]{:S(2)}) copy-start(f32[3,1,1152]{2,0,1:T(4,128)} %copy-done.34) | copy-start | bytes 41476
  512.6 50.8 %collective-permute-start.19 = (bf16[1152,640]{1,0:T(8,128)(2,1)}, bf16[1152,640]{1,0:T(8,128)(2,1)}, u32[]{:S(2)}, u32[]{:S(2)}) collective-permute-start(bf16[1152,640]{1,0:T(8,128)(2,1)} %convolution_convert_fusion.8), channel_id=1, source_target_pairs={{0,2},{2,0},{1,3},{3,1},{4,6},{6,4},{5,7},{7,5},{8,10},{10,8},{9,1... | collective-permute-start | bytes 4423688 | tf_op jit(solution)/shard_map/ppermute | solution.py:337
  512.6 237.4 %reduce-scatter.6.cloned.1.call-start = ((), (), s32[]{:S(2)}) async-start(), calls=%async_computation.7 | async-start | bytes 7630848 | tf_op jit(solution)/shard_map/reduce_scatter | solution.py:566
  561.9 290.0 %collective-permute-start.18 = (bf16[512,1152]{1,0:T(8,128)(2,1)}, bf16[512,1152]{1,0:T(8,128)(2,1)}, u32[]{:S(2)}, u32[]{:S(2)}) collective-permute-start(bf16[512,1152]{1,0:T(8,128)(2,1)} %get-tuple-element.207), channel_id=1, source_target_pairs={{0,1},{1,0},{2,3},{3,2},{4,5},{5,4},{6,7},{7,6},{8,9},{9,8},{10,11... | collective-permute-start | bytes 3538952 | tf_op jit(solution)/shard_map/ppermute | solution.py:340
  578.7 34.2 %collective-permute-start.29 = (f32[10368]{0:T(1024)}, f32[10368]{0:T(1024)}, u32[]{:S(2)}, u32[]{:S(2)}) collective-permute-start(f32[10368]{0:T(1024)} %get-tuple-element.180), channel_id=1, source_target_pairs={{0,1},{1,0},{2,3},{3,2},{4,5},{5,4},{6,7},{7,6},{8,9},{9,8},{10,11... | collective-permute-start | bytes 124424 | tf_op jit(solution)/shard_map/ppermute | solution.py:340
  611.2 120.3 %collective-permute-start.21 = (bf16[512,1152]{1,0:T(8,128)(2,1)}, bf16[512,1152]{1,0:T(8,128)(2,1)}, u32[]{:S(2)}, u32[]{:S(2)}) collective-permute-start(bf16[512,1152]{1,0:T(8,128)(2,1)} %slice.206), channel_id=1, source_target_pairs={{0,1},{1,0},{2,3},{3,2},{4,5},{5,4},{6,7},{7,6},{8,9},{9,8},{10,11... | collective-permute-start | bytes 3538952 | tf_op jit(solution)/shard_map/ppermute | solution.py:340
  612.8 270.6 %reduce-scatter.8.cloned.1.call-start = ((), (), s32[]{:S(2)}) async-start(), calls=%async_computation.8 | async-start | bytes 4644864 | tf_op jit(solution)/shard_map/reduce_scatter | solution.py:566
  613.7 7.4 collective-permute-start.30
  621.2 27.5 %collective-permute-start.31 = (f32[2,10368]{1,0:T(2,128)S(1)}, f32[2,10368]{1,0:T(2,128)S(1)}, u32[]{:S(2)}, u32[]{:S(2)}) collective-permute-start(f32[2,10368]{1,0:T(2,128)S(1)} %maximum_bitcast_fusion), channel_id=1, source_target_pairs={{0,8},{4,12},{8,0},{12,4},{16,24},{20,28},{24,16},{28,20},{1,9},{5... | collective-permute-start | bytes 248840 | tf_op jit(solution)/shard_map/ppermute | solution.py:357
  648.3 87.9 %collective-permute-start.20 = (bf16[512,1152]{1,0:T(8,128)(2,1)}, bf16[512,1152]{1,0:T(8,128)(2,1)}, u32[]{:S(2)}, u32[]{:S(2)}) collective-permute-start(bf16[512,1152]{1,0:T(8,128)(2,1)} %slice.203), channel_id=1, source_target_pairs={{0,1},{1,0},{2,3},{3,2},{4,5},{5,4},{6,7},{7,6},{8,9},{9,8},{10,11... | collective-permute-start | bytes 3538952 | tf_op jit(solution)/shard_map/ppermute | solution.py:340
  649.3 80.6 %collective-permute-start.32 = (f32[4,10368]{1,0:T(4,128)S(1)}, f32[4,10368]{1,0:T(4,128)S(1)}, u32[]{:S(2)}, u32[]{:S(2)}) collective-permute-start(f32[4,10368]{1,0:T(4,128)S(1)} %reshape.797), channel_id=1, source_target_pairs={{0,4},{4,0},{8,12},{12,8},{16,20},{20,16},{24,28},{28,24},{1,5},{5... | collective-permute-start | bytes 497672 | tf_op jit(solution)/shard_map/ppermute | solution.py:357
  731.5 31.1 %collective-permute-start.33 = (f32[8,10368]{1,0:T(8,128)}, f32[8,10368]{1,0:T(8,128)}, u32[]{:S(2)}, u32[]{:S(2)}) collective-permute-start(f32[8,10368]{1,0:T(8,128)} %reshape.798), channel_id=1, source_target_pairs={{0,2},{2,0},{1,3},{3,1},{4,6},{6,4},{5,7},{7,5},{8,10},{10,8},{9,1... | collective-permute-start | bytes 995336 | tf_op jit(solution)/shard_map/ppermute | solution.py:357
  761.9 21.9 %collective-permute-start.22 = (bf16[1152,1792]{1,0:T(8,128)(2,1)}, bf16[1152,1792]{1,0:T(8,128)(2,1)}, u32[]{:S(2)}, u32[]{:S(2)}) collective-permute-start(bf16[1152,1792]{1,0:T(8,128)(2,1)} %convolution_convert_fusion.4), channel_id=1, source_target_pairs={{0,2},{2,0},{1,3},{3,1},{4,6},{6,4},{5,7},{7,5},{8,10},{10,8},{9,1... | collective-permute-start | bytes 12386312 | tf_op jit(solution)/shard_map/ppermute | solution.py:337
  771.6 8.4 collective-permute-start.42
  774.6 22.1 %collective-permute-start.46 = (bf16[144,1,1152]{2,1,0:T(2,128)(2,1)}, bf16[144,1,1152]{2,1,0:T(2,128)(2,1)}, u32[]{:S(2)}, u32[]{:S(2)}) collective-permute-start(bf16[144,1,1152]{2,1,0:T(2,128)(2,1)} %dynamic-slice_bitcast_fusion.4), channel_id=1, source_target_pairs={{0,1},{1,0},{2,3},{3,2},{4,5},{5,4},{6,7},{7,6},{8,9},{9,8},{10,11... | collective-permute-start | bytes 995336 | tf_op jit(solution)/shard_map/ppermute | solution.py:340
  780.3 2.3 collective-permute-start.43
  781.1 26.4 %collective-permute-start.44 = (bf16[144,1,1152]{2,1,0:T(2,128)(2,1)S(1)}, bf16[144,1,1152]{2,1,0:T(2,128)(2,1)}, u32[]{:S(2)}, u32[]{:S(2)}) collective-permute-start(bf16[144,1,1152]{2,1,0:T(2,128)(2,1)S(1)} %dynamic-slice_bitcast_fusion.5), channel_id=1, source_target_pairs={{0,1},{1,0},{2,3},{3,2},{4,5},{5,4},{6,7},{7,6},{8,9},{9,8},{10,11... | collective-permute-start | bytes 995336 | tf_op jit(solution)/shard_map/ppermute | solution.py:340
  799.0 10.8 %collective-permute-start.47 = (f32[72,1,1,1152]{3,2,0,1:T(1,128)S(1)}, f32[72,1,1,1152]{3,2,0,1:T(1,128)S(1)}, u32[]{:S(2)}, u32[]{:S(2)}) collective-permute-start(f32[72,1,1,1152]{3,2,0,1:T(1,128)S(1)} %dynamic-slice_bitcast_fusion.6), channel_id=1, source_target_pairs={{0,2},{2,0},{1,3},{3,1},{4,6},{6,4},{5,7},{7,5},{8,10},{10,8},{9,1... | collective-permute-start | bytes 995336 | tf_op jit(solution)/shard_map/ppermute | solution.py:337
  809.7 1.7 collective-permute-start.45
  815.3 25.2 %copy-start.57 = (pred[3,3]{1,0:T(4,128)(4,1)S(1)}, pred[3,3]{1,0:T(4,128)(4,1)}, u32[]{:S(2)}) copy-start(pred[3,3]{1,0:T(4,128)(4,1)} %copy-done.55) | copy-start | bytes 31
  840.9 3.8 collective-permute-start.24
  843.0 33.9 %copy-start.24 = (bf16[1536,1152]{1,0:T(8,128)(2,1)S(1)}, bf16[1536,1152]{1,0:T(8,128)(2,1)}, u32[]{:S(2)}) copy-start(bf16[1536,1152]{1,0:T(8,128)(2,1)} %get-tuple-element.92) | copy-start | bytes 10616836
  844.8 6.4 collective-permute-start.25
  849.8 27.1 %collective-permute-start.23 = (bf16[512,1152]{1,0:T(8,128)(2,1)S(1)}, bf16[512,1152]{1,0:T(8,128)(2,1)S(1)}, u32[]{:S(2)}, u32[]{:S(2)}) collective-permute-start(bf16[512,1152]{1,0:T(8,128)(2,1)S(1)} %slice.208), channel_id=1, source_target_pairs={{0,1},{1,0},{2,3},{3,2},{4,5},{5,4},{6,7},{7,6},{8,9},{9,8},{10,11... | collective-permute-start | bytes 3538952 | tf_op jit(solution)/shard_map/ppermute | solution.py:340
  883.5 6.2 collective-permute-start.26
  890.7 4.5 collective-permute-start.27
  893.7 8.9 collective-permute-start.40
  895.7 7.4 collective-permute-start.28
  903.0 25.0 %collective-permute-start.41 = (f32[72,3,1,288]{3,2,0,1:T(1,128)S(1)}, f32[72,3,1,288]{3,2,0,1:T(1,128)S(1)}, u32[]{:S(2)}, u32[]{:S(2)}) collective-permute-start(f32[72,3,1,288]{3,2,0,1:T(1,128)S(1)} %squeeze.162), channel_id=1, source_target_pairs={{0,2},{2,0},{1,3},{3,1},{4,6},{6,4},{5,7},{7,5},{8,10},{10,8},{9,1... | collective-permute-start | bytes 746504 | tf_op jit(solution)/shard_map/ppermute | solution.py:337
  905.9 3.8 collective-permute-start.34
  908.1 7.8 collective-permute-start.39
  910.5 4.9 collective-permute-start.35
  915.4 4.0 collective-permute-start.36
  919.5 4.3 collective-permute-start.37
  923.9 3.1 collective-permute-start.38
  (66 other events, 562.6 us)
Sparse Core Ops, SparseCore 0:
  24.5 77.9 all-gather.3
  105.3 103.4 all-gather.7
  211.5 85.1 all-gather.5
  512.7 102.5 reduce-scatter.3
  619.4 126.0 reduce-scatter.5
  796.8 86.6 reduce-scatter.7
